TPU v7x, 32 devices: a whole 2x2x4 slice. The times are simulated.
32 devices in a mesh: row: 8 (over y, x, core), col: 4 (over z).
Axes of the slice: x: 2, y: 2, z: 4, core: 2. Of those that a mesh axis runs over, the one named last changes fastest.
Arguments:
- inverse_block: float32 [16384, 16384], P('row', 'col'), may hold values from -6 to 6
- tile_list: int32 [32], replicated, may hold values from 0 to 63, as said below
- panels: bfloat16 [3, 16384, 512], P(None, 'row'), may hold values from -0.0625 to 0.0625
- links: bfloat16 [2, 512, 512], P(None, 'col'), may hold values from -0.25 to 0.25
- diag_inverse: float32 [3, 512, 512], P(None, None, 'col'), may hold values from -6 to 6
Outputs:
- panel_inverse: float32 [3, 16384, 512], P(None, 'row', 'col')
- cross_inverse: float32 [2, 512, 512], P(None, None, 'col')
- diag_block: float32 [3, 512, 512], P(None, None, 'col')
Inputs may be any that keep to these rules, and one draw needn't show every extreme that they name: `tile_list`: 32 different tile numbers in ascending order; for each g from 0 to 4 - 1, the aligned group of tiles g * (64 // 4) to (g + 1) * (64 // 4) - 1 holds at least one of them.
All inputs are finite; a program needn't handle non-finite values.
Results may differ from a plain program's by a relative error of at most 0.0003.
Values may be sent and summed in bfloat16 or wider, within the bound.
No kernel may reach another device: no remote copies, remote signals or barrier semaphores. Data moves between devices by JAX's collectives and lax.ppermute only.
A program may use at most 128 MiB of HBM per device.

v0:
```python
import jax
import jax.numpy as jnp
from jax import lax
from jax.sharding import PartitionSpec as P

ORDER = 16384
TILE = 256


precise = lax.Precision.HIGHEST


def spread(array, axis, root):
    mine = lax.axis_index(axis) == root
    return lax.psum(jnp.where(mine, array, jnp.zeros_like(array)), axis)


def product(left, right):
    return jnp.dot(left, right, precision=precise, preferred_element_type=jnp.float32)


def local(inverse_block, tile_list, panels, links, diag_inverse):
    rows_here = inverse_block.shape[0]
    width_here = diag_inverse.shape[2]
    ratio = lax.axis_size("row") // lax.axis_size("col")
    row_number = lax.axis_index("row")
    col_number = lax.axis_index("col")
    tile_count = ORDER // TILE
    listed = jnp.any(
        tile_list[:, None] == jnp.arange(tile_count, dtype=jnp.int32)[None, :], axis=0
    ).astype(jnp.float32)
    tiles_here = rows_here // TILE
    mine = lax.dynamic_slice_in_dim(listed, row_number * tiles_here, tiles_here)
    row_mask = jnp.broadcast_to(mine[:, None], (tiles_here, TILE)).reshape(-1)
    supernodes = panels.shape[0]
    panel_parts = []
    cross_parts = []
    diag_parts = []
    previous = None
    diag_prev = None
    for supernode in range(supernodes):
        masked_panel = panels[supernode] * row_mask[:, None].astype(jnp.bfloat16)
        pieces = []
        for source in range(ratio):
            pieces.append(spread(masked_panel, "row", col_number * ratio + source))
        column_factor = jnp.concatenate(pieces, axis=0).astype(jnp.float32)
        local_factor = masked_panel.astype(jnp.float32)
        partial_rows = product(inverse_block, column_factor)
        if supernode > 0:
            link_block = lax.all_gather(links[supernode - 1], "col", axis=0, tiled=True).astype(
                jnp.float32
            )
            link_share = lax.dynamic_slice_in_dim(
                link_block, col_number * width_here, width_here, 1
            )
            diag_full = lax.all_gather(diag_prev, "col", axis=1, tiled=True)
            factor_share = lax.dynamic_slice_in_dim(
                local_factor, col_number * width_here, width_here, 1
            )
            cross_term = product(previous.T, factor_share)
            carried = product(diag_full, link_share)
        current = lax.psum_scatter(partial_rows, "col", scatter_dimension=1, tiled=True)
        if supernode > 0:
            current = current + product(previous, link_share)
        current = -current * row_mask[:, None]
        if supernode + 1 < supernodes:
            current_full = lax.all_gather(current, "col", axis=1, tiled=True)
        own_term = product(local_factor.T, current)
        own_sum = lax.psum(own_term, "row")
        diag_now = diag_inverse[supernode] - own_sum
        if supernode > 0:
            cross_block = -(lax.psum(cross_term, "row") + carried)
            diag_now = diag_now - product(link_block.T, cross_block)
        if supernode > 0:
            cross_parts.append(cross_block)
        panel_parts.append(current)
        diag_parts.append(diag_now)
        if supernode + 1 < supernodes:
            previous = current_full
        diag_prev = diag_now
    return (jnp.stack(panel_parts), jnp.stack(cross_parts), jnp.stack(diag_parts))


def solution(mesh):
    in_specs = (
        P("row", "col"),
        P(),
        P(None, "row", None),
        P(None, "col", None),
        P(None, None, "col"),
    )
    out_specs = (P(None, "row", "col"), P(None, None, "col"), P(None, None, "col"))
    return jax.shard_map(local, mesh=mesh, in_specs=in_specs, out_specs=out_specs, check_vma=False)
```

profile of v0, /device:TPU:0, one launch (start us, length us, event | category | flops | bytes accessed | tf_op | source)
XLA Modules:
  0.0 794.9 jit_solution(18022950061840392368)
XLA Ops:
  8.1 5.6 broadcast_select_fusion.5
  16.5 177.0 %all-reduce.7.cloned.1.call-done = (bf16[2048,512]{1,0:T(8,128)(2,1)}, bf16[2048,512]{1,0:T(8,128)(2,1)}, bf16[2048,512]{1,0:T(8,128)(2,1)}, bf16[2048,512]{1,0:...) async-done(((bf16[2048,512]{1,0:T(8,128)(2,1)}, bf16[2048,512]{1,0:T(8,128)(2,1)}, bf16[2048,512]{1,0:T(8,128)(2,1)}, bf16[2048,512]{1,0:T(8,128)(2,1)}, ...) | async-done | bytes 12582928 | tf_op jit(solution)/shard_map/psum | solution.py:15
  193.5 38.6 %fusion.18 = f32[2048,512]{0,1:T(8,128)} fusion(f32[2048,4096]{1,0:T(8,128)} %param.5, bf16[2048,512]{1,0:T(8,128)(2,1)} %get-tuple-element.18, bf16[2048,512]{1,0:T(8,128)(2,1)} %get-tuple-element.19), kind=kOutput, calls=%fused_computation.14 | convolution fusion | flops 51547996160 | bytes 41943040 | tf_op jit(solution)/shard_map/dot_general | solution.py:19
  232.3 38.6 %fusion.15 = f32[2048,512]{0,1:T(8,128)} fusion(f32[2048,4096]{1,0:T(8,128)} %param.5, bf16[2048,512]{1,0:T(8,128)(2,1)} %get-tuple-element.16, bf16[2048,512]{1,0:T(8,128)(2,1)} %get-tuple-element.17), kind=kOutput, calls=%fused_computation.13 | convolution fusion | flops 51547996160 | bytes 41943040 | tf_op jit(solution)/shard_map/dot_general | solution.py:19
  271.0 38.1 %reduce-scatter.4.cloned.1.call-done = f32[2048,128]{0,1:T(8,128)} async-done(((f32[2048,512]{0,1:T(8,128)}), f32[2048,128]{0,1:T(8,128)}) %reduce-scatter.4.cloned.1.call-update) | async-done | bytes 1048592 | tf_op jit(solution)/shard_map/reduce_scatter | solution.py:62
  311.9 38.6 %fusion.12 = f32[2048,512]{0,1:T(8,128)} fusion(f32[2048,4096]{1,0:T(8,128)} %param.5, bf16[2048,512]{1,0:T(8,128)(2,1)} %get-tuple-element.14, bf16[2048,512]{1,0:T(8,128)(2,1)} %get-tuple-element.15), kind=kOutput, calls=%fused_computation.12 | convolution fusion | flops 51547996160 | bytes 41943040 | tf_op jit(solution)/shard_map/dot_general | solution.py:19
  351.5 23.1 %all-gather = bf16[1,512,512]{2,1,0:T(8,128)(2,1)S(1)} all-gather(bf16[1,128,512]{2,1,0:T(8,128)(2,1)S(1)} %get-tuple-element.31), channel_id=2, replica_groups=mesh['row'=8,'col'=4] {'col'}, dimensions={1}, use_global_device_ids=true | all-gather | bytes 655360 | tf_op jit(solution)/shard_map/all_gather | solution.py:50
  374.5 22.6 %reduce-scatter.6.cloned.1.call-done = f32[2048,128]{0,1:T(8,128)} async-done(((f32[2048,512]{0,1:T(8,128)}), f32[2048,128]{0,1:T(8,128)}) %reduce-scatter.6.cloned.1.call-update) | async-done | bytes 1048592 | tf_op jit(solution)/shard_map/reduce_scatter | solution.py:62
  397.1 83.3 %all-gather.7.cloned.1.call-done = f32[2048,512]{0,1:T(8,128)} async-done(((f32[2048,128]{0,1:T(8,128)}), f32[2048,512]{0,1:T(8,128)}) %all-gather.7.cloned.1.call-update) | async-done | bytes 4194320 | tf_op jit(solution)/shard_map/all_gather | solution.py:67
  480.5 5.1 fusion.24
  485.7 21.9 %all-gather.1 = bf16[1,512,512]{2,1,0:T(8,128)(2,1)} all-gather(bf16[1,128,512]{2,1,0:T(8,128)(2,1)S(1)} %get-tuple-element.30), channel_id=3, replica_groups=mesh['row'=8,'col'=4] {'col'}, dimensions={1}, use_global_device_ids=true | all-gather | bytes 655360 | tf_op jit(solution)/shard_map/all_gather | solution.py:50
  507.6 5.4 fusion.30
  513.1 3.1 fusion.57
  516.2 2.7 fusion.36
  518.9 47.4 %reduce-scatter.8.cloned.1.call-done = f32[2048,128]{0,1:T(8,128)} async-done(((f32[2048,512]{0,1:T(8,128)}), f32[2048,128]{0,1:T(8,128)}) %reduce-scatter.8.cloned.1.call-update) | async-done | bytes 1048592 | tf_op jit(solution)/shard_map/reduce_scatter | solution.py:62
  566.3 82.7 %all-gather.9.cloned.1.call-done = f32[2048,512]{0,1:T(8,128)} async-done(((f32[2048,128]{0,1:T(8,128)}), f32[2048,512]{0,1:T(8,128)}) %all-gather.9.cloned.1.call-update) | async-done | bytes 4194320 | tf_op jit(solution)/shard_map/all_gather | solution.py:67
  649.0 4.3 fusion.22
  654.3 3.1 fusion.58
  657.4 2.9 fusion.34
  660.4 57.6 %all-reduce.5.cloned.1.call-done = (f32[512,128]{1,0:T(8,128)}, f32[512,128]{1,0:T(8,128)}, f32[512,128]{1,0:T(8,128)}, f32[512,128]{1,0:T(8,128)}, f32[512,128]{1,0:T(8,128)}) async-done(((f32[512,128]{1,0:T(8,128)}, f32[512,128]{1,0:T(8,128)}, f32[512,128]{1,0:T(8,128)}, f32[512,128]{1,0:T(8,128)}, f32[512,128]{1,0:T(8,128)}), (f32[512,128]{1,0:T(8,128)}, f32[512,128]{1,0:T(8,128)}, f32[512,128]{1,0:T(8,128)}, ...) | async-done | bytes 1310736 | tf_op jit(solution)/shard_map/psum | solution.py:72
  719.9 29.7 %all-gather.11.cloned.1.call-done = f32[512,512]{1,0:T(8,128)} async-done(((f32[512,128]{1,0:T(8,128)}), f32[512,512]{1,0:T(8,128)}) %all-gather.11.cloned.1.call-update) | async-done | bytes 1048592 | tf_op jit(solution)/shard_map/all_gather | solution.py:56
  751.5 2.6 fusion.27
  756.2 3.6 copy.17
  759.8 23.0 %all-gather.13.cloned.1.call-done = f32[512,512]{1,0:T(8,128)} async-done(((f32[512,128]{1,0:T(8,128)}), f32[512,512]{1,0:T(8,128)}) %all-gather.13.cloned.1.call-update) | async-done | bytes 1048592 | tf_op jit(solution)/shard_map/all_gather | solution.py:56
  (65 shorter events, 19.8 us)
Async XLA Ops:
  7.2 186.3 %all-reduce.7.cloned.1.call-start = ((), (), s32[]{:S(2)}) async-start(), calls=%async_computation.11 | async-start | bytes 25165824 | tf_op jit(solution)/shard_map/psum | solution.py:15
  13.8 2.6 copy-start
  16.4 292.7 %reduce-scatter.4.cloned.1.call-start = ((), (), s32[]{:S(2)}) async-start(), calls=%async_computation.3 | async-start | bytes 5242880 | tf_op jit(solution)/shard_map/reduce_scatter | solution.py:62
  232.1 165.1 %reduce-scatter.6.cloned.1.call-start = ((), (), s32[]{:S(2)}) async-start(), calls=%async_computation.4 | async-start | bytes 5242880 | tf_op jit(solution)/shard_map/reduce_scatter | solution.py:62
  271.0 209.5 %all-gather.7.cloned.1.call-start = ((), (), s32[]{:S(2)}) async-start(), calls=%async_computation.5 | async-start | bytes 5242880 | tf_op jit(solution)/shard_map/all_gather | solution.py:67
  311.4 254.8 %reduce-scatter.8.cloned.1.call-start = ((), (), s32[]{:S(2)}) async-start(), calls=%async_computation.6 | async-start | bytes 5242880 | tf_op jit(solution)/shard_map/reduce_scatter | solution.py:62
  350.5 0.9 copy-start.13
  350.5 298.5 %all-gather.9.cloned.1.call-start = ((), (), s32[]{:S(2)}) async-start(), calls=%async_computation.7 | async-start | bytes 5242880 | tf_op jit(solution)/shard_map/all_gather | solution.py:67
  374.5 105.9 %copy-start.9 = (bf16[1,512,512]{2,1,0:T(8,128)(2,1)}, bf16[1,512,512]{2,1,0:T(8,128)(2,1)S(1)}, u32[]{:S(2)}) copy-start(bf16[1,512,512]{2,1,0:T(8,128)(2,1)S(1)} %all-gather) | copy-start | bytes 1572868
  485.6 27.5 %copy-start.4 = (f32[2048,128]{0,1:T(8,128)S(1)}, f32[2048,128]{0,1:T(8,128)}, u32[]{:S(2)}) copy-start(f32[2048,128]{0,1:T(8,128)} %fusion.24) | copy-start | bytes 3145732
  485.6 232.4 %all-reduce.5.cloned.1.call-start = ((), (), s32[]{:S(2)}) async-start(), calls=%async_computation.10 | async-start | bytes 2621440 | tf_op jit(solution)/shard_map/psum | solution.py:72
  485.6 27.4 %copy-start.1 = (bf16[2048,512]{1,0:T(8,128)(2,1)S(1)}, bf16[2048,512]{1,0:T(8,128)(2,1)}, u32[]{:S(2)}) copy-start(bf16[2048,512]{1,0:T(8,128)(2,1)} %copy-done) | copy-start | bytes 6291460
  507.6 8.6 %copy-start.2 = (f32[2048,512]{0,1:T(8,128)S(1)}, f32[2048,512]{0,1:T(8,128)}, u32[]{:S(2)}) copy-start(f32[2048,512]{0,1:T(8,128)} %all-gather.7.cloned.1.call-done) | copy-start | bytes 12582916
  649.0 8.4 %copy-start.3 = (f32[2048,512]{0,1:T(8,128)S(1)}, f32[2048,512]{0,1:T(8,128)}, u32[]{:S(2)}) copy-start(f32[2048,512]{0,1:T(8,128)} %all-gather.9.cloned.1.call-done) | copy-start | bytes 12582916
  653.3 1.0 copy-start.5
  660.3 93.9 %copy-start.7 = (f32[2048,128]{0,1:T(8,128)S(1)}, f32[2048,128]{0,1:T(8,128)}, u32[]{:S(2)}) copy-start(f32[2048,128]{0,1:T(8,128)} %reduce-scatter.4.cloned.1.call-done) | copy-start | bytes 3145732
  660.4 89.2 %all-gather.11.cloned.1.call-start = ((), (), s32[]{:S(2)}) async-start(), calls=%async_computation.8 | async-start | bytes 1310720 | tf_op jit(solution)/shard_map/all_gather | solution.py:56
  719.8 34.5 %copy-start.6 = (f32[2048,128]{0,1:T(8,128)S(1)}, f32[2048,128]{0,1:T(8,128)}, u32[]{:S(2)}) copy-start(f32[2048,128]{0,1:T(8,128)} %copy-done.5) | copy-start | bytes 3145732
  719.8 63.0 %all-gather.13.cloned.1.call-start = ((), (), s32[]{:S(2)}) async-start(), calls=%async_computation.9 | async-start | bytes 1310720 | tf_op jit(solution)/shard_map/all_gather | solution.py:56
  756.2 26.6 %copy-start.8 = (bf16[1,512,512]{2,1,0:T(8,128)(2,1)S(1)}, bf16[1,512,512]{2,1,0:T(8,128)(2,1)}, u32[]{:S(2)}) copy-start(bf16[1,512,512]{2,1,0:T(8,128)(2,1)} %all-gather.1) | copy-start | bytes 1572868
  756.2 26.6 %copy-start.12 = (f32[512,128]{1,0:T(8,128)S(1)}, f32[512,128]{1,0:T(8,128)}, u32[]{:S(2)}) copy-start(f32[512,128]{1,0:T(8,128)} %get-tuple-element.9) | copy-start | bytes 786436
  756.2 28.5 %copy-start.14 = (f32[512,128]{1,0:T(8,128)S(1)}, f32[512,128]{1,0:T(8,128)}, u32[]{:S(2)}) copy-start(f32[512,128]{1,0:T(8,128)} %get-tuple-element.13) | copy-start | bytes 786436
  759.8 27.3 %copy-start.10 = (f32[512,128]{1,0:T(8,128)S(1)}, f32[512,128]{1,0:T(8,128)}, u32[]{:S(2)}) copy-start(f32[512,128]{1,0:T(8,128)} %bitcast_subtract_fusion.2) | copy-start | bytes 786436
  759.8 27.3 %copy-start.11 = (f32[512,128]{1,0:T(8,128)S(1)}, f32[512,128]{1,0:T(8,128)}, u32[]{:S(2)}) copy-start(f32[512,128]{1,0:T(8,128)} %fusion.27) | copy-start | bytes 786436
Sparse Core Ops, SparseCore 0:
  16.5 176.8 all-reduce.6
  232.2 76.8 reduce-scatter.3
  311.4 85.6 reduce-scatter.5
  399.2 81.2 all-gather.6
  482.7 83.5 reduce-scatter.7
  567.7 81.2 all-gather.8
  660.5 57.5 all-reduce.4
  720.2 29.3 all-gather.10
  754.3 28.4 all-gather.12
where the time goes:
time: 802 us; the launch traced here: 795 us
  waiting for transfers between devices  562 us (70%)
  matrix products  151 us (19%)
  blocking collectives  45 us (6%)
  other arithmetic  16.7 us (2%)
  between operations  14.2 us (2%)
    psum x1, waiting for transfers between devices, spread(): return lax.psum(jnp.where(mine, array, jnp.zeros_like(array)), axis)  177 us
    all_gather x2, waiting for transfers between devices, local(): current_full = lax.all_gather(current, 'col', axis=1, tiled=True)  166 us
    dot_general x14, matrix products, product(): jnp.dot(left, right, precision=precise, preferred_element_type=jnp.float32)  151 us
    reduce_scatter x3, waiting for transfers between devices, local(): lax.psum_scatter(partial_rows, 'col', scatter_dimension=1, tiled=True)  108 us
    psum x1, waiting for transfers between devices, local(): cross_block = -(lax.psum(cross_term, 'row') + carried)  57.6 us
    all_gather x2, waiting for transfers between devices, local(): diag_full = lax.all_gather(diag_prev, 'col', axis=1, tiled=True)  52.7 us
    all_gather x2, blocking collectives, local(): lax.all_gather(links[supernode - 1], 'col', axis=0, tiled=True)  45 us
  transfers between devices with their start and end apart: 9, of which 9 were waited for; matrix products, arithmetic and copies ran while one was open for 13% of the time, Pallas kernels for 0%

commit v1 on v0

v1 whole, which is shorter than its diff:
```python
import functools

import jax
import jax.numpy as jnp
from jax import lax
from jax.experimental import pallas as pl
from jax.experimental.pallas import tpu as pltpu
from jax.sharding import PartitionSpec as P

ORDER = 16384
TILE = 256
PAD = 16

precise = lax.Precision.HIGHEST
f32 = jnp.float32
bf16 = jnp.bfloat16
BOTH = ("row", "col")


def product(left, right):
    return jnp.dot(left, right, precision=precise, preferred_element_type=f32)


def split(value):
    high = value.astype(bf16)
    return high, (value - high.astype(f32)).astype(bf16)


def split_dot(value, right):
    high, low = split(value)
    return jnp.dot(high, right, preferred_element_type=f32) + jnp.dot(
        low, right, preferred_element_type=f32
    )


def shift(value, by, size):
    return lax.ppermute(value, "col", [(z, (z + by) % size) for z in range(size)])


def swap(value, bit, size):
    return lax.ppermute(value, "row", [(r, r ^ bit) for r in range(size)])


def messages_of(rows, cols):
    tiles = rows // TILE
    out = []
    for by in range(1, cols):
        if 2 * by == cols and tiles % 2 == 0:
            out += [(by, 0, rows // 2), (by, rows // 2, rows // 2)]
        else:
            out.append((by, 0, rows))
    return out


def panel_kernel(plan, first, last, meta, s_ref, own_ref, oth_ref, *rest):
    cols, pieces, messages = plan
    rest = list(rest)
    if not first:
        link_ref, prev_ref = rest[:2]
        rest = rest[2:]
    part_ref = None
    if not last:
        part_ref = rest.pop(0)
    mine_ref = rest.pop(0)
    out_refs = rest[: len(messages)]
    p_ref, exp_ref, sem = rest[len(messages) :]
    step = pl.program_id(0)
    group = own_ref.shape[0]
    piece = group // pieces
    width = p_ref.shape[1]
    share = width // cols
    lane, start, col = meta[0], meta[1], meta[2]

    def copies():
        found = []
        for half, ref in ((lane, own_ref), (1 - lane, oth_ref)):
            for j in range(pieces):
                at = half * group + lax.rem(start + j, pieces) * piece
                found.append(
                    pltpu.make_async_copy(
                        ref.at[pl.ds(j * piece, piece)],
                        p_ref.at[pl.ds(pl.multiple_of(at, piece), piece)],
                        sem,
                    )
                )
        return found

    @pl.when(step == 0)
    def _():
        exp_ref[...] = jnp.zeros_like(exp_ref)
        for copy in copies():
            copy.start()
        for copy in copies():
            copy.wait()

    def emit(value):
        if value is None:
            quant = jnp.zeros((TILE, width), jnp.int16)
            power = jnp.zeros((1, width), jnp.int16)
        else:
            top = jnp.max(jnp.abs(value), axis=0, keepdims=True)
            expo = jnp.clip(jnp.ceil(jnp.log2(jnp.maximum(top, 1e-30))), -100.0, 100.0)
            scaled = jnp.round(value * jnp.exp2(15.0 - expo))
            quant = jnp.clip(scaled, -32767.0, 32767.0).astype(jnp.int32).astype(jnp.int16)
            power = expo.astype(jnp.int32).astype(jnp.int16)
        if part_ref is not None:
            part_ref[...] = jnp.zeros((TILE, width), f32) if value is None else value
        for here in range(cols):

            @pl.when(col == here)
            def _(here=here):
                mine = slice(here * share, (here + 1) * share)
                mine_ref[...] = (
                    jnp.zeros((TILE, share), f32) if value is None else value[:, mine]
                )
                for (by, row, count), ref in zip(messages, out_refs):
                    to = (here + by) % cols
                    chunk = slice(to * share, (to + 1) * share)
                    at = step * TILE - row

                    @pl.when((at >= 0) & (at < count))
                    def _():
                        ref[pl.ds(pl.multiple_of(at, TILE), TILE), :] = quant[:, chunk]

        spot = lax.broadcasted_iota(jnp.int32, exp_ref.shape, 0) == step
        exp_ref[...] = jnp.where(
            spot, jnp.broadcast_to(power.astype(jnp.int32), exp_ref.shape), exp_ref[...]
        )

    listed = meta[3 + step] > 0

    @pl.when(listed)
    def _():
        total = split_dot(s_ref[...], p_ref[...])
        if not first:
            total = total + split_dot(prev_ref[...], link_ref[...])
        emit(-total)

    @pl.when(jnp.logical_not(listed))
    def _():
        emit(None)

    @pl.when(step == pl.num_programs(0) - 1)
    def _():
        powers = exp_ref[...].astype(jnp.int16)
        for here in range(cols):

            @pl.when(col == here)
            def _(here=here):
                for (by, row, count), ref in zip(messages, out_refs):
                    to = (here + by) % cols
                    ref[count : count + PAD, :] = powers[:, to * share : (to + 1) * share]


def panel_call(plan, meta, inverse_block, own, oth, link, prev, last):
    cols, pieces, messages = plan
    rows, depth = inverse_block.shape
    width = own.shape[1]
    share = width // cols
    first = link is None
    whole = lambda i, m: (0, 0)
    by_tile = lambda i, m: (i, 0)
    in_specs = [
        pl.BlockSpec((TILE, depth), by_tile),
        pl.BlockSpec(memory_space=pl.ANY),
        pl.BlockSpec(memory_space=pl.ANY),
    ]
    operands = [inverse_block, own, oth]
    if not first:
        in_specs += [pl.BlockSpec((width, width), whole), pl.BlockSpec((TILE, width), by_tile)]
        operands += [link, prev]
    out_specs, out_shape = [], []
    if not last:
        out_specs.append(pl.BlockSpec((TILE, width), by_tile))
        out_shape.append(jax.ShapeDtypeStruct((rows, width), f32))
    out_specs.append(pl.BlockSpec((TILE, share), by_tile))
    out_shape.append(jax.ShapeDtypeStruct((rows, share), f32))
    for _, _, count in messages:
        out_specs.append(pl.BlockSpec((count + PAD, share), whole))
        out_shape.append(jax.ShapeDtypeStruct((count + PAD, share), jnp.int16))
    return pl.pallas_call(
        functools.partial(panel_kernel, plan, first, last),
        grid_spec=pltpu.PrefetchScalarGridSpec(
            num_scalar_prefetch=1,
            grid=(rows // TILE,),
            in_specs=in_specs,
            out_specs=out_specs,
            scratch_shapes=[
                pltpu.VMEM((depth, width), bf16),
                pltpu.VMEM((PAD, width), jnp.int32),
                pltpu.SemaphoreType.DMA,
            ],
        ),
        out_shape=out_shape,
        compiler_params=pltpu.CompilerParams(vmem_limit_bytes=40 << 20),
        cost_estimate=pl.CostEstimate(
            flops=4 * rows * depth * width, bytes_accessed=4 * rows * depth, transcendentals=0
        ),
    )(meta, *operands)


def sum_kernel(messages, mine_ref, *rest):
    out_ref = rest[-1]
    tiles = mine_ref.shape[0] // TILE
    for tile in range(tiles):
        rows = slice(tile * TILE, (tile + 1) * TILE)
        total = mine_ref[rows, :]
        for (_, row, count), ref in zip(messages, rest[:-1]):
            at = tile * TILE - row
            if 0 <= at < count:
                powers = ref[count : count + PAD, :].astype(jnp.int32).astype(f32)
                scale = jnp.exp2(powers[tile : tile + 1, :] - 15.0)
                total = total + ref[at : at + TILE, :].astype(jnp.int32).astype(f32) * scale
        out_ref[rows, :] = total


def sum_call(messages, mine, received):
    return pl.pallas_call(
        functools.partial(sum_kernel, messages),
        out_shape=jax.ShapeDtypeStruct(mine.shape, f32),
        compiler_params=pltpu.CompilerParams(vmem_limit_bytes=24 << 20),
    )(mine, *received)


def around(pieces, col_number):
    size = len(pieces)
    ring = jnp.stack(pieces[::-1] + pieces[:0:-1])
    return lax.dynamic_slice_in_dim(ring, size - 1 - col_number, size, 0)


def row_sum_half(value, lane, row_size):
    half = value.shape[0] // 2
    keep = lax.dynamic_slice_in_dim(value, lane * half, half, 0)
    give = lax.dynamic_slice_in_dim(value, (1 - lane) * half, half, 0)
    keep = keep + swap(give, 1, row_size)
    bit = 2
    while bit < row_size:
        keep = keep + swap(keep, bit, row_size)
        bit *= 2
    return keep


def both_halves(half, lane, row_size):
    other = swap(half, 1, row_size)
    pick = lane == 0
    return jnp.where(pick, half, other), jnp.where(pick, other, half)


def local(inverse_block, tile_list, panels, links, diag_inverse):
    rows_here = inverse_block.shape[0]
    share = diag_inverse.shape[2]
    row_size, col_size = lax.axis_size("row"), lax.axis_size("col")
    row_number, col_number = lax.axis_index("row"), lax.axis_index("col")
    place, lane = row_number // 2, row_number % 2
    supernodes, _, width = panels.shape
    tiles_here = rows_here // TILE
    tiles = row_number * tiles_here + jnp.arange(tiles_here, dtype=jnp.int32)
    flags = jnp.any(tile_list[None, :] == tiles[:, None], axis=1)
    row_mask = jnp.broadcast_to(flags[:, None], (tiles_here, TILE)).reshape(-1, 1)

    pieces = col_size
    piece = rows_here // pieces
    away = (col_number - place) % col_size
    start = (place - col_number) % col_size
    sent_mask = lax.dynamic_slice_in_dim(row_mask, away * piece, piece, 0)
    sent = jnp.where(
        sent_mask[None],
        lax.dynamic_slice_in_dim(panels, away * piece, piece, 1),
        jnp.zeros((), bf16),
    )

    def gather(k):
        got = []
        for j in range(pieces):
            pairs = []
            for c in range(col_size):
                for d in range(col_size):
                    rel = (d - j) % col_size
                    if rel == 0:
                        continue
                    to = (c + rel) % col_size
                    for i in range(2):
                        pairs.append(
                            ((c * 2 + i) * col_size + (c + d) % col_size, (to * 2 + i) * col_size + c)
                        )
            got.append(lax.ppermute(sent[k], BOTH, pairs))
        own = jnp.where(
            start == 0,
            jnp.where(row_mask, panels[k], jnp.zeros((), bf16)),
            jnp.concatenate(got, axis=0),
        )
        return own, swap(own, 1, row_size)

    gathered = [gather(k) for k in range(supernodes)]

    flat = links.reshape(-1, width)
    half = flat.shape[0] // 2
    my_links = lax.dynamic_slice_in_dim(flat, lane * half, half, 0)
    got = around([my_links] + [shift(my_links, s, col_size) for s in range(1, col_size)], col_number)
    low, high = both_halves(got, lane, row_size)
    link_full = jnp.concatenate([low, high], axis=1)
    link_full = link_full.reshape(col_size, supernodes - 1, -1, width)
    link_full = link_full.transpose(1, 0, 2, 3).reshape(supernodes - 1, width, width)

    messages = messages_of(rows_here, col_size)
    plan = (col_size, pieces, messages)
    meta = jnp.concatenate(
        [jnp.stack([lane, start, col_number]), flags.astype(jnp.int32)]
    ).astype(jnp.int32)

    panel_parts, cross_parts, diag_parts = [], [], []
    part = None
    full_diag = None
    turned = None
    for k in range(supernodes):
        last = k + 1 == supernodes
        own, oth = gathered[k]
        found = panel_call(
            plan, meta, inverse_block, own, oth, None if k == 0 else link_full[k - 1], part, last
        )
        if not last:
            part = found[0]
            found = found[1:]
        mine, out = found[0], found[1:]
        received = [None] * len(messages)
        for n, (by, row, count) in enumerate(messages):
            if 2 * by == col_size and count < rows_here:
                step = 1 if row == 0 else -1
                value = out[n]
                for _ in range(by):
                    value = shift(value, step, col_size)
                received[n] = value
        for n, (by, row, count) in enumerate(messages):
            if received[n] is None:
                received[n] = shift(out[n], by, col_size)
        current = sum_call(messages, mine, received)
        panel_parts.append(current)

        factors = [panels[k]] if last else [panels[k], panels[k + 1]]
        sums = jnp.concatenate([product(f.astype(f32).T, current) for f in factors], axis=0)
        sums = sums.reshape(len(factors), 2, width // 2, share).transpose(1, 0, 2, 3)
        summed = row_sum_half(sums.reshape(-1, share), lane, row_size)
        low, high = both_halves(summed, lane, row_size)
        blocks = jnp.stack([low, high]).reshape(2, len(factors), width // 2, share)
        blocks = blocks.transpose(1, 0, 2, 3).reshape(len(factors), width, share)
        diag_now = diag_inverse[k] - blocks[0]
        if k > 0:
            link = link_full[k - 1].astype(f32)
            link_share = lax.dynamic_slice_in_dim(link, col_number * share, share, 1)
            cross = -(turned + product(full_diag, link_share))
            diag_now = diag_now - product(link.T, cross)
            cross_parts.append(cross)
        diag_parts.append(diag_now)
        if not last:
            rest = blocks[1].reshape(col_size, share, share)
            arrived = []
            for s in range(col_size):
                block = lax.dynamic_index_in_dim(rest, (col_number + s) % col_size, 0, False)
                sent_now = jnp.concatenate([diag_now, block], axis=0)
                arrived.append(shift(sent_now, s, col_size) if s else sent_now)
            ordered = around(arrived, col_number)
            full_diag = ordered[:, :width].transpose(1, 0, 2).reshape(width, width)
            turned = ordered[:, width:].transpose(0, 2, 1).reshape(width, share)
    return jnp.stack(panel_parts), jnp.stack(cross_parts), jnp.stack(diag_parts)


def solution(mesh):
    in_specs = (
        P("row", "col"),
        P(),
        P(None, "row", None),
        P(None, "col", None),
        P(None, None, "col"),
    )
    out_specs = (P(None, "row", "col"), P(None, None, "col"), P(None, None, "col"))
    return jax.shard_map(local, mesh=mesh, in_specs=in_specs, out_specs=out_specs, check_vma=False)
```

time: 802 us -> 660 us (0.82)
  waiting for transfers between devices: 562 us -> 300 us
  starting transfers between devices: 0.99 us -> 208 us
  matrix products: 151 us -> 19.8 us
  Pallas kernels: 0 us -> 51.2 us
  blocking collectives: 45 us -> 0 us
  local copies, waits for them, and re-layouts: 5.85 us -> 39.9 us
  other arithmetic: 16.7 us -> 34.4 us
  between operations: 14.2 us -> 1.89 us
    ppermute x0 -> x55, waiting for transfers between devices: none -> 300 us  [the longest x27 175 us: shift(): lax.ppermute(value, 'col', [(z, (z + by) % size) for z in range(size)])]
    psum x2 -> x0, waiting for transfers between devices: 235 us -> none  [the longest x1 177 us: spread(): return lax.psum(jnp.where(mine, array, jnp.zeros_like(array)), axis)]
    all_gather x4 -> x0, waiting for transfers between devices: 219 us -> none  [the longest x2 166 us: local(): current_full = lax.all_gather(current, 'col', axis=1, tiled=True)]
    ppermute x0 -> x55, starting transfers between devices: none -> 208 us  [the longest x12 122 us: gather(): got.append(lax.ppermute(sent[k], BOTH, pairs))]
    dot_general x14 -> x9, matrix products: 151 us -> 19.8 us  [product(): return jnp.dot(left, right, precision=precise, preferred_element_type=f32)]
    reduce_scatter x3 -> x0, waiting for transfers between devices: 108 us -> none  [local(): lax.psum_scatter(partial_rows, 'col', scatter_dimension=1, tiled=True)]
    pallas_call x0 -> x6, Pallas kernels: none -> 51.2 us  [the longest x3 47.5 us: panel_call(): pl.pallas_call(functools.partial(panel_kernel, plan, first, last), grid_s...]
    all_gather x2 -> x0, blocking collectives: 45 us -> none  [local(): lax.all_gather(links[supernode - 1], 'col', axis=0, tiled=True)]
  transfers between devices with their start and end apart: 9 -> 55, of which waited for: 9 -> 18; matrix products, arithmetic and copies ran while one was open for 13% -> 6% of each run, Pallas kernels for 0% -> 8%
where the time goes in v1:
time: 660 us; the launch traced here: 656 us
  waiting for transfers between devices  300 us (45%)
  starting transfers between devices  208 us (32%)
  Pallas kernels  51.2 us (8%)
  local copies, waits for them, and re-layouts  39.9 us (6%)
  other arithmetic  34.4 us (5%)
  matrix products  19.8 us (3%)
    ppermute x27, waiting for transfers between devices, shift(): lax.ppermute(value, 'col', [(z, (z + by) % size) for z in range(size)])  175 us
    ppermute x12, starting transfers between devices, gather(): got.append(lax.ppermute(sent[k], BOTH, pairs))  122 us
    ppermute x12, waiting for transfers between devices, gather(): got.append(lax.ppermute(sent[k], BOTH, pairs))  101 us
    ppermute x27, starting transfers between devices, shift(): lax.ppermute(value, 'col', [(z, (z + by) % size) for z in range(size)])  64.4 us
    pallas_call x3, Pallas kernels, panel_call(): pl.pallas_call(functools.partial(panel_kernel, plan, first, last), grid_s...  47.5 us
    ppermute x16, waiting for transfers between devices, swap(): return lax.ppermute(value, 'row', [(r, r ^ bit) for r in range(size)])  24.7 us
    ppermute x16, starting transfers between devices, swap(): return lax.ppermute(value, 'row', [(r, r ^ bit) for r in range(size)])  22.3 us
    unnamed x100, local copies, waits for them, and re-layouts  21.5 us
  transfers between devices with their start and end apart: 55, of which 18 were waited for; matrix products, arithmetic and copies ran while one was open for 6% of the time, Pallas kernels for 8%

profile of v1, /device:TPU:0, one launch (start us, length us, event | category | flops | bytes accessed | tf_op | source)
XLA Modules:
  0.0 655.8 jit_solution(1919332721445907733)
XLA Ops:
  5.3 10.6 %collective-permute-start.1 = (bf16[512,512]{1,0:T(8,128)(2,1)}, bf16[512,512]{1,0:T(8,128)(2,1)S(1)}, u32[]{:S(2)}, u32[]{:S(2)}) collective-permute-start(bf16[512,512]{1,0:T(8,128)(2,1)} %get-tuple-element.40), channel_id=1, source_target_pairs={{0,24},{4,28},{2,8},{6,12},{3,16},{7,20},{9,1},{13,5},{11,17},{15,... | collective-permute-start | bytes 1572872 | tf_op jit(solution)/shard_map/ppermute | solution.py:286
  18.0 91.9 %collective-permute-done.16 = bf16[128,512]{1,0:T(8,128)(2,1)S(1)} collective-permute-done((bf16[128,512]{1,0:T(8,128)(2,1)S(1)}, bf16[128,512]{1,0:T(8,128)(2,1)S(1)}, u32[]{:S(2)}, u32[]{:S(2)}) %collective-permute-start.16) | collective-permute-done | bytes 131104 | tf_op jit(solution)/shard_map/ppermute | solution.py:37
  113.9 5.4 collective-permute-start.14
  124.5 40.0 %collective-permute-done.12 = bf16[512,512]{1,0:T(8,128)(2,1)S(1)} collective-permute-done((bf16[512,512]{1,0:T(8,128)(2,1)}, bf16[512,512]{1,0:T(8,128)(2,1)S(1)}, u32[]{:S(2)}, u32[]{:S(2)}) %collective-permute-start.12) | collective-permute-done | bytes 524320 | tf_op jit(solution)/shard_map/ppermute | solution.py:286
  164.5 5.1 collective-permute-start.27
  169.5 89.0 %collective-permute-start.28 = (bf16[512,512]{1,0:T(8,128)(2,1)}, bf16[512,512]{1,0:T(8,128)(2,1)S(1)}, u32[]{:S(2)}, u32[]{:S(2)}) collective-permute-start(bf16[512,512]{1,0:T(8,128)(2,1)} %get-tuple-element.41), channel_id=1, source_target_pairs={{0,16},{4,20},{1,24},{5,28},{3,8},{7,12},{9,25},{13,29},{10,1},{14... | collective-permute-start | bytes 1572872 | tf_op jit(solution)/shard_map/ppermute | solution.py:286
  265.5 48.2 %collective-permute-done.29 = bf16[512,512]{1,0:T(8,128)(2,1)S(1)} collective-permute-done((bf16[512,512]{1,0:T(8,128)(2,1)}, bf16[512,512]{1,0:T(8,128)(2,1)S(1)}, u32[]{:S(2)}, u32[]{:S(2)}) %collective-permute-start.29) | collective-permute-done | bytes 524320 | tf_op jit(solution)/shard_map/ppermute | solution.py:286
  313.7 10.9 %collective-permute-done.3 = bf16[512,512]{1,0:T(8,128)(2,1)S(1)} collective-permute-done((bf16[512,512]{1,0:T(8,128)(2,1)}, bf16[512,512]{1,0:T(8,128)(2,1)S(1)}, u32[]{:S(2)}, u32[]{:S(2)}) %collective-permute-start.3) | collective-permute-done | bytes 524320 | tf_op jit(solution)/shard_map/ppermute | solution.py:286
  324.6 13.9 %maximum_select_fusion = (bf16[2048,512]{1,0:T(8,128)(2,1)}, bf16[2048,512]{1,0:T(8,128)(2,1)}, bf16[2048,512]{1,0:T(8,128)(2,1)S(1)}) fusion(bf16[512,512]{1,0:T(8,128)(2,1)S(1)} %collective-permute-done.3, bf16[512,512]{1,0:T(8,128)(2,1)} %collective-permute-done.2, bf16[512,512]{1,0:T(8,128)(2,1)} %copy-done.28, ...), kind=kLoop, calls=%fused_computation.1 | loop fusion | flops 31457280 | bytes 18876416 | tf_op jit(solution)/shard_map/jit(_where)/select_n | solution.py:287
  346.4 16.8 %shard_map.76 = (f32[2048,512]{1,0:T(8,128)S(1)}, f32[2048,128]{1,0:T(8,128)S(1)}, s16[2064,128]{1,0:T(8,128)(2,1)S(1)}, s16[1040,128]{1,0:T(8,128)(2,1)S(1)}, s...) custom-call(s32[11]{0:T(128)S(1)} %pad_add_fusion.meta, f32[2048,4096]{1,0:T(8,128)} %s_ref.5, ...), custom_call_target="tpu_custom_call" | custom-call | flops 17179869184 | bytes 33554432 | tf_op jit(solution)/shard_map/pallas_call | solution.py:181
  366.0 8.2 %collective-permute-start.8 = (s16[1040,128]{1,0:T(8,128)(2,1)S(1)}, s16[1040,128]{1,0:T(8,128)(2,1)S(1)}, u32[]{:S(2)}, u32[]{:S(2)}) collective-permute-start(s16[1040,128]{1,0:T(8,128)(2,1)S(1)} %get-tuple-element.23), channel_id=1, source_target_pairs={{0,3},{1,0},{2,1},{3,2},{4,7},{5,4},{6,5},{7,6},{8,11},{9,8},{10,9... | collective-permute-start | bytes 798728 | tf_op jit(solution)/shard_map/ppermute | solution.py:37
  376.2 16.2 %shard_map.78 = (f32[2048,512]{1,0:T(8,128)S(1)}, f32[2048,128]{1,0:T(8,128)S(1)}, s16[2064,128]{1,0:T(8,128)(2,1)}, s16[1040,128]{1,0:T(8,128)(2,1)S(1)}, s16[1...) custom-call(s32[11]{0:T(128)S(1)} %pad_add_fusion.meta, f32[2048,4096]{1,0:T(8,128)} %s_ref.5, ...), custom_call_target="tpu_custom_call" | custom-call | flops 17179869184 | bytes 33554432 | tf_op jit(solution)/shard_map/pallas_call | solution.py:181
  402.6 14.5 %shard_map.80 = (f32[2048,128]{1,0:T(8,128)S(1)}, s16[2064,128]{1,0:T(8,128)(2,1)S(1)}, s16[1040,128]{1,0:T(8,128)(2,1)S(1)}, s16[1040,128]{1,0:T(8,128)(2,1)S(1)}, s16[2064,128]{1,0:T(8,128)(2,1)S(1)}) custom-call(s32[11]{0:T(128)S(1)} %pad_add_fusion.meta, f32[2048,4096]{1,0:T(8,128)} %s_ref.5, bf16[2048,512]{1,0:T(8,128)(2,1)S(1)} %get-tuple-element.39.own_ref, ...), custom_call_target="tpu_custom_call" | custom-call | flops 17179869184 | bytes 33554432 | tf_op jit(solution)/shard_map/pallas_call | solution.py:181
  421.3 13.3 %collective-permute-start.25 = (s16[2064,128]{1,0:T(8,128)(2,1)}, s16[2064,128]{1,0:T(8,128)(2,1)}, u32[]{:S(2)}, u32[]{:S(2)}) collective-permute-start(s16[2064,128]{1,0:T(8,128)(2,1)} %get-tuple-element.30), channel_id=1, source_target_pairs={{0,3},{1,0},{2,1},{3,2},{4,7},{5,4},{6,5},{7,6},{8,11},{9,8},{10,9... | collective-permute-start | bytes 1585160 | tf_op jit(solution)/shard_map/ppermute | solution.py:37
  441.8 19.4 %collective-permute-done.32 = s16[1040,128]{1,0:T(8,128)(2,1)S(1)} collective-permute-done((s16[1040,128]{1,0:T(8,128)(2,1)S(1)}, s16[1040,128]{1,0:T(8,128)(2,1)S(1)}, u32[]{:S(2)}, u32[]{:S(2)}) %collective-permute-start.32) | collective-permute-done | bytes 266272 | tf_op jit(solution)/shard_map/ppermute | solution.py:37
  461.8 7.5 %collective-permute-start.24 = (s16[1040,128]{1,0:T(8,128)(2,1)}, s16[1040,128]{1,0:T(8,128)(2,1)}, u32[]{:S(2)}, u32[]{:S(2)}) collective-permute-start(s16[1040,128]{1,0:T(8,128)(2,1)} %collective-permute-done.23), channel_id=1, source_target_pairs={{0,3},{1,0},{2,1},{3,2},{4,7},{5,4},{6,5},{7,6},{8,11},{9,8},{10,9... | collective-permute-start | bytes 798728 | tf_op jit(solution)/shard_map/ppermute | solution.py:37
  497.8 9.0 %collective-permute-done.36.rest_3_ = s16[2064,128]{1,0:T(8,128)(2,1)} collective-permute-done((s16[2064,128]{1,0:T(8,128)(2,1)}, s16[2064,128]{1,0:T(8,128)(2,1)}, u32[]{:S(2)}, u32[]{:S(2)}) %collective-permute-start.36) | collective-permute-done | bytes 528416 | tf_op jit(solution)/shard_map/ppermute | solution.py:37
  520.6 15.8 %collective-permute-start.38 = (f32[512,128]{1,0:T(8,128)S(1)}, f32[512,128]{1,0:T(8,128)S(1)}, u32[]{:S(2)}, u32[]{:S(2)}) collective-permute-start(f32[512,128]{1,0:T(8,128)S(1)} %dynamic-slice_add_fusion.1), channel_id=1, source_target_pairs={{0,8},{4,12},{8,0},{12,4},{16,24},{20,28},{24,16},{28,20},{1,9},{5... | collective-permute-start | bytes 786440 | tf_op jit(solution)/shard_map/ppermute | solution.py:41
  539.2 7.1 %collective-permute-done.52 = f32[256,128]{0,1:T(8,128)S(1)} collective-permute-done((f32[256,128]{0,1:T(8,128)S(1)}, f32[256,128]{0,1:T(8,128)S(1)}, u32[]{:S(2)}, u32[]{:S(2)}) %collective-permute-start.52) | collective-permute-done | bytes 131104 | tf_op jit(solution)/shard_map/ppermute | solution.py:41
  548.5 8.7 %collective-permute-done.53 = f32[256,128]{0,1:T(8,128)S(1)} collective-permute-done((f32[256,128]{0,1:T(8,128)S(1)}, f32[256,128]{0,1:T(8,128)S(1)}, u32[]{:S(2)}, u32[]{:S(2)}) %collective-permute-start.53) | collective-permute-done | bytes 131104 | tf_op jit(solution)/shard_map/ppermute | solution.py:41
  563.0 5.0 collective-permute-done.46
  580.0 7.2 %collective-permute-done.41 = f32[640,128]{1,0:T(8,128)} collective-permute-done((f32[640,128]{1,0:T(8,128)}, f32[640,128]{1,0:T(8,128)}, u32[]{:S(2)}, u32[]{:S(2)}) %collective-permute-start.41) | collective-permute-done | bytes 327712 | tf_op jit(solution)/shard_map/ppermute | solution.py:37
  588.2 16.1 %collective-permute-done.42 = f32[640,128]{1,0:T(8,128)S(1)} collective-permute-done((f32[640,128]{1,0:T(8,128)}, f32[640,128]{1,0:T(8,128)S(1)}, u32[]{:S(2)}, u32[]{:S(2)}) %collective-permute-start.42) | collective-permute-done | bytes 327712 | tf_op jit(solution)/shard_map/ppermute | solution.py:37
  628.4 22.6 %collective-permute-done.49 = f32[640,128]{1,0:T(8,128)S(1)} collective-permute-done((f32[640,128]{1,0:T(8,128)S(1)}, f32[640,128]{1,0:T(8,128)S(1)}, u32[]{:S(2)}, u32[]{:S(2)}) %collective-permute-start.49) | collective-permute-done | bytes 327712 | tf_op jit(solution)/shard_map/ppermute | solution.py:37
  (264 shorter events, 151.6 us)
Async XLA Ops:
  4.6 109.3 %collective-permute-start = (bf16[512,512]{1,0:T(8,128)(2,1)}, bf16[512,512]{1,0:T(8,128)(2,1)S(1)}, u32[]{:S(2)}, u32[]{:S(2)}) collective-permute-start(bf16[512,512]{1,0:T(8,128)(2,1)} %get-tuple-element.40), channel_id=1, source_target_pairs={{1,8},{5,12},{2,16},{6,20},{3,24},{7,28},{10,17},{14,21},{11,25},{... | collective-permute-start | bytes 1572872 | tf_op jit(solution)/shard_map/ppermute | solution.py:286
  5.3 114.0 %collective-permute-start.1 = (bf16[512,512]{1,0:T(8,128)(2,1)}, bf16[512,512]{1,0:T(8,128)(2,1)S(1)}, u32[]{:S(2)}, u32[]{:S(2)}) collective-permute-start(bf16[512,512]{1,0:T(8,128)(2,1)} %get-tuple-element.40), channel_id=1, source_target_pairs={{0,24},{4,28},{2,8},{6,12},{3,16},{7,20},{9,1},{13,5},{11,17},{15,... | collective-permute-start | bytes 1572872 | tf_op jit(solution)/shard_map/ppermute | solution.py:286
  15.9 93.9 %collective-permute-start.16 = (bf16[128,512]{1,0:T(8,128)(2,1)S(1)}, bf16[128,512]{1,0:T(8,128)(2,1)S(1)}, u32[]{:S(2)}, u32[]{:S(2)}) collective-permute-start(bf16[128,512]{1,0:T(8,128)(2,1)S(1)} %constant_dynamic-slice_fusion.3), channel_id=1, source_target_pairs={{0,3},{1,0},{2,1},{3,2},{4,7},{5,4},{6,5},{7,6},{8,11},{9,8},{10,9... | collective-permute-start | bytes 393224 | tf_op jit(solution)/shard_map/ppermute | solution.py:37
  17.3 93.9 %collective-permute-start.17 = (bf16[128,512]{1,0:T(8,128)(2,1)S(1)}, bf16[128,512]{1,0:T(8,128)(2,1)}, u32[]{:S(2)}, u32[]{:S(2)}) collective-permute-start(bf16[128,512]{1,0:T(8,128)(2,1)S(1)} %constant_dynamic-slice_fusion.3), channel_id=1, source_target_pairs={{0,2},{1,3},{2,0},{3,1},{4,6},{5,7},{6,4},{7,5},{8,10},{9,11},{10,... | collective-permute-start | bytes 393224 | tf_op jit(solution)/shard_map/ppermute | solution.py:37
  17.3 95.2 %collective-permute-start.18 = (bf16[128,512]{1,0:T(8,128)(2,1)S(1)}, bf16[128,512]{1,0:T(8,128)(2,1)}, u32[]{:S(2)}, u32[]{:S(2)}) collective-permute-start(bf16[128,512]{1,0:T(8,128)(2,1)S(1)} %constant_dynamic-slice_fusion.3), channel_id=1, source_target_pairs={{0,1},{1,2},{2,3},{3,0},{4,5},{5,6},{6,7},{7,4},{8,9},{9,10},{10,1... | collective-permute-start | bytes 393224 | tf_op jit(solution)/shard_map/ppermute | solution.py:37
  111.2 53.3 %collective-permute-start.12 = (bf16[512,512]{1,0:T(8,128)(2,1)}, bf16[512,512]{1,0:T(8,128)(2,1)S(1)}, u32[]{:S(2)}, u32[]{:S(2)}) collective-permute-start(bf16[512,512]{1,0:T(8,128)(2,1)} %get-tuple-element.42), channel_id=1, source_target_pairs={{0,24},{4,28},{2,8},{6,12},{3,16},{7,20},{9,1},{13,5},{11,17},{15,... | collective-permute-start | bytes 1572872 | tf_op jit(solution)/shard_map/ppermute | solution.py:286
  112.5 57.0 %collective-permute-start.13 = (bf16[512,512]{1,0:T(8,128)(2,1)}, bf16[512,512]{1,0:T(8,128)(2,1)S(1)}, u32[]{:S(2)}, u32[]{:S(2)}) collective-permute-start(bf16[512,512]{1,0:T(8,128)(2,1)} %get-tuple-element.42), channel_id=1, source_target_pairs={{0,16},{4,20},{1,24},{5,28},{3,8},{7,12},{9,25},{13,29},{10,1},{14... | collective-permute-start | bytes 1572872 | tf_op jit(solution)/shard_map/ppermute | solution.py:286
  113.9 144.7 %collective-permute-start.14 = (bf16[512,512]{1,0:T(8,128)(2,1)}, bf16[512,512]{1,0:T(8,128)(2,1)S(1)}, u32[]{:S(2)}, u32[]{:S(2)}) collective-permute-start(bf16[512,512]{1,0:T(8,128)(2,1)} %get-tuple-element.42), channel_id=1, source_target_pairs={{0,8},{4,12},{1,16},{5,20},{2,24},{6,28},{9,17},{13,21},{10,25},{1... | collective-permute-start | bytes 1572872 | tf_op jit(solution)/shard_map/ppermute | solution.py:286
  119.3 140.7 %collective-permute-start.2 = (bf16[512,512]{1,0:T(8,128)(2,1)}, bf16[512,512]{1,0:T(8,128)(2,1)}, u32[]{:S(2)}, u32[]{:S(2)}) collective-permute-start(bf16[512,512]{1,0:T(8,128)(2,1)} %get-tuple-element.40), channel_id=1, source_target_pairs={{0,16},{4,20},{1,24},{5,28},{3,8},{7,12},{9,25},{13,29},{10,1},{14... | collective-permute-start | bytes 1572872 | tf_op jit(solution)/shard_map/ppermute | solution.py:286
  123.8 140.3 %collective-permute-start.26 = (bf16[512,512]{1,0:T(8,128)(2,1)}, bf16[512,512]{1,0:T(8,128)(2,1)S(1)}, u32[]{:S(2)}, u32[]{:S(2)}) collective-permute-start(bf16[512,512]{1,0:T(8,128)(2,1)} %get-tuple-element.41), channel_id=1, source_target_pairs={{1,8},{5,12},{2,16},{6,20},{3,24},{7,28},{10,17},{14,21},{11,25},{... | collective-permute-start | bytes 1572872 | tf_op jit(solution)/shard_map/ppermute | solution.py:286
  164.5 99.6 %collective-permute-start.27 = (bf16[512,512]{1,0:T(8,128)(2,1)}, bf16[512,512]{1,0:T(8,128)(2,1)S(1)}, u32[]{:S(2)}, u32[]{:S(2)}) collective-permute-start(bf16[512,512]{1,0:T(8,128)(2,1)} %get-tuple-element.41), channel_id=1, source_target_pairs={{0,24},{4,28},{2,8},{6,12},{3,16},{7,20},{9,1},{13,5},{11,17},{15,... | collective-permute-start | bytes 1572872 | tf_op jit(solution)/shard_map/ppermute | solution.py:286
  169.5 96.0 %collective-permute-start.28 = (bf16[512,512]{1,0:T(8,128)(2,1)}, bf16[512,512]{1,0:T(8,128)(2,1)S(1)}, u32[]{:S(2)}, u32[]{:S(2)}) collective-permute-start(bf16[512,512]{1,0:T(8,128)(2,1)} %get-tuple-element.41), channel_id=1, source_target_pairs={{0,16},{4,20},{1,24},{5,28},{3,8},{7,12},{9,25},{13,29},{10,1},{14... | collective-permute-start | bytes 1572872 | tf_op jit(solution)/shard_map/ppermute | solution.py:286
  258.6 55.1 %collective-permute-start.29 = (bf16[512,512]{1,0:T(8,128)(2,1)}, bf16[512,512]{1,0:T(8,128)(2,1)S(1)}, u32[]{:S(2)}, u32[]{:S(2)}) collective-permute-start(bf16[512,512]{1,0:T(8,128)(2,1)} %get-tuple-element.41), channel_id=1, source_target_pairs={{0,8},{4,12},{1,16},{5,20},{2,24},{6,28},{9,17},{13,21},{10,25},{1... | collective-permute-start | bytes 1572872 | tf_op jit(solution)/shard_map/ppermute | solution.py:286
  259.9 64.7 %collective-permute-start.3 = (bf16[512,512]{1,0:T(8,128)(2,1)}, bf16[512,512]{1,0:T(8,128)(2,1)S(1)}, u32[]{:S(2)}, u32[]{:S(2)}) collective-permute-start(bf16[512,512]{1,0:T(8,128)(2,1)} %get-tuple-element.40), channel_id=1, source_target_pairs={{0,8},{4,12},{1,16},{5,20},{2,24},{6,28},{9,17},{13,21},{10,25},{1... | collective-permute-start | bytes 1572872 | tf_op jit(solution)/shard_map/ppermute | solution.py:286
  341.2 53.3 %collective-permute-start.30 = (bf16[2048,512]{1,0:T(8,128)(2,1)S(1)}, bf16[2048,512]{1,0:T(8,128)(2,1)S(1)}, u32[]{:S(2)}, u32[]{:S(2)}) collective-permute-start(bf16[2048,512]{1,0:T(8,128)(2,1)S(1)} %get-tuple-element.39.own_ref), channel_id=1, source_target_pairs={{0,4},{4,0},{8,12},{12,8},{16,20},{20,16},{24,28},{28,24},{1,5},{5... | collective-permute-start | bytes 6291464 | tf_op jit(solution)/shard_map/ppermute | solution.py:41
  374.2 43.0 %collective-permute-start.10 = (s16[2064,128]{1,0:T(8,128)(2,1)S(1)}, s16[2064,128]{1,0:T(8,128)(2,1)S(1)}, u32[]{:S(2)}, u32[]{:S(2)}) collective-permute-start(s16[2064,128]{1,0:T(8,128)(2,1)S(1)} %get-tuple-element.24), channel_id=1, source_target_pairs={{0,3},{1,0},{2,1},{3,2},{4,7},{5,4},{6,5},{7,6},{8,11},{9,8},{10,9... | collective-permute-start | bytes 1585160 | tf_op jit(solution)/shard_map/ppermute | solution.py:37
  376.2 43.0 %collective-permute-start.5 = (s16[2064,128]{1,0:T(8,128)(2,1)S(1)}, s16[2064,128]{1,0:T(8,128)(2,1)S(1)}, u32[]{:S(2)}, u32[]{:S(2)}) collective-permute-start(s16[2064,128]{1,0:T(8,128)(2,1)S(1)} %get-tuple-element.21), channel_id=1, source_target_pairs={{0,1},{1,2},{2,3},{3,0},{4,5},{5,6},{6,7},{7,4},{8,9},{9,10},{10,1... | collective-permute-start | bytes 1585160 | tf_op jit(solution)/shard_map/ppermute | solution.py:37
  394.5 43.4 %collective-permute-start.21 = (s16[1040,128]{1,0:T(8,128)(2,1)S(1)}, s16[1040,128]{1,0:T(8,128)(2,1)}, u32[]{:S(2)}, u32[]{:S(2)}) collective-permute-start(s16[1040,128]{1,0:T(8,128)(2,1)S(1)} %get-tuple-element.28), channel_id=1, source_target_pairs={{0,1},{1,2},{2,3},{3,0},{4,5},{5,6},{6,7},{7,4},{8,9},{9,10},{10,1... | collective-permute-start | bytes 798728 | tf_op jit(solution)/shard_map/ppermute | solution.py:37
  395.6 39.0 %collective-permute-start.9 = (s16[1040,128]{1,0:T(8,128)(2,1)S(1)}, s16[1040,128]{1,0:T(8,128)(2,1)S(1)}, u32[]{:S(2)}, u32[]{:S(2)}) collective-permute-start(s16[1040,128]{1,0:T(8,128)(2,1)S(1)} %collective-permute-done.8), channel_id=1, source_target_pairs={{0,3},{1,0},{2,1},{3,2},{4,7},{5,4},{6,5},{7,6},{8,11},{9,8},{10,9... | collective-permute-start | bytes 798728 | tf_op jit(solution)/shard_map/ppermute | solution.py:37
  419.3 58.0 %collective-permute-start.20 = (s16[2064,128]{1,0:T(8,128)(2,1)}, s16[2064,128]{1,0:T(8,128)(2,1)S(1)}, u32[]{:S(2)}, u32[]{:S(2)}) collective-permute-start(s16[2064,128]{1,0:T(8,128)(2,1)} %get-tuple-element.27), channel_id=1, source_target_pairs={{0,1},{1,2},{2,3},{3,0},{4,5},{5,6},{6,7},{7,4},{8,9},{9,10},{10,1... | collective-permute-start | bytes 1585160 | tf_op jit(solution)/shard_map/ppermute | solution.py:37
  421.3 60.7 %collective-permute-start.25 = (s16[2064,128]{1,0:T(8,128)(2,1)}, s16[2064,128]{1,0:T(8,128)(2,1)}, u32[]{:S(2)}, u32[]{:S(2)}) collective-permute-start(s16[2064,128]{1,0:T(8,128)(2,1)} %get-tuple-element.30), channel_id=1, source_target_pairs={{0,3},{1,0},{2,1},{3,2},{4,7},{5,4},{6,5},{7,6},{8,11},{9,8},{10,9... | collective-permute-start | bytes 1585160 | tf_op jit(solution)/shard_map/ppermute | solution.py:37
  437.9 39.4 %collective-permute-start.34 = (s16[1040,128]{1,0:T(8,128)(2,1)S(1)}, s16[1040,128]{1,0:T(8,128)(2,1)}, u32[]{:S(2)}, u32[]{:S(2)}) collective-permute-start(s16[1040,128]{1,0:T(8,128)(2,1)S(1)} %get-tuple-element.35), channel_id=1, source_target_pairs={{0,3},{1,0},{2,1},{3,2},{4,7},{5,4},{6,5},{7,6},{8,11},{9,8},{10,9... | collective-permute-start | bytes 798728 | tf_op jit(solution)/shard_map/ppermute | solution.py:37
  441.7 40.2 %collective-permute-start.22 = (s16[1040,128]{1,0:T(8,128)(2,1)}, s16[1040,128]{1,0:T(8,128)(2,1)S(1)}, u32[]{:S(2)}, u32[]{:S(2)}) collective-permute-start(s16[1040,128]{1,0:T(8,128)(2,1)} %collective-permute-done.21), channel_id=1, source_target_pairs={{0,1},{1,2},{2,3},{3,0},{4,5},{5,6},{6,7},{7,4},{8,9},{9,10},{10,1... | collective-permute-start | bytes 798728 | tf_op jit(solution)/shard_map/ppermute | solution.py:37
  497.2 39.5 %collective-permute-start.44 = (f32[512,128]{1,0:T(8,128)S(1)}, f32[512,128]{1,0:T(8,128)S(1)}, u32[]{:S(2)}, u32[]{:S(2)}) collective-permute-start(f32[512,128]{1,0:T(8,128)S(1)} %constant_dynamic-slice_fusion), channel_id=1, source_target_pairs={{0,4},{4,0},{8,12},{12,8},{16,20},{20,16},{24,28},{28,24},{1,5},{5... | collective-permute-start | bytes 786440 | tf_op jit(solution)/shard_map/ppermute | solution.py:41
  (72 other events, 1714.6 us)

commit v2 on v0

v2 whole, which is shorter than its diff:
```python
import functools

import jax
import jax.numpy as jnp
from jax import lax
from jax.experimental import pallas as pl
from jax.experimental.pallas import tpu as pltpu
from jax.sharding import PartitionSpec as P

TILE = 256
PAD = 16
LANES = 2
STREAMS = 2

precise = lax.Precision.HIGHEST
f32 = jnp.float32
bf16 = jnp.bfloat16
i16 = jnp.int16
BOTH = ("row", "col")


def product(left, right):
    return jnp.dot(left, right, precision=precise, preferred_element_type=f32)


def turned_product(left, right):
    return lax.dot_general(
        left, right, (((0,), (0,)), ((), ())), precision=precise, preferred_element_type=f32
    )


def split_dot(value, right):
    high = value.astype(bf16)
    low = (value - high.astype(f32)).astype(bf16)
    return jnp.dot(high, right, preferred_element_type=f32) + jnp.dot(
        low, right, preferred_element_type=f32
    )


def shift(value, by, size):
    return lax.ppermute(value, "col", [(z, (z + by) % size) for z in range(size)])


def swap(value, bit, size):
    return lax.ppermute(value, "row", [(r, r ^ bit) for r in range(size)])


def quantize(value):
    top = jnp.max(jnp.abs(value), axis=0, keepdims=True)
    power = jnp.clip(jnp.ceil(jnp.log2(jnp.maximum(top, 1e-30))), -100.0, 100.0)
    scaled = jnp.clip(jnp.round(value * jnp.exp2(15.0 - power)), -32767.0, 32767.0)
    return scaled.astype(jnp.int32).astype(i16), power.astype(jnp.int32)


def restore(ref, at, tile):
    count = ref.shape[0] - PAD
    powers = ref[count:, :].astype(jnp.int32).astype(f32)
    scale = jnp.exp2(powers[tile : tile + 1, :] - 15.0)
    return ref[at : at + TILE, :].astype(jnp.int32).astype(f32) * scale


def first_kernel(meta, s_own, s_oth, own, oth, total):
    @pl.when(meta[2 + pl.program_id(0)] > 0)
    def _():
        total[...] = split_dot(s_own[...], own[...]) + split_dot(s_oth[...], oth[...])


def second_kernel(cols, chained, meta, s_own, s_oth, own, oth, before, *rest):
    rest = list(rest)
    if chained:
        link, prev = rest[:2]
        rest = rest[2:]
    part, out_a, out_b, powers = rest
    step = pl.program_id(0)
    tiles = pl.num_programs(0)
    share = part.shape[2]
    half = out_a.shape[0] - PAD
    far = lax.rem(meta[1] + cols // 2, cols)

    @pl.when(step == 0)
    def _():
        powers[...] = jnp.zeros_like(powers)

    def put(quant):
        at = step * TILE

        @pl.when(at < half)
        def _():
            out_a[pl.ds(pl.multiple_of(at, TILE), TILE), :] = quant

        @pl.when(at >= half)
        def _():
            out_b[pl.ds(pl.multiple_of(at - half, TILE), TILE), :] = quant

    listed = meta[2 + step] > 0

    @pl.when(listed)
    def _():
        total = before[...] + split_dot(s_own[...], own[...]) + split_dot(s_oth[...], oth[...])
        if chained:
            earlier = jnp.concatenate([prev[j] for j in range(cols)], axis=1)
            total = total + split_dot(earlier, link[...])
        for j in range(cols):
            part[j] = -total[:, j * share : (j + 1) * share]
        quant, power = quantize(part[far])
        put(quant)
        spot = lax.broadcasted_iota(jnp.int32, powers.shape, 0) == step
        powers[...] = jnp.where(spot, jnp.broadcast_to(power, powers.shape), powers[...])

    @pl.when(jnp.logical_not(listed))
    def _():
        part[...] = jnp.zeros_like(part)
        put(jnp.zeros((TILE, share), i16))

    @pl.when(step == tiles - 1)
    def _():
        out_a[half:, :] = powers[...].astype(i16)
        out_b[out_b.shape[0] - PAD :, :] = powers[...].astype(i16)


def panel_specs(rows, depth, width, stream):
    block = rows // STREAMS
    by_lane = lambda i, m: (i, m[0] * STREAMS + stream)
    by_other = lambda i, m: (i, (1 - m[0]) * STREAMS + stream)
    whole = lambda i, m: (0, 0)
    return [
        pl.BlockSpec((TILE, block), by_lane),
        pl.BlockSpec((TILE, block), by_other),
        pl.BlockSpec((block, width), whole),
        pl.BlockSpec((block, width), whole),
    ]


def panel_first(meta, matrix, own, oth):
    rows, depth = matrix.shape
    width = own.shape[1]
    return pl.pallas_call(
        first_kernel,
        grid_spec=pltpu.PrefetchScalarGridSpec(
            num_scalar_prefetch=1,
            grid=(rows // TILE,),
            in_specs=panel_specs(rows, depth, width, 0),
            out_specs=pl.BlockSpec((TILE, width), lambda i, m: (i, 0)),
        ),
        out_shape=jax.ShapeDtypeStruct((rows, width), f32),
        compiler_params=pltpu.CompilerParams(vmem_limit_bytes=24 << 20),
        cost_estimate=pl.CostEstimate(
            flops=2 * rows * depth * width, bytes_accessed=2 * rows * depth, transcendentals=0
        ),
    )(meta, matrix, matrix, own, oth)


def panel_second(meta, matrix, own, oth, before, link, prev, cols):
    rows, depth = matrix.shape
    width = own.shape[1]
    share = width // cols
    half = rows // 2
    whole = lambda i, m: (0, 0)
    tile_of = pl.BlockSpec((cols, TILE, share), lambda i, m: (0, i, 0))
    in_specs = panel_specs(rows, depth, width, 1) + [pl.BlockSpec((TILE, width), lambda i, m: (i, 0))]
    operands = [matrix, matrix, own, oth, before]
    if link is not None:
        in_specs += [pl.BlockSpec((width, width), whole), tile_of]
        operands += [link, prev]
    message = jax.ShapeDtypeStruct((half + PAD, share), i16)
    return pl.pallas_call(
        functools.partial(second_kernel, cols, link is not None),
        grid_spec=pltpu.PrefetchScalarGridSpec(
            num_scalar_prefetch=1,
            grid=(rows // TILE,),
            in_specs=in_specs,
            out_specs=[tile_of] + [pl.BlockSpec((half + PAD, share), whole)] * 2,
            scratch_shapes=[pltpu.VMEM((PAD, share), jnp.int32)],
        ),
        out_shape=[jax.ShapeDtypeStruct((cols, rows, share), f32), message, message],
        compiler_params=pltpu.CompilerParams(vmem_limit_bytes=28 << 20),
        cost_estimate=pl.CostEstimate(
            flops=2 * rows * depth * width, bytes_accessed=2 * rows * depth, transcendentals=0
        ),
    )(meta, *operands)


def pass_kernel(meta, right, left, got_right, got_left, out_right, out_left):
    rows = right.shape[1]
    spot = lax.broadcasted_iota(jnp.int32, (PAD, right.shape[2]), 0)
    for mine, got, out, low in ((right, got_right, out_right, True), (left, got_left, out_left, False)):
        count = got.shape[0] - PAD
        begin = 0 if low else rows - count
        powers = jnp.zeros(spot.shape, jnp.int32)
        for tile in range(rows // TILE):
            at = tile * TILE
            total = mine[0, at : at + TILE, :]
            if begin <= at < begin + count:
                total = total + restore(got, at - begin, tile)
            quant, power = quantize(total)
            out[at : at + TILE, :] = quant
            powers = jnp.where(spot == tile, jnp.broadcast_to(power, spot.shape), powers)
        out[rows:, :] = powers.astype(i16)


def pass_on(meta, part, got_right, got_left, hop):
    cols, rows, share = part.shape
    everything = lambda i, m: (0, 0)
    message = jax.ShapeDtypeStruct((rows + PAD, share), i16)
    return pl.pallas_call(
        pass_kernel,
        grid_spec=pltpu.PrefetchScalarGridSpec(
            num_scalar_prefetch=1,
            grid=(1,),
            in_specs=[
                pl.BlockSpec((1, rows, share), lambda i, m: (lax.rem(m[1] + hop, cols), 0, 0)),
                pl.BlockSpec((1, rows, share), lambda i, m: (lax.rem(m[1] + cols - hop, cols), 0, 0)),
                pl.BlockSpec(got_right.shape, everything),
                pl.BlockSpec(got_left.shape, everything),
            ],
            out_specs=[pl.BlockSpec((rows + PAD, share), everything)] * 2,
        ),
        out_shape=[message, message],
        compiler_params=pltpu.CompilerParams(vmem_limit_bytes=20 << 20),
    )(meta, part, part, got_right, got_left)


def sum_kernel(tiles, count, meta, mine, got_right, got_left, *rest):
    factors = rest[:count]
    x_ref, sums = rest[-2:]
    step = pl.program_id(0)

    @pl.when(step == 0)
    def _():
        sums[...] = jnp.zeros_like(sums)

    for tile in range(tiles):

        @pl.when(step == tile)
        def _(tile=tile):
            total = mine[0]
            for got, low in ((got_right, True), (got_left, False)):
                rows = got.shape[0] - PAD
                begin = 0 if low else tiles * TILE - rows
                if begin <= tile * TILE < begin + rows:
                    total = total + restore(got, tile * TILE - begin, tile)
            x_ref[0] = total

    turned = x_ref[0].T
    width = factors[0].shape[2]
    for n, factor in enumerate(factors):
        sums[:, n * width : (n + 1) * width] += split_dot(turned, factor[0])


def sum_parts(meta, part, got_right, got_left, panels, k, carried):
    cols, rows, share = part.shape
    supernodes, _, width = panels.shape
    tiles = rows // TILE
    count = 1 if k + 1 == supernodes else 2
    everything = lambda i, m: (0, 0)
    in_specs = [
        pl.BlockSpec((1, TILE, share), lambda i, m: (m[1], i, 0)),
        pl.BlockSpec(got_right.shape, everything),
        pl.BlockSpec(got_left.shape, everything),
    ] + [pl.BlockSpec((1, TILE, width), lambda i, m, n=n: (k + n, i, 0)) for n in range(count)]
    operands = [part, got_right, got_left] + [panels] * count
    aliases = {}
    if carried is not None:
        in_specs.append(pl.BlockSpec(memory_space=pl.ANY))
        operands.append(carried)
        aliases = {len(operands): 0}
    return pl.pallas_call(
        functools.partial(sum_kernel, tiles, count),
        grid_spec=pltpu.PrefetchScalarGridSpec(
            num_scalar_prefetch=1,
            grid=(tiles,),
            in_specs=in_specs,
            out_specs=[
                pl.BlockSpec((1, TILE, share), lambda i, m: (k, i, 0)),
                pl.BlockSpec((share, count * width), everything),
            ],
        ),
        out_shape=[
            jax.ShapeDtypeStruct((supernodes, rows, share), f32),
            jax.ShapeDtypeStruct((share, count * width), f32),
        ],
        input_output_aliases=aliases,
        compiler_params=pltpu.CompilerParams(vmem_limit_bytes=20 << 20),
    )(meta, *operands)


def around(pieces, col_number):
    size = len(pieces)
    ring = jnp.stack(pieces[::-1] + pieces[:0:-1])
    return lax.dynamic_slice_in_dim(ring, size - 1 - col_number, size, 0)


def row_sum_half(value, lane, row_size):
    half = value.shape[0] // 2
    keep = lax.dynamic_slice_in_dim(value, lane * half, half, 0)
    give = lax.dynamic_slice_in_dim(value, (1 - lane) * half, half, 0)
    keep = keep + swap(give, 1, row_size)
    bit = 2
    while bit < row_size:
        keep = keep + swap(keep, bit, row_size)
        bit *= 2
    return keep


def both_halves(half, lane, row_size, axis):
    other = swap(half, 1, row_size)
    pick = lane == 0
    return jnp.concatenate(
        [jnp.where(pick, half, other), jnp.where(pick, other, half)], axis=axis
    )


def gather_chain(chunks, turn, order, row_size):
    size, supernodes = len(order), len(chunks)
    got = []
    for step in range(supernodes + size - 2):
        pairs = []
        for t in range(size - 1):
            if 0 <= step - t < supernodes:
                for c in range(size):
                    for i in range(LANES):
                        source = ((c ^ order[t]) * LANES + i) * size + c
                        target = ((c ^ order[t + 1]) * LANES + i) * size + c
                        pairs.append((source, target))
        if step == 0:
            value = chunks[0]
        elif step < supernodes:
            value = jnp.where(turn == 0, chunks[step], got[step - 1])
        else:
            value = got[step - 1]
        got.append(lax.ppermute(value, BOTH, pairs))
    found = []
    for k in range(supernodes):
        value = chunks[k]
        for t in range(1, size):
            value = jnp.where(turn == t, got[k + t - 1], value)
        found.append(value)
    return found


def local(inverse_block, tile_list, panels, links, diag_inverse):
    rows_here = inverse_block.shape[0]
    share = diag_inverse.shape[2]
    row_size, col_size = lax.axis_size("row"), lax.axis_size("col")
    row_number, col_number = lax.axis_index("row"), lax.axis_index("col")
    place, lane = row_number // LANES, row_number % LANES
    supernodes, _, width = panels.shape
    tiles_here = rows_here // TILE
    tiles = row_number * tiles_here + jnp.arange(tiles_here, dtype=jnp.int32)
    flags = jnp.any(tile_list[None, :] == tiles[:, None], axis=1)
    row_mask = jnp.broadcast_to(flags[:, None], (tiles_here, TILE)).reshape(-1, 1)
    meta = jnp.concatenate(
        [jnp.stack([lane, col_number]).astype(jnp.int32), flags.astype(jnp.int32)]
    )

    order = [t ^ (t >> 1) for t in range(col_size)]
    back = [order[-t] for t in range(col_size)]
    relative = place ^ col_number
    turn = sum(jnp.where(relative == order[t], t, 0) for t in range(col_size))
    turn_back = (col_size - turn) % col_size
    piece = rows_here // (2 * STREAMS)
    found = []
    for stream in range(STREAMS):
        ways = []
        for way, (path, at) in enumerate(((order, turn), (back, turn_back))):
            rows = slice((2 * stream + way) * piece, (2 * stream + way + 1) * piece)
            chunks = [
                jnp.where(row_mask[rows], panels[k, rows], jnp.zeros((), bf16))
                for k in range(supernodes)
            ]
            ways.append(gather_chain(chunks, at, path, row_size))
        found.append(ways)

    flat = links.reshape(-1, width)
    half = flat.shape[0] // 2
    my_links = lax.dynamic_slice_in_dim(flat, lane * half, half, 0)
    got = around([my_links] + [shift(my_links, s, col_size) for s in range(1, col_size)], col_number)
    link_full = both_halves(got, lane, row_size, 1)
    link_full = link_full.reshape(col_size, supernodes - 1, -1, width)
    link_full = link_full.transpose(1, 0, 2, 3).reshape(supernodes - 1, width, width)

    cross_parts, diag_parts = [], []
    part = carried = cross = stacked = full_turned = None
    for k in range(supernodes):
        last = k + 1 == supernodes
        own = [jnp.concatenate([found[s][0][k], found[s][1][k]], axis=0) for s in range(STREAMS)]
        oth = [swap(value, 1, row_size) for value in own]
        before = panel_first(meta, inverse_block, own[0], oth[0])
        link = None if k == 0 else link_full[k - 1]
        part, right, left = panel_second(
            meta, inverse_block, own[1], oth[1], before, link, part, col_size
        )
        for hop in range(col_size // 2 - 1, -1, -1):
            right, left = shift(right, 1, col_size), shift(left, -1, col_size)
            if hop > 0:
                right, left = pass_on(meta, part, right, left, hop)
        carried, sums = sum_parts(meta, part, right, left, panels, k, carried)

        summed = row_sum_half(sums, lane, row_size)
        mine = lax.dynamic_slice_in_dim(diag_inverse[k], lane * (share // 2), share // 2, 1).T
        turned = mine - summed[:, :width]
        if k > 0:
            link_wide = link.astype(f32)
            link_share = lax.dynamic_slice_in_dim(link_wide, col_number * share, share, 1)
            cross = -(stacked + turned_product(full_turned, link_share))
            cross_parts.append(cross)
            cross_half = lax.dynamic_slice_in_dim(cross, lane * (share // 2), share // 2, 1)
            turned = turned - turned_product(cross_half, link_wide)
        if last:
            diag_parts.append(both_halves(turned, lane, row_size, 0).T)
        else:
            arrived = []
            for s in range(col_size):
                at = (col_number + s) % col_size * share
                block = lax.dynamic_slice_in_dim(summed[:, width:], at, share, 1)
                message = jnp.concatenate([turned, block], axis=1)
                arrived.append(shift(message, s, col_size) if s else message)
            ordered = both_halves(around(arrived, col_number), lane, row_size, 1)
            full_turned = ordered[:, :, :width].reshape(width, width)
            stacked = ordered[:, :, width:].reshape(width, share)
            diag_parts.append(
                lax.dynamic_slice_in_dim(full_turned, col_number * share, share, 0).T
            )
    return carried, jnp.stack(cross_parts), jnp.stack(diag_parts)


def solution(mesh):
    in_specs = (
        P("row", "col"),
        P(),
        P(None, "row", None),
        P(None, "col", None),
        P(None, None, "col"),
    )
    out_specs = (P(None, "row", "col"), P(None, None, "col"), P(None, None, "col"))
    return jax.shard_map(local, mesh=mesh, in_specs=in_specs, out_specs=out_specs, check_vma=False)
```

time: 802 us -> 534 us (0.67)
  waiting for transfers between devices: 562 us -> 177 us
  starting transfers between devices: 0.99 us -> 207 us
  matrix products: 151 us -> 3.12 us
  Pallas kernels: 0 us -> 73.6 us
  blocking collectives: 45 us -> 0 us
  local copies, waits for them, and re-layouts: 5.85 us -> 32.6 us
  other arithmetic: 16.7 us -> 35 us
  between operations: 14.2 us -> 1.8 us
    psum x2 -> x0, waiting for transfers between devices: 235 us -> none  [the longest x1 177 us: spread(): return lax.psum(jnp.where(mine, array, jnp.zeros_like(array)), axis)]
    all_gather x4 -> x0, waiting for transfers between devices: 219 us -> none  [the longest x2 166 us: local(): current_full = lax.all_gather(current, 'col', axis=1, tiled=True)]
    ppermute x0 -> x60, starting transfers between devices: none -> 207 us  [the longest x20 107 us: gather_chain(): got.append(lax.ppermute(value, BOTH, pairs))]
    ppermute x0 -> x60, waiting for transfers between devices: none -> 177 us  [the longest x21 83.3 us: shift(): lax.ppermute(value, 'col', [(z, (z + by) % size) for z in range(size)])]
    dot_general x14 -> x4, matrix products: 151 us -> 3.12 us  [turned_product(): lax.dot_general(left, right, (((0,), (0,)), ((), ())), precision=precise,...]
    reduce_scatter x3 -> x0, waiting for transfers between devices: 108 us -> none  [local(): lax.psum_scatter(partial_rows, 'col', scatter_dimension=1, tiled=True)]
    pallas_call x0 -> x12, Pallas kernels: none -> 73.6 us  [the longest x3 28.9 us: panel_second(): pl.pallas_call(functools.partial(second_kernel, cols, link is not None),...]
    all_gather x2 -> x0, blocking collectives: 45 us -> none  [local(): lax.all_gather(links[supernode - 1], 'col', axis=0, tiled=True)]
  transfers between devices with their start and end apart: 9 -> 60, of which waited for: 9 -> 30; matrix products, arithmetic and copies ran while one was open for 13% -> 6% of each run, Pallas kernels for 0% -> 14%
where the time goes in v2:
time: 534 us; the launch traced here: 530 us
  starting transfers between devices  207 us (39%)
  waiting for transfers between devices  177 us (33%)
  Pallas kernels  73.6 us (14%)
  other arithmetic  35 us (7%)
  local copies, waits for them, and re-layouts  32.6 us (6%)
    ppermute x20, starting transfers between devices, gather_chain(): got.append(lax.ppermute(value, BOTH, pairs))  107 us
    ppermute x21, waiting for transfers between devices, shift(): lax.ppermute(value, 'col', [(z, (z + by) % size) for z in range(size)])  83.3 us
    ppermute x20, waiting for transfers between devices, gather_chain(): got.append(lax.ppermute(value, BOTH, pairs))  79.1 us
    ppermute x21, starting transfers between devices, shift(): lax.ppermute(value, 'col', [(z, (z + by) % size) for z in range(size)])  54.3 us
    ppermute x19, starting transfers between devices, swap(): return lax.ppermute(value, 'row', [(r, r ^ bit) for r in range(size)])  45.4 us
    pallas_call x3, Pallas kernels, panel_second(): pl.pallas_call(functools.partial(second_kernel, cols, link is not None),...  28.9 us
    pallas_call x3, Pallas kernels, panel_first(): pl.pallas_call(first_kernel, grid_spec=pltpu.PrefetchScalarGridSpec(num_s...  27 us
    unnamed x108, local copies, waits for them, and re-layouts  21.4 us
  transfers between devices with their start and end apart: 60, of which 30 were waited for; matrix products, arithmetic and copies ran while one was open for 6% of the time, Pallas kernels for 14%

profile of v2, /device:TPU:0, one launch (start us, length us, event | category | flops | bytes accessed | tf_op | source)
XLA Modules:
  0.0 530.2 jit_solution(8577882371199918204)
XLA Ops:
  7.8 11.1 %collective-permute-done.11 = bf16[512,512]{1,0:T(8,128)(2,1)S(1)} collective-permute-done((bf16[512,512]{1,0:T(8,128)(2,1)S(1)}, bf16[512,512]{1,0:T(8,128)(2,1)S(1)}, u32[]{:S(2)}, u32[]{:S(2)}) %collective-permute-start.11) | collective-permute-done | bytes 524320 | tf_op jit(solution)/shard_map/ppermute | solution.py:331
  24.5 10.3 %collective-permute-done.12 = bf16[512,512]{1,0:T(8,128)(2,1)S(1)} collective-permute-done((bf16[512,512]{1,0:T(8,128)(2,1)S(1)}, bf16[512,512]{1,0:T(8,128)(2,1)S(1)}, u32[]{:S(2)}, u32[]{:S(2)}) %collective-permute-start.12) | collective-permute-done | bytes 524320 | tf_op jit(solution)/shard_map/ppermute | solution.py:331
  40.4 9.3 %collective-permute-done.13 = bf16[512,512]{1,0:T(8,128)(2,1)S(1)} collective-permute-done((bf16[512,512]{1,0:T(8,128)(2,1)S(1)}, bf16[512,512]{1,0:T(8,128)(2,1)S(1)}, u32[]{:S(2)}, u32[]{:S(2)}) %collective-permute-start.13) | collective-permute-done | bytes 524320 | tf_op jit(solution)/shard_map/ppermute | solution.py:331
  55.5 26.9 %collective-permute-start.16 = (bf16[512,512]{1,0:T(8,128)(2,1)S(1)}, bf16[512,512]{1,0:T(8,128)(2,1)S(1)}, u32[]{:S(2)}, u32[]{:S(2)}) collective-permute-start(bf16[512,512]{1,0:T(8,128)(2,1)S(1)} %get-tuple-element.62), channel_id=1, source_target_pairs={{0,16},{4,20},{9,25},{13,29},{18,2},{22,6},{27,11},{31,15}} | collective-permute-start | bytes 1572872 | tf_op jit(solution)/shard_map/ppermute | solution.py:331
  82.4 7.1 %collective-permute-done.16 = bf16[512,512]{1,0:T(8,128)(2,1)S(1)} collective-permute-done((bf16[512,512]{1,0:T(8,128)(2,1)S(1)}, bf16[512,512]{1,0:T(8,128)(2,1)S(1)}, u32[]{:S(2)}, u32[]{:S(2)}) %collective-permute-start.16) | collective-permute-done | bytes 524320 | tf_op jit(solution)/shard_map/ppermute | solution.py:331
  95.9 7.1 %collective-permute-done.17 = bf16[512,512]{1,0:T(8,128)(2,1)S(1)} collective-permute-done((bf16[512,512]{1,0:T(8,128)(2,1)S(1)}, bf16[512,512]{1,0:T(8,128)(2,1)S(1)}, u32[]{:S(2)}, u32[]{:S(2)}) %collective-permute-start.17) | collective-permute-done | bytes 524320 | tf_op jit(solution)/shard_map/ppermute | solution.py:331
  117.1 8.1 %collective-permute-start.5 = (bf16[512,512]{1,0:T(8,128)(2,1)S(1)}, bf16[512,512]{1,0:T(8,128)(2,1)S(1)}, u32[]{:S(2)}, u32[]{:S(2)}) collective-permute-start(bf16[512,512]{1,0:T(8,128)(2,1)S(1)} %get-tuple-element.63), channel_id=1, source_target_pairs={{0,16},{4,20},{9,25},{13,29},{18,2},{22,6},{27,11},{31,15}} | collective-permute-start | bytes 1572872 | tf_op jit(solution)/shard_map/ppermute | solution.py:331
  136.0 13.9 %collective-permute-start.1 = (bf16[512,512]{1,0:T(8,128)(2,1)S(1)}, bf16[512,512]{1,0:T(8,128)(2,1)S(1)}, u32[]{:S(2)}, u32[]{:S(2)}) collective-permute-start(bf16[512,512]{1,0:T(8,128)(2,1)S(1)} %get-tuple-element.66), channel_id=1, source_target_pairs={{0,8},{4,12},{9,1},{13,5},{18,26},{22,30},{27,19},{31,23},{8,24},{... | collective-permute-start | bytes 1572872 | tf_op jit(solution)/shard_map/ppermute | solution.py:331
  150.0 10.6 %collective-permute-done.1 = bf16[512,512]{1,0:T(8,128)(2,1)S(1)} collective-permute-done((bf16[512,512]{1,0:T(8,128)(2,1)S(1)}, bf16[512,512]{1,0:T(8,128)(2,1)S(1)}, u32[]{:S(2)}, u32[]{:S(2)}) %collective-permute-start.1) | collective-permute-done | bytes 524320 | tf_op jit(solution)/shard_map/ppermute | solution.py:331
  193.2 17.4 %collective-permute-start.7 = (bf16[512,512]{1,0:T(8,128)(2,1)}, bf16[512,512]{1,0:T(8,128)(2,1)}, u32[]{:S(2)}, u32[]{:S(2)}) collective-permute-start(bf16[512,512]{1,0:T(8,128)(2,1)} %get-tuple-element.67), channel_id=1, source_target_pairs={{0,16},{4,20},{9,25},{13,29},{18,2},{22,6},{27,11},{31,15},{16,24}... | collective-permute-start | bytes 1572872 | tf_op jit(solution)/shard_map/ppermute | solution.py:331
  225.6 9.0 %shard_map.78.before = f32[2048,512]{1,0:T(8,128)S(1)} custom-call(s32[10]{0:T(128)S(1)} %pad_add_fusion.meta, f32[2048,4096]{1,0:T(8,128)} %s_oth.11, f32[2048,4096]{1,0:T(8,128)} %s_oth.11, bf16[1024,512]{1,0:T(8,128)(2,1)S(1)} %pad_maximum_fusion.8.own, bf16[1024,512]{1,0:T(8,128)(2,1)S(1)} %collective-permute-done.29.oth), custom_call_target="tpu_custom_call" | custom-call | flops 8589934592 | bytes 16777216 | tf_op jit(solution)/shard_map/pallas_call | solution.py:137
  234.7 9.0 %shard_map.77.before = f32[2048,512]{1,0:T(8,128)S(1)} custom-call(s32[10]{0:T(128)S(1)} %pad_add_fusion.meta, f32[2048,4096]{1,0:T(8,128)} %s_oth.11, f32[2048,4096]{1,0:T(8,128)} %s_oth.11, bf16[1024,512]{1,0:T(8,128)(2,1)S(1)} %pad_maximum_fusion.6.own, bf16[1024,512]{1,0:T(8,128)(2,1)S(1)} %collective-permute-done.27.oth), custom_call_target="tpu_custom_call" | custom-call | flops 8589934592 | bytes 16777216 | tf_op jit(solution)/shard_map/pallas_call | solution.py:137
  243.7 9.4 %shard_map.79 = (f32[4,2048,128]{2,1,0:T(8,128)S(1)}, s16[1040,128]{1,0:T(8,128)(2,1)S(1)}, s16[1040,128]{1,0:T(8,128)(2,1)S(1)}) custom-call(s32[10]{0:T(128)S(1)} %pad_add_fusion.meta, f32[2048,4096]{1,0:T(8,128)} %s_oth.11, f32[2048,4096]{1,0:T(8,128)} %s_oth.11, bf16[1024,512]{1,0:T(8,128)(2,1)S(1)} %pad_maximum_fusion.7.own, ...), custom_call_target="tpu_custom_call" | custom-call | flops 8589934592 | bytes 16777216 | tf_op jit(solution)/shard_map/pallas_call | solution.py:166
  253.2 22.6 %collective-permute-start.38 = (s16[1040,128]{1,0:T(8,128)(2,1)S(1)}, s16[1040,128]{1,0:T(8,128)(2,1)S(1)}, u32[]{:S(2)}, u32[]{:S(2)}) collective-permute-start(s16[1040,128]{1,0:T(8,128)(2,1)S(1)} %get-tuple-element.35), channel_id=1, source_target_pairs={{0,1},{1,2},{2,3},{3,0},{4,5},{5,6},{6,7},{7,4},{8,9},{9,10},{10,1... | collective-permute-start | bytes 798728 | tf_op jit(solution)/shard_map/ppermute | solution.py:41
  276.9 9.7 %shard_map.80 = (f32[4,2048,128]{2,1,0:T(8,128)S(1)}, s16[1040,128]{1,0:T(8,128)(2,1)S(1)}, s16[1040,128]{1,0:T(8,128)(2,1)S(1)}) custom-call(s32[10]{0:T(128)S(1)} %pad_add_fusion.meta, f32[2048,4096]{1,0:T(8,128)} %s_oth.11, f32[2048,4096]{1,0:T(8,128)} %s_oth.11, bf16[1024,512]{1,0:T(8,128)(2,1)S(1)} %pad_maximum_fusion.5.own, ...), custom_call_target="tpu_custom_call" | custom-call | flops 8589934592 | bytes 16777216 | tf_op jit(solution)/shard_map/pallas_call | solution.py:166
  298.0 9.4 %collective-permute-done.35.got_left = s16[1040,128]{1,0:T(8,128)(2,1)S(1)} collective-permute-done((s16[1040,128]{1,0:T(8,128)(2,1)S(1)}, s16[1040,128]{1,0:T(8,128)(2,1)S(1)}, u32[]{:S(2)}, u32[]{:S(2)}) %collective-permute-start.35) | collective-permute-done | bytes 266272 | tf_op jit(solution)/shard_map/ppermute | solution.py:41
  314.9 15.0 %collective-permute-done.41.got_left = s16[2064,128]{1,0:T(8,128)(2,1)S(1)} collective-permute-done((s16[2064,128]{1,0:T(8,128)(2,1)}, s16[2064,128]{1,0:T(8,128)(2,1)S(1)}, u32[]{:S(2)}, u32[]{:S(2)}) %collective-permute-start.41) | collective-permute-done | bytes 528416 | tf_op jit(solution)/shard_map/ppermute | solution.py:41
  349.5 17.4 %collective-permute-start.43 = (f32[64,1024]{1,0:T(8,128)S(1)}, f32[64,1024]{1,0:T(8,128)}, u32[]{:S(2)}, u32[]{:S(2)}) collective-permute-start(f32[64,1024]{1,0:T(8,128)S(1)} %dynamic-slice_add_fusion.1), channel_id=1, source_target_pairs={{0,8},{4,12},{8,0},{12,4},{16,24},{20,28},{24,16},{28,20},{1,9},{5... | collective-permute-start | bytes 786440 | tf_op jit(solution)/shard_map/ppermute | solution.py:45
  398.5 9.0 %shard_map.76.before = f32[2048,512]{1,0:T(8,128)S(1)} custom-call(s32[10]{0:T(128)S(1)} %pad_add_fusion.meta, f32[2048,4096]{1,0:T(8,128)} %s_oth.11, f32[2048,4096]{1,0:T(8,128)} %s_oth.11, bf16[1024,512]{1,0:T(8,128)(2,1)S(1)} %pad_maximum_fusion.3.own, bf16[1024,512]{1,0:T(8,128)(2,1)S(1)} %collective-permute-done.21.oth), custom_call_target="tpu_custom_call" | custom-call | flops 8589934592 | bytes 16777216 | tf_op jit(solution)/shard_map/pallas_call | solution.py:137
  410.1 12.1 %collective-permute-done.46 = f32[64,640]{1,0:T(8,128)S(1)} collective-permute-done((f32[64,640]{1,0:T(8,128)S(1)}, f32[64,640]{1,0:T(8,128)S(1)}, u32[]{:S(2)}, u32[]{:S(2)}) %collective-permute-start.46) | collective-permute-done | bytes 163872 | tf_op jit(solution)/shard_map/ppermute | solution.py:41
  423.5 9.7 %shard_map.81 = (f32[4,2048,128]{2,1,0:T(8,128)S(1)}, s16[1040,128]{1,0:T(8,128)(2,1)S(1)}, s16[1040,128]{1,0:T(8,128)(2,1)S(1)}) custom-call(s32[10]{0:T(128)S(1)} %pad_add_fusion.meta, f32[2048,4096]{1,0:T(8,128)} %s_oth.11, f32[2048,4096]{1,0:T(8,128)} %s_oth.11, bf16[1024,512]{1,0:T(8,128)(2,1)S(1)} %pad_maximum_fusion.2.own, ...), custom_call_target="tpu_custom_call" | custom-call | flops 8589934592 | bytes 16777216 | tf_op jit(solution)/shard_map/pallas_call | solution.py:166
  468.2 8.3 %collective-permute-done.33.got_left = s16[2064,128]{1,0:T(8,128)(2,1)S(1)} collective-permute-done((s16[2064,128]{1,0:T(8,128)(2,1)S(1)}, s16[2064,128]{1,0:T(8,128)(2,1)S(1)}, u32[]{:S(2)}, u32[]{:S(2)}) %collective-permute-start.33) | collective-permute-done | bytes 528416 | tf_op jit(solution)/shard_map/ppermute | solution.py:41
  489.8 8.6 %collective-permute-done.53 = f32[64,640]{1,0:T(8,128)S(1)} collective-permute-done((f32[64,640]{1,0:T(8,128)S(1)}, f32[64,640]{1,0:T(8,128)S(1)}, u32[]{:S(2)}, u32[]{:S(2)}) %collective-permute-start.53) | collective-permute-done | bytes 163872 | tf_op jit(solution)/shard_map/ppermute | solution.py:41
  501.8 10.7 %collective-permute-start.57 = (f32[64,512]{1,0:T(8,128)S(1)}, f32[64,512]{1,0:T(8,128)S(1)}, u32[]{:S(2)}, u32[]{:S(2)}) collective-permute-start(f32[64,512]{1,0:T(8,128)S(1)} %dynamic-slice_add_fusion.2), channel_id=1, source_target_pairs={{0,8},{4,12},{8,0},{12,4},{16,24},{20,28},{24,16},{28,20},{1,9},{5... | collective-permute-start | bytes 393224 | tf_op jit(solution)/shard_map/ppermute | solution.py:45
  (302 shorter events, 246.4 us)
Async XLA Ops:
  2.8 16.0 %collective-permute-start.11 = (bf16[512,512]{1,0:T(8,128)(2,1)S(1)}, bf16[512,512]{1,0:T(8,128)(2,1)S(1)}, u32[]{:S(2)}, u32[]{:S(2)}) collective-permute-start(bf16[512,512]{1,0:T(8,128)(2,1)S(1)} %bitcast_select_fusion.3), channel_id=1, source_target_pairs={{0,8},{4,12},{9,1},{13,5},{18,26},{22,30},{27,19},{31,23}} | collective-permute-start | bytes 1572872 | tf_op jit(solution)/shard_map/ppermute | solution.py:331
  55.5 34.0 %collective-permute-start.16 = (bf16[512,512]{1,0:T(8,128)(2,1)S(1)}, bf16[512,512]{1,0:T(8,128)(2,1)S(1)}, u32[]{:S(2)}, u32[]{:S(2)}) collective-permute-start(bf16[512,512]{1,0:T(8,128)(2,1)S(1)} %get-tuple-element.62), channel_id=1, source_target_pairs={{0,16},{4,20},{9,25},{13,29},{18,2},{22,6},{27,11},{31,15}} | collective-permute-start | bytes 1572872 | tf_op jit(solution)/shard_map/ppermute | solution.py:331
  117.1 14.8 %collective-permute-start.5 = (bf16[512,512]{1,0:T(8,128)(2,1)S(1)}, bf16[512,512]{1,0:T(8,128)(2,1)S(1)}, u32[]{:S(2)}, u32[]{:S(2)}) collective-permute-start(bf16[512,512]{1,0:T(8,128)(2,1)S(1)} %get-tuple-element.63), channel_id=1, source_target_pairs={{0,16},{4,20},{9,25},{13,29},{18,2},{22,6},{27,11},{31,15}} | collective-permute-start | bytes 1572872 | tf_op jit(solution)/shard_map/ppermute | solution.py:331
  136.0 24.5 %collective-permute-start.1 = (bf16[512,512]{1,0:T(8,128)(2,1)S(1)}, bf16[512,512]{1,0:T(8,128)(2,1)S(1)}, u32[]{:S(2)}, u32[]{:S(2)}) collective-permute-start(bf16[512,512]{1,0:T(8,128)(2,1)S(1)} %get-tuple-element.66), channel_id=1, source_target_pairs={{0,8},{4,12},{9,1},{13,5},{18,26},{22,30},{27,19},{31,23},{8,24},{... | collective-permute-start | bytes 1572872 | tf_op jit(solution)/shard_map/ppermute | solution.py:331
  193.2 23.6 %collective-permute-start.7 = (bf16[512,512]{1,0:T(8,128)(2,1)}, bf16[512,512]{1,0:T(8,128)(2,1)}, u32[]{:S(2)}, u32[]{:S(2)}) collective-permute-start(bf16[512,512]{1,0:T(8,128)(2,1)} %get-tuple-element.67), channel_id=1, source_target_pairs={{0,16},{4,20},{9,25},{13,29},{18,2},{22,6},{27,11},{31,15},{16,24}... | collective-permute-start | bytes 1572872 | tf_op jit(solution)/shard_map/ppermute | solution.py:331
  225.2 18.6 %collective-permute-start.28 = (bf16[1024,512]{1,0:T(8,128)(2,1)S(1)}, bf16[1024,512]{1,0:T(8,128)(2,1)S(1)}, u32[]{:S(2)}, u32[]{:S(2)}) collective-permute-start(bf16[1024,512]{1,0:T(8,128)(2,1)S(1)} %pad_maximum_fusion.7.own), channel_id=1, source_target_pairs={{0,4},{4,0},{8,12},{12,8},{16,20},{20,16},{24,28},{28,24},{1,5},{5... | collective-permute-start | bytes 3145736 | tf_op jit(solution)/shard_map/ppermute | solution.py:45
  234.6 42.3 %collective-permute-start.26 = (bf16[1024,512]{1,0:T(8,128)(2,1)S(1)}, bf16[1024,512]{1,0:T(8,128)(2,1)S(1)}, u32[]{:S(2)}, u32[]{:S(2)}) collective-permute-start(bf16[1024,512]{1,0:T(8,128)(2,1)S(1)} %pad_maximum_fusion.5.own), channel_id=1, source_target_pairs={{0,4},{4,0},{8,12},{12,8},{16,20},{20,16},{24,28},{28,24},{1,5},{5... | collective-permute-start | bytes 3145736 | tf_op jit(solution)/shard_map/ppermute | solution.py:45
  253.2 37.4 %collective-permute-start.38 = (s16[1040,128]{1,0:T(8,128)(2,1)S(1)}, s16[1040,128]{1,0:T(8,128)(2,1)S(1)}, u32[]{:S(2)}, u32[]{:S(2)}) collective-permute-start(s16[1040,128]{1,0:T(8,128)(2,1)S(1)} %get-tuple-element.35), channel_id=1, source_target_pairs={{0,1},{1,2},{2,3},{3,0},{4,5},{5,6},{6,7},{7,4},{8,9},{9,10},{10,1... | collective-permute-start | bytes 798728 | tf_op jit(solution)/shard_map/ppermute | solution.py:41
  275.8 14.7 %collective-permute-start.39 = (s16[1040,128]{1,0:T(8,128)(2,1)S(1)}, s16[1040,128]{1,0:T(8,128)(2,1)S(1)}, u32[]{:S(2)}, u32[]{:S(2)}) collective-permute-start(s16[1040,128]{1,0:T(8,128)(2,1)S(1)} %get-tuple-element.36), channel_id=1, source_target_pairs={{0,3},{1,0},{2,1},{3,2},{4,7},{5,4},{6,5},{7,6},{8,11},{9,8},{10,9... | collective-permute-start | bytes 798728 | tf_op jit(solution)/shard_map/ppermute | solution.py:41
  287.7 19.7 %collective-permute-start.35 = (s16[1040,128]{1,0:T(8,128)(2,1)S(1)}, s16[1040,128]{1,0:T(8,128)(2,1)S(1)}, u32[]{:S(2)}, u32[]{:S(2)}) collective-permute-start(s16[1040,128]{1,0:T(8,128)(2,1)S(1)} %get-tuple-element.32), channel_id=1, source_target_pairs={{0,3},{1,0},{2,1},{3,2},{4,7},{5,4},{6,5},{7,6},{8,11},{9,8},{10,9... | collective-permute-start | bytes 798728 | tf_op jit(solution)/shard_map/ppermute | solution.py:41
  292.5 22.4 %collective-permute-start.40 = (s16[2064,128]{1,0:T(8,128)(2,1)}, s16[2064,128]{1,0:T(8,128)(2,1)S(1)}, u32[]{:S(2)}, u32[]{:S(2)}) collective-permute-start(s16[2064,128]{1,0:T(8,128)(2,1)} %get-tuple-element.37), channel_id=1, source_target_pairs={{0,1},{1,2},{2,3},{3,0},{4,5},{5,6},{6,7},{7,4},{8,9},{9,10},{10,1... | collective-permute-start | bytes 1585160 | tf_op jit(solution)/shard_map/ppermute | solution.py:41
  292.5 37.5 %collective-permute-start.41 = (s16[2064,128]{1,0:T(8,128)(2,1)}, s16[2064,128]{1,0:T(8,128)(2,1)S(1)}, u32[]{:S(2)}, u32[]{:S(2)}) collective-permute-start(s16[2064,128]{1,0:T(8,128)(2,1)} %get-tuple-element.38), channel_id=1, source_target_pairs={{0,3},{1,0},{2,1},{3,2},{4,7},{5,4},{6,5},{7,6},{8,11},{9,8},{10,9... | collective-permute-start | bytes 1585160 | tf_op jit(solution)/shard_map/ppermute | solution.py:41
  309.4 30.1 %collective-permute-start.36 = (s16[2064,128]{1,0:T(8,128)(2,1)}, s16[2064,128]{1,0:T(8,128)(2,1)S(1)}, u32[]{:S(2)}, u32[]{:S(2)}) collective-permute-start(s16[2064,128]{1,0:T(8,128)(2,1)} %get-tuple-element.33), channel_id=1, source_target_pairs={{0,1},{1,2},{2,3},{3,0},{4,5},{5,6},{6,7},{7,4},{8,9},{9,10},{10,1... | collective-permute-start | bytes 1585160 | tf_op jit(solution)/shard_map/ppermute | solution.py:41
  309.4 34.5 %collective-permute-start.37 = (s16[2064,128]{1,0:T(8,128)(2,1)}, s16[2064,128]{1,0:T(8,128)(2,1)S(1)}, u32[]{:S(2)}, u32[]{:S(2)}) collective-permute-start(s16[2064,128]{1,0:T(8,128)(2,1)} %get-tuple-element.34), channel_id=1, source_target_pairs={{0,3},{1,0},{2,1},{3,2},{4,7},{5,4},{6,5},{7,6},{8,11},{9,8},{10,9... | collective-permute-start | bytes 1585160 | tf_op jit(solution)/shard_map/ppermute | solution.py:41
  348.3 18.6 %collective-permute-start.49 = (f32[64,1024]{1,0:T(8,128)S(1)}, f32[64,1024]{1,0:T(8,128)S(1)}, u32[]{:S(2)}, u32[]{:S(2)}) collective-permute-start(f32[64,1024]{1,0:T(8,128)S(1)} %constant_dynamic-slice_fusion.7), channel_id=1, source_target_pairs={{0,4},{4,0},{8,12},{12,8},{16,20},{20,16},{24,28},{28,24},{1,5},{5... | collective-permute-start | bytes 786440 | tf_op jit(solution)/shard_map/ppermute | solution.py:45
  349.5 24.6 %collective-permute-start.43 = (f32[64,1024]{1,0:T(8,128)S(1)}, f32[64,1024]{1,0:T(8,128)}, u32[]{:S(2)}, u32[]{:S(2)}) collective-permute-start(f32[64,1024]{1,0:T(8,128)S(1)} %dynamic-slice_add_fusion.1), channel_id=1, source_target_pairs={{0,8},{4,12},{8,0},{12,4},{16,24},{20,28},{24,16},{28,20},{1,9},{5... | collective-permute-start | bytes 786440 | tf_op jit(solution)/shard_map/ppermute | solution.py:45
  367.8 30.7 %collective-permute-start.21 = (bf16[1024,512]{1,0:T(8,128)(2,1)S(1)}, bf16[1024,512]{1,0:T(8,128)(2,1)S(1)}, u32[]{:S(2)}, u32[]{:S(2)}) collective-permute-start(bf16[1024,512]{1,0:T(8,128)(2,1)S(1)} %pad_maximum_fusion.3.own), channel_id=1, source_target_pairs={{0,4},{4,0},{8,12},{12,8},{16,20},{20,16},{24,28},{28,24},{1,5},{5... | collective-permute-start | bytes 3145736 | tf_op jit(solution)/shard_map/ppermute | solution.py:45
  375.2 19.4 %collective-permute-start.44 = (f32[64,1024]{1,0:T(8,128)S(1)}, f32[64,1024]{1,0:T(8,128)}, u32[]{:S(2)}, u32[]{:S(2)}) collective-permute-start(f32[64,1024]{1,0:T(8,128)S(1)} %add.144), channel_id=1, source_target_pairs={{0,16},{4,20},{8,24},{12,28},{16,0},{20,4},{24,8},{28,12},{1,17},{... | collective-permute-start | bytes 786440 | tf_op jit(solution)/shard_map/ppermute | solution.py:45
  407.5 15.7 %collective-permute-start.10 = (bf16[1024,512]{1,0:T(8,128)(2,1)S(1)}, bf16[1024,512]{1,0:T(8,128)(2,1)S(1)}, u32[]{:S(2)}, u32[]{:S(2)}) collective-permute-start(bf16[1024,512]{1,0:T(8,128)(2,1)S(1)} %pad_maximum_fusion.2.own), channel_id=1, source_target_pairs={{0,4},{4,0},{8,12},{12,8},{16,20},{20,16},{24,28},{28,24},{1,5},{5... | collective-permute-start | bytes 3145736 | tf_op jit(solution)/shard_map/ppermute | solution.py:45
  423.3 32.0 %collective-permute-start.48 = (f32[4,64,640]{2,1,0:T(8,128)}, f32[4,64,640]{2,1,0:T(8,128)}, u32[]{:S(2)}, u32[]{:S(2)}) collective-permute-start(f32[4,64,640]{2,1,0:T(8,128)} %constant_dynamic-slice_fusion.9), channel_id=1, source_target_pairs={{0,4},{4,0},{8,12},{12,8},{16,20},{20,16},{24,28},{28,24},{1,5},{5... | collective-permute-start | bytes 1966088 | tf_op jit(solution)/shard_map/ppermute | solution.py:45
  451.4 16.8 %collective-permute-start.32 = (s16[2064,128]{1,0:T(8,128)(2,1)S(1)}, s16[2064,128]{1,0:T(8,128)(2,1)S(1)}, u32[]{:S(2)}, u32[]{:S(2)}) collective-permute-start(s16[2064,128]{1,0:T(8,128)(2,1)S(1)} %get-tuple-element.29), channel_id=1, source_target_pairs={{0,1},{1,2},{2,3},{3,0},{4,5},{5,6},{6,7},{7,4},{8,9},{9,10},{10,1... | collective-permute-start | bytes 1585160 | tf_op jit(solution)/shard_map/ppermute | solution.py:41
  451.4 25.0 %collective-permute-start.33 = (s16[2064,128]{1,0:T(8,128)(2,1)S(1)}, s16[2064,128]{1,0:T(8,128)(2,1)S(1)}, u32[]{:S(2)}, u32[]{:S(2)}) collective-permute-start(s16[2064,128]{1,0:T(8,128)(2,1)S(1)} %get-tuple-element.30), channel_id=1, source_target_pairs={{0,3},{1,0},{2,1},{3,2},{4,7},{5,4},{6,5},{7,6},{8,11},{9,8},{10,9... | collective-permute-start | bytes 1585160 | tf_op jit(solution)/shard_map/ppermute | solution.py:41
  461.1 28.7 %collective-permute-start.52 = (f32[64,640]{1,0:T(8,128)S(1)}, f32[64,640]{1,0:T(8,128)S(1)}, u32[]{:S(2)}, u32[]{:S(2)}) collective-permute-start(f32[64,640]{1,0:T(8,128)S(1)} %get-tuple-element.92), channel_id=1, source_target_pairs={{0,3},{1,0},{2,1},{3,2},{4,7},{5,4},{6,5},{7,6},{8,11},{9,8},{10,9... | collective-permute-start | bytes 491528 | tf_op jit(solution)/shard_map/ppermute | solution.py:41
  499.5 24.5 %collective-permute-start.55 = (f32[4,64,640]{2,1,0:T(8,128)}, f32[4,64,640]{2,1,0:T(8,128)}, u32[]{:S(2)}, u32[]{:S(2)}) collective-permute-start(f32[4,64,640]{2,1,0:T(8,128)} %constant_dynamic-slice_fusion.2), channel_id=1, source_target_pairs={{0,4},{4,0},{8,12},{12,8},{16,20},{20,16},{24,28},{28,24},{1,5},{5... | collective-permute-start | bytes 1966088 | tf_op jit(solution)/shard_map/ppermute | solution.py:45
  (81 other events, 923.7 us)

commit v3 on v2

--- a/solution.py
+++ b/solution.py
@@ -11,6 +11,8 @@
 PAD = 16
 LANES = 2
 STREAMS = 2
+FEED_COST = 10_000_000_000
+HEAD = 4
 
 precise = lax.Precision.HIGHEST
 f32 = jnp.float32
@@ -60,7 +62,7 @@
 
 
 def first_kernel(meta, s_own, s_oth, own, oth, total):
-    @pl.when(meta[2 + pl.program_id(0)] > 0)
+    @pl.when(meta[HEAD + pl.program_id(0)] > 0)
     def _():
         total[...] = split_dot(s_own[...], own[...]) + split_dot(s_oth[...], oth[...])
 
@@ -92,7 +94,7 @@
         def _():
             out_b[pl.ds(pl.multiple_of(at - half, TILE), TILE), :] = quant
 
-    listed = meta[2 + step] > 0
+    listed = meta[HEAD + step] > 0
 
     @pl.when(listed)
     def _():
@@ -310,10 +312,121 @@
     )
 
 
-def gather_chain(chunks, turn, order, row_size):
-    size, supernodes = len(order), len(chunks)
+def after(value, *others):
+    return lax.optimization_barrier((value, *others))[0]
+
+
+def own_blocks(meta, row, rows):
+    block = min(rows, TILE)
+    return [(at, block, meta[HEAD + (row + at) // TILE]) for at in range(0, rows, block)]
+
+
+def feed_kernel(spots, meta, *refs):
+    ways = len(spots)
+    own, outs = refs[:ways], refs[-ways:]
+    arrived = refs[ways:-ways]
+    for way, row in enumerate(spots):
+        out = outs[way]
+
+        def fill(way=way, row=row, out=out):
+            for at, block, flag in own_blocks(meta, row, out.shape[0]):
+                value = own[way][0, at : at + block, :]
+                out[at : at + block, :] = jnp.where(flag > 0, value, jnp.zeros_like(value))
+
+        if not arrived:
+            fill()
+        else:
+            first = meta[2 + way] == 0
+            pl.when(first)(fill)
+
+            @pl.when(jnp.logical_not(first))
+            def _(way=way, out=out):
+                out[...] = arrived[way][...]
+
+
+def feed(meta, panels, k, stream, arrived):
+    _, rows, width = panels.shape
+    ways = 2
+    piece = rows // (ways * STREAMS)
+    block = pl.BlockSpec((piece, width), lambda i, m: (0, 0))
+    return pl.pallas_call(
+        functools.partial(feed_kernel, [(stream * ways + way) * piece for way in range(ways)]),
+        grid_spec=pltpu.PrefetchScalarGridSpec(
+            num_scalar_prefetch=1,
+            grid=(1,),
+            in_specs=[
+                pl.BlockSpec((1, piece, width), lambda i, m, w=w: (k, stream * ways + w, 0))
+                for w in range(ways)
+            ]
+            + [block] * len(arrived),
+            out_specs=[block] * ways,
+        ),
+        out_shape=[jax.ShapeDtypeStruct((piece, width), bf16)] * ways,
+        cost_estimate=pl.CostEstimate(flops=FEED_COST, bytes_accessed=0, transcendentals=0),
+    )(meta, *[panels] * ways, *arrived)
+
+
+def pick_kernel(k, spots, meta, panels, *refs):
+    ways = len(spots)
+    zeros, sems = refs[-2:]
+    out = refs[-3]
+    turns = len(refs[:-3]) // ways
+    piece = out.shape[0] // ways
+    zeros[...] = jnp.zeros_like(zeros)
+
+    def each(act):
+        for way, row in enumerate(spots):
+            base = way * piece
+            turn = meta[2 + way]
+            for t in range(turns):
+
+                @pl.when(turn == t + 1)
+                def _(way=way, t=t, base=base):
+                    target = out.at[pl.ds(base, piece)]
+                    act(pltpu.make_async_copy(refs[way * turns + t], target, sems.at[way, 0]))
+
+            for n, (at, block, flag) in enumerate(own_blocks(meta, row, piece)):
+                target = out.at[pl.ds(base + at, block)]
+
+                @pl.when((turn == 0) & (flag > 0))
+                def _(way=way, n=n, row=row, at=at, block=block, target=target):
+                    source = panels.at[k, pl.ds(row + at, block)]
+                    act(pltpu.make_async_copy(source, target, sems.at[way, n]))
+
+                @pl.when((turn == 0) & (flag == 0))
+                def _(way=way, n=n, target=target):
+                    act(pltpu.make_async_copy(zeros, target, sems.at[way, n]))
+
+    each(lambda copy: copy.start())
+    each(lambda copy: copy.wait())
+
+
+def pick(meta, panels, k, stream, received):
+    _, rows, width = panels.shape
+    ways = len(received)
+    piece = rows // (ways * STREAMS)
+    block = min(piece, TILE)
+    operands = [panels] + [value for way in received for value in way]
+    return pl.pallas_call(
+        functools.partial(pick_kernel, k, [(stream * ways + way) * piece for way in range(ways)]),
+        grid_spec=pltpu.PrefetchScalarGridSpec(
+            num_scalar_prefetch=1,
+            grid=(1,),
+            in_specs=[pl.BlockSpec(memory_space=pl.ANY)] * len(operands),
+            out_specs=pl.BlockSpec(memory_space=pl.ANY),
+            scratch_shapes=[
+                pltpu.VMEM((block, width), bf16),
+                pltpu.SemaphoreType.DMA((ways, piece // block)),
+            ],
+        ),
+        out_shape=jax.ShapeDtypeStruct((ways * piece, width), bf16),
+    )(meta, *operands)
+
+
+def send_on(values, orders, step, supernodes):
+    size = len(orders[0])
     got = []
-    for step in range(supernodes + size - 2):
+    for value, order in zip(values, orders):
         pairs = []
         for t in range(size - 1):
             if 0 <= step - t < supernodes:
@@ -322,20 +435,8 @@
                         source = ((c ^ order[t]) * LANES + i) * size + c
                         target = ((c ^ order[t + 1]) * LANES + i) * size + c
                         pairs.append((source, target))
-        if step == 0:
-            value = chunks[0]
-        elif step < supernodes:
-            value = jnp.where(turn == 0, chunks[step], got[step - 1])
-        else:
-            value = got[step - 1]
         got.append(lax.ppermute(value, BOTH, pairs))
-    found = []
-    for k in range(supernodes):
-        value = chunks[k]
-        for t in range(1, size):
-            value = jnp.where(turn == t, got[k + t - 1], value)
-        found.append(value)
-    return found
+    return got
 
 
 def local(inverse_block, tile_list, panels, links, diag_inverse):
@@ -348,28 +449,18 @@
     tiles_here = rows_here // TILE
     tiles = row_number * tiles_here + jnp.arange(tiles_here, dtype=jnp.int32)
     flags = jnp.any(tile_list[None, :] == tiles[:, None], axis=1)
-    row_mask = jnp.broadcast_to(flags[:, None], (tiles_here, TILE)).reshape(-1, 1)
-    meta = jnp.concatenate(
-        [jnp.stack([lane, col_number]).astype(jnp.int32), flags.astype(jnp.int32)]
-    )
 
     order = [t ^ (t >> 1) for t in range(col_size)]
     back = [order[-t] for t in range(col_size)]
+    orders = (order, back)
     relative = place ^ col_number
     turn = sum(jnp.where(relative == order[t], t, 0) for t in range(col_size))
-    turn_back = (col_size - turn) % col_size
-    piece = rows_here // (2 * STREAMS)
-    found = []
-    for stream in range(STREAMS):
-        ways = []
-        for way, (path, at) in enumerate(((order, turn), (back, turn_back))):
-            rows = slice((2 * stream + way) * piece, (2 * stream + way + 1) * piece)
-            chunks = [
-                jnp.where(row_mask[rows], panels[k, rows], jnp.zeros((), bf16))
-                for k in range(supernodes)
-            ]
-            ways.append(gather_chain(chunks, at, path, row_size))
-        found.append(ways)
+    meta = jnp.concatenate(
+        [
+            jnp.stack([lane, col_number, turn, (col_size - turn) % col_size]).astype(jnp.int32),
+            flags.astype(jnp.int32),
+        ]
+    )
 
     flat = links.reshape(-1, width)
     half = flat.shape[0] // 2
@@ -380,21 +471,70 @@
     link_full = link_full.transpose(1, 0, 2, 3).reshape(supernodes - 1, width, width)
 
     cross_parts, diag_parts = [], []
-    part = carried = cross = stacked = full_turned = None
+    carried = cross = stacked = full_turned = None
+    events = []
+    steps = supernodes + col_size - 2
+    parts = []
+    befores = []
+    done = 0
+
+    def arrive(n):
+        nonlocal done
+        while done < 2 * supernodes and 2 * (done // 2 + col_size - 2) + done % 2 <= n:
+            k, stream = done // 2, done % 2
+            received = [
+                [events[2 * (k + t - 1) + stream][way] for t in range(1, col_size)]
+                for way in range(2)
+            ]
+            own = pick(meta, panels, k, stream, received)
+            oth = swap(own, 1, row_size)
+            link = None if k == 0 else link_full[k - 1]
+            if stream == 0:
+                if k > 0:
+                    own = after(own, parts[-1][0])
+                befores.append(panel_first(meta, inverse_block, own, oth))
+            else:
+                parts.append(
+                    panel_second(
+                        meta, inverse_block, own, oth, befores[-1], link,
+                        parts[-1][0] if k > 0 else None, col_size,
+                    )
+                )
+            done += 1
+
+    for step in range(steps):
+        for stream in range(STREAMS):
+            arrived = events[-STREAMS] if step > 0 else []
+            if step < supernodes:
+                values = feed(meta, panels, step, stream, arrived)
+            else:
+                values = arrived
+            tie = events[-STREAMS - 1] if len(events) > STREAMS else []
+            if len(events) == 2 * col_size - 1 and befores:
+                tie = tie + befores[:1]
+            elif len(events) == 2 * col_size + 1 and parts:
+                tie = tie + [parts[0][0]]
+            values = lax.optimization_barrier((*values, *tie))[: len(orders)]
+            events.append(send_on(values, orders, step, supernodes))
+            arrive(len(events) - 1)
+    hops = []
+    for part, right, left in parts:
+        stages = []
+        for hop in range(col_size // 2 - 1, -1, -1):
+            right, left = shift(right, 1, col_size), shift(left, -1, col_size)
+            stages.append((right, left))
+            if hop > 0:
+                right, left = pass_on(meta, part, right, left, hop)
+                stages.append((right, left))
+        hops.append(stages)
+    gates = [[befores[-1]]] + [hops[-1][0]] * (supernodes - 2) + [()]
     for k in range(supernodes):
         last = k + 1 == supernodes
-        own = [jnp.concatenate([found[s][0][k], found[s][1][k]], axis=0) for s in range(STREAMS)]
-        oth = [swap(value, 1, row_size) for value in own]
-        before = panel_first(meta, inverse_block, own[0], oth[0])
         link = None if k == 0 else link_full[k - 1]
-        part, right, left = panel_second(
-            meta, inverse_block, own[1], oth[1], before, link, part, col_size
-        )
-        for hop in range(col_size // 2 - 1, -1, -1):
-            right, left = shift(right, 1, col_size), shift(left, -1, col_size)
-            if hop > 0:
-                right, left = pass_on(meta, part, right, left, hop)
+        part = parts[k][0]
+        right, left = hops[k][-1]
         carried, sums = sum_parts(meta, part, right, left, panels, k, carried)
+        sums = after(sums, *gates[k])
 
         summed = row_sum_half(sums, lane, row_size)
         mine = lax.dynamic_slice_in_dim(diag_inverse[k], lane * (share // 2), share // 2, 1).T
@@ -414,6 +554,7 @@
                 at = (col_number + s) % col_size * share
                 block = lax.dynamic_slice_in_dim(summed[:, width:], at, share, 1)
                 message = jnp.concatenate([turned, block], axis=1)
+                message = after(message, *hops[-1][min(1, len(hops[-1]) - 1)])
                 arrived.append(shift(message, s, col_size) if s else message)
             ordered = both_halves(around(arrived, col_number), lane, row_size, 1)
             full_turned = ordered[:, :, :width].reshape(width, width)

time: 534 us -> 563 us (1.054)
  waiting for transfers between devices: 177 us -> 73.3 us
  starting transfers between devices: 207 us -> 287 us
  Pallas kernels: 73.6 us -> 132 us
  other arithmetic: 35 us -> 13.8 us
  local copies, waits for them, and re-layouts: 32.6 us -> 47.2 us
    ppermute x21, starting transfers between devices: 54.3 us -> 194 us  [shift(): lax.ppermute(value, 'col', [(z, (z + by) % size) for z in range(size)])]
    ppermute x20, waiting for transfers between devices: 79.1 us -> 18.8 us  [send_on(): got.append(lax.ppermute(value, BOTH, pairs))]
    pallas_call x0 -> x12, Pallas kernels: none -> 53.2 us  [the longest x6 34.4 us: pick(): pl.pallas_call(functools.partial(pick_kernel, k, [(stream * ways + way) *...]
    ppermute x20, starting transfers between devices: 107 us -> 63.1 us  [send_on(): got.append(lax.ppermute(value, BOTH, pairs))]
    ppermute x21, waiting for transfers between devices: 83.3 us -> 40 us  [shift(): lax.ppermute(value, 'col', [(z, (z + by) % size) for z in range(size)])]
    select_n x11 -> x0, other arithmetic: 19.8 us -> none  [the longest x5 11.8 us: gather_chain(): value = jnp.where(turn == t, got[k + t - 1], value)]
    ppermute x19, starting transfers between devices: 45.4 us -> 29.4 us  [swap(): return lax.ppermute(value, 'row', [(r, r ^ bit) for r in range(size)])]
    unnamed x108 -> x124, local copies, waits for them, and re-layouts: 21.4 us -> 37.3 us
  transfers between devices with their start and end apart: 60 -> 60, of which waited for: 30 -> 24; matrix products, arithmetic and copies ran while one was open for 6% -> 5% of each run, Pallas kernels for 14% -> 24%
where the time goes in v3:
time: 563 us; the launch traced here: 559 us
  starting transfers between devices  287 us (51%)
  Pallas kernels  132 us (23%)
  waiting for transfers between devices  73.3 us (13%)
  local copies, waits for them, and re-layouts  47.2 us (8%)
  other arithmetic  13.8 us (2%)
    ppermute x21, starting transfers between devices, shift(): lax.ppermute(value, 'col', [(z, (z + by) % size) for z in range(size)])  194 us
    ppermute x20, starting transfers between devices, send_on(): got.append(lax.ppermute(value, BOTH, pairs))  63.1 us
    ppermute x21, waiting for transfers between devices, shift(): lax.ppermute(value, 'col', [(z, (z + by) % size) for z in range(size)])  40 us
    unnamed x124, local copies, waits for them, and re-layouts  37.3 us
    pallas_call x6, Pallas kernels, pick(): pl.pallas_call(functools.partial(pick_kernel, k, [(stream * ways + way) *...  34.4 us
    pallas_call x3, Pallas kernels, panel_second(): pl.pallas_call(functools.partial(second_kernel, cols, link is not None),...  31 us
    ppermute x19, starting transfers between devices, swap(): return lax.ppermute(value, 'row', [(r, r ^ bit) for r in range(size)])  29.4 us
    pallas_call x3, Pallas kernels, panel_first(): pl.pallas_call(first_kernel, grid_spec=pltpu.PrefetchScalarGridSpec(num_s...  27.3 us
  transfers between devices with their start and end apart: 60, of which 24 were waited for; matrix products, arithmetic and copies ran while one was open for 5% of the time, Pallas kernels for 24%

profile of v3, /device:TPU:0, one launch (start us, length us, event | category | flops | bytes accessed | tf_op | source)
XLA Modules:
  0.0 559.3 jit_solution(5379845354762684822)
XLA Ops:
  75.5 9.8 %shard_map.82.own = bf16[1024,512]{1,0:T(8,128)(2,1)} custom-call(s32[12]{0:T(128)} %concatenate.39.meta, bf16[3,2048,512]{2,1,0:T(8,128)(2,1)} %rest_0_.5, bf16[512,512]{1,0:T(8,128)(2,1)} %copy-done.47, bf16[512,512]{1,0:T(8,128)(2,1)} %copy-done.35, bf16[512,512]{1,0:T(8,128)(2,1)} %copy-done.27, bf16[512,512]{1,0:T(8,128)(2,1)} %copy-done.48, ...), custom_call_target="tpu_custom_call" | custom-call | tf_op jit(solution)/shard_map/pallas_call | solution.py:410
  86.1 26.8 %collective-permute-start.9 = (bf16[512,512]{1,0:T(8,128)(2,1)}, bf16[512,512]{1,0:T(8,128)(2,1)S(1)}, u32[]{:S(2)}, u32[]{:S(2)}) collective-permute-start(bf16[512,512]{1,0:T(8,128)(2,1)} %get-tuple-element.75), channel_id=1, source_target_pairs={{0,16},{4,20},{9,25},{13,29},{18,2},{22,6},{27,11},{31,15},{16,24}... | collective-permute-start | bytes 1572872 | tf_op jit(solution)/shard_map/ppermute | solution.py:438
  117.2 7.7 %collective-permute-done.9.refs_5_.refs_3_.refs_4_ = bf16[512,512]{1,0:T(8,128)(2,1)S(1)} collective-permute-done((bf16[512,512]{1,0:T(8,128)(2,1)}, bf16[512,512]{1,0:T(8,128)(2,1)S(1)}, u32[]{:S(2)}, u32[]{:S(2)}) %collective-permute-start.9) | collective-permute-done | bytes 524320 | tf_op jit(solution)/shard_map/ppermute | solution.py:438
  132.7 9.8 %shard_map.89.own = bf16[1024,512]{1,0:T(8,128)(2,1)} custom-call(s32[12]{0:T(128)} %concatenate.39.meta, bf16[3,2048,512]{2,1,0:T(8,128)(2,1)} %rest_0_.5, bf16[512,512]{1,0:T(8,128)(2,1)} %copy-done.35, bf16[512,512]{1,0:T(8,128)(2,1)} %copy-done.27, bf16[512,512]{1,0:T(8,128)(2,1)} %collective-permute-done.15.refs_1_.refs_2_, ...), custom_call_target="tpu_custom_call" | custom-call | tf_op jit(solution)/shard_map/pallas_call | solution.py:410
  143.1 9.2 %shard_map.83.before = f32[2048,512]{1,0:T(8,128)S(1)} custom-call(s32[12]{0:T(128)S(1)} %copy-done.20, f32[2048,4096]{1,0:T(8,128)} %s_oth.11, f32[2048,4096]{1,0:T(8,128)} %s_oth.11, bf16[1024,512]{1,0:T(8,128)(2,1)S(1)} %copy-done.16, bf16[1024,512]{1,0:T(8,128)(2,1)} %collective-permute-done.12.oth), custom_call_target="tpu_custom_call" | custom-call | flops 8589934592 | bytes 16777216 | tf_op jit(solution)/shard_map/pallas_call | solution.py:139
  153.9 10.4 %shard_map.85 = (f32[4,2048,128]{2,1,0:T(8,128)S(1)}, s16[1040,128]{1,0:T(8,128)(2,1)}, s16[1040,128]{1,0:T(8,128)(2,1)S(1)}) custom-call(s32[12]{0:T(128)S(1)} %copy-done.20, f32[2048,4096]{1,0:T(8,128)} %s_oth.11, f32[2048,4096]{1,0:T(8,128)} %s_oth.11, bf16[1024,512]{1,0:T(8,128)(2,1)S(1)} %copy-done.18, bf16[1024,512]{1,0:T(8,128)(2,1)} %collective-permute-done.17.oth, ...), custom_call_target="tpu_custom_call" | custom-call | flops 8589934592 | bytes 16777216 | tf_op jit(solution)/shard_map/pallas_call | solution.py:168
  166.3 68.2 %collective-permute-start.38 = (s16[1040,128]{1,0:T(8,128)(2,1)}, s16[1040,128]{1,0:T(8,128)(2,1)S(1)}, u32[]{:S(2)}, u32[]{:S(2)}) collective-permute-start(s16[1040,128]{1,0:T(8,128)(2,1)} %get-tuple-element.101), channel_id=1, source_target_pairs={{0,1},{1,2},{2,3},{3,0},{4,5},{5,6},{6,7},{7,4},{8,9},{9,10},{10,1... | collective-permute-start | bytes 798728 | tf_op jit(solution)/shard_map/ppermute | solution.py:43
  239.5 9.8 %shard_map.87.own = bf16[1024,512]{1,0:T(8,128)(2,1)} custom-call(s32[12]{0:T(128)} %concatenate.39.meta, bf16[3,2048,512]{2,1,0:T(8,128)(2,1)} %rest_0_.5, bf16[512,512]{1,0:T(8,128)(2,1)} %copy-done.27, bf16[512,512]{1,0:T(8,128)(2,1)} %collective-permute-done.15.refs_1_.refs_2_, bf16[512,512]{1,0:T(8,128)(2,1)} %collective-permute-done.21.refs_2_, ...), custom_call_target="tpu_custom_call" | custom-call | tf_op jit(solution)/shard_map/pallas_call | solution.py:410
  254.0 57.6 %collective-permute-start.40 = (s16[2064,128]{1,0:T(8,128)(2,1)}, s16[2064,128]{1,0:T(8,128)(2,1)S(1)}, u32[]{:S(2)}, u32[]{:S(2)}) collective-permute-start(s16[2064,128]{1,0:T(8,128)(2,1)} %get-tuple-element.103), channel_id=1, source_target_pairs={{0,1},{1,2},{2,3},{3,0},{4,5},{5,6},{6,7},{7,4},{8,9},{9,10},{10,1... | collective-permute-start | bytes 1585160 | tf_op jit(solution)/shard_map/ppermute | solution.py:43
  313.8 8.9 %shard_map.90.before = f32[2048,512]{1,0:T(8,128)S(1)} custom-call(s32[12]{0:T(128)S(1)} %copy-done.21, f32[2048,4096]{1,0:T(8,128)} %s_oth.11, f32[2048,4096]{1,0:T(8,128)} %s_oth.11, bf16[1024,512]{1,0:T(8,128)(2,1)S(1)} %copy-done.13, bf16[1024,512]{1,0:T(8,128)(2,1)S(1)} %collective-permute-done.24.oth), custom_call_target="tpu_custom_call" | custom-call | flops 8589934592 | bytes 16777216 | tf_op jit(solution)/shard_map/pallas_call | solution.py:139
  325.5 10.2 %collective-permute-start.41 = (s16[2064,128]{1,0:T(8,128)(2,1)}, s16[2064,128]{1,0:T(8,128)(2,1)}, u32[]{:S(2)}, u32[]{:S(2)}) collective-permute-start(s16[2064,128]{1,0:T(8,128)(2,1)} %get-tuple-element.104), channel_id=1, source_target_pairs={{0,3},{1,0},{2,1},{3,2},{4,7},{5,4},{6,5},{7,6},{8,11},{9,8},{10,9... | collective-permute-start | bytes 1585160 | tf_op jit(solution)/shard_map/ppermute | solution.py:43
  341.9 10.1 %shard_map.91 = (f32[4,2048,128]{2,1,0:T(8,128)S(1)}, s16[1040,128]{1,0:T(8,128)(2,1)S(1)}, s16[1040,128]{1,0:T(8,128)(2,1)S(1)}) custom-call(s32[12]{0:T(128)S(1)} %copy-done.22, f32[2048,4096]{1,0:T(8,128)} %s_oth.11, f32[2048,4096]{1,0:T(8,128)} %s_oth.11, bf16[1024,512]{1,0:T(8,128)(2,1)S(1)} %copy-done.14, ...), custom_call_target="tpu_custom_call" | custom-call | flops 8589934592 | bytes 16777216 | tf_op jit(solution)/shard_map/pallas_call | solution.py:168
  352.0 29.1 %collective-permute-start.34 = (s16[1040,128]{1,0:T(8,128)(2,1)S(1)}, s16[1040,128]{1,0:T(8,128)(2,1)S(1)}, u32[]{:S(2)}, u32[]{:S(2)}) collective-permute-start(s16[1040,128]{1,0:T(8,128)(2,1)S(1)} %get-tuple-element.97), channel_id=1, source_target_pairs={{0,1},{1,2},{2,3},{3,0},{4,5},{5,6},{6,7},{7,4},{8,9},{9,10},{10,1... | collective-permute-start | bytes 798728 | tf_op jit(solution)/shard_map/ppermute | solution.py:43
  384.3 9.2 %shard_map.92.before = f32[2048,512]{1,0:T(8,128)S(1)} custom-call(s32[12]{0:T(128)S(1)} %copy-done.22, f32[2048,4096]{1,0:T(8,128)} %s_oth.11, f32[2048,4096]{1,0:T(8,128)} %s_oth.11, bf16[1024,512]{1,0:T(8,128)(2,1)S(1)} %copy-done.15, bf16[1024,512]{1,0:T(8,128)(2,1)} %collective-permute-done.29.oth), custom_call_target="tpu_custom_call" | custom-call | flops 8589934592 | bytes 16777216 | tf_op jit(solution)/shard_map/pallas_call | solution.py:139
  401.1 10.5 %shard_map.93 = (f32[4,2048,128]{2,1,0:T(8,128)S(1)}, s16[1040,128]{1,0:T(8,128)(2,1)}, s16[1040,128]{1,0:T(8,128)(2,1)}) custom-call(s32[12]{0:T(128)S(1)} %copy-done.22, f32[2048,4096]{1,0:T(8,128)} %s_oth.11, f32[2048,4096]{1,0:T(8,128)} %s_oth.11, bf16[1024,512]{1,0:T(8,128)(2,1)S(1)} %copy-done.17, bf16[1024,512]{1,0:T(8,128)(2,1)S(1)} %collective-permute-done.20.oth, ...), custom_call_target="tpu_custom_call" | custom-call | flops 8589934592 | bytes 16777216 | tf_op jit(solution)/shard_map/pallas_call | solution.py:168
  422.4 5.7 %shard_map.97 = (f32[3,2048,128]{2,1,0:T(8,128)}, f32[128,1024]{1,0:T(8,128)S(1)}) custom-call(s32[12]{0:T(128)S(1)} %copy-done.22, f32[4,2048,128]{2,1,0:T(8,128)S(1)} %copy-done.5, s16[2064,128]{1,0:T(8,128)(2,1)S(1)} %collective-permute-done.40.got_right, s16[2064,128]{1,0:T(8,128)(2,1)} %collective-permute-done.41.got_left, ...), custom_call_target="tpu_custom_call" | custom-call | tf_op jit(solution)/shard_map/pallas_call | solution.py:269
  428.3 4.4 shard_map.98
  436.7 17.1 %collective-permute-start.43 = (f32[64,1024]{1,0:T(8,128)S(1)}, f32[64,1024]{1,0:T(8,128)S(1)}, u32[]{:S(2)}, u32[]{:S(2)}) collective-permute-start(f32[64,1024]{1,0:T(8,128)S(1)} %dynamic-slice_add_fusion.1), channel_id=1, source_target_pairs={{0,8},{4,12},{8,0},{12,4},{16,24},{20,28},{24,16},{28,20},{1,9},{5... | collective-permute-start | bytes 786440 | tf_op jit(solution)/shard_map/ppermute | solution.py:47
  453.9 7.0 %collective-permute-done.43 = f32[64,1024]{1,0:T(8,128)S(1)} collective-permute-done((f32[64,1024]{1,0:T(8,128)S(1)}, f32[64,1024]{1,0:T(8,128)S(1)}, u32[]{:S(2)}, u32[]{:S(2)}) %collective-permute-start.43) | collective-permute-done | bytes 262176 | tf_op jit(solution)/shard_map/ppermute | solution.py:47
  479.0 4.3 collective-permute-done.45
  483.4 7.1 %collective-permute-done.46 = f32[64,640]{1,0:T(8,128)S(1)} collective-permute-done((f32[64,640]{1,0:T(8,128)S(1)}, f32[64,640]{1,0:T(8,128)S(1)}, u32[]{:S(2)}, u32[]{:S(2)}) %collective-permute-start.46) | collective-permute-done | bytes 163872 | tf_op jit(solution)/shard_map/ppermute | solution.py:43
  509.7 10.7 %collective-permute-done.33.got_left = s16[2064,128]{1,0:T(8,128)(2,1)S(1)} collective-permute-done((s16[2064,128]{1,0:T(8,128)(2,1)S(1)}, s16[2064,128]{1,0:T(8,128)(2,1)S(1)}, u32[]{:S(2)}, u32[]{:S(2)}) %collective-permute-start.33) | collective-permute-done | bytes 528416 | tf_op jit(solution)/shard_map/ppermute | solution.py:43
  531.9 9.4 %collective-permute-done.53 = f32[64,640]{1,0:T(8,128)S(1)} collective-permute-done((f32[64,640]{1,0:T(8,128)S(1)}, f32[64,640]{1,0:T(8,128)S(1)}, u32[]{:S(2)}, u32[]{:S(2)}) %collective-permute-start.53) | collective-permute-done | bytes 163872 | tf_op jit(solution)/shard_map/ppermute | solution.py:43
  545.1 4.5 collective-permute-done.57
  (302 shorter events, 200.1 us)
Async XLA Ops:
  1.6 23.2 %collective-permute-start.27 = (bf16[128,512]{1,0:T(8,128)(2,1)S(1)}, bf16[128,512]{1,0:T(8,128)(2,1)S(1)}, u32[]{:S(2)}, u32[]{:S(2)}) collective-permute-start(bf16[128,512]{1,0:T(8,128)(2,1)S(1)} %constant_dynamic-slice_fusion.17), channel_id=1, source_target_pairs={{0,1},{1,2},{2,3},{3,0},{4,5},{5,6},{6,7},{7,4},{8,9},{9,10},{10,1... | collective-permute-start | bytes 393224 | tf_op jit(solution)/shard_map/ppermute | solution.py:43
  20.8 19.5 %collective-permute-start = (bf16[512,512]{1,0:T(8,128)(2,1)}, bf16[512,512]{1,0:T(8,128)(2,1)S(1)}, u32[]{:S(2)}, u32[]{:S(2)}) collective-permute-start(bf16[512,512]{1,0:T(8,128)(2,1)} %get-tuple-element.62), channel_id=1, source_target_pairs={{0,8},{4,12},{9,1},{13,5},{18,26},{22,30},{27,19},{31,23}} | collective-permute-start | bytes 1572872 | tf_op jit(solution)/shard_map/ppermute | solution.py:438
  68.3 47.5 %collective-permute-start.8 = (bf16[512,512]{1,0:T(8,128)(2,1)}, bf16[512,512]{1,0:T(8,128)(2,1)S(1)}, u32[]{:S(2)}, u32[]{:S(2)}) collective-permute-start(bf16[512,512]{1,0:T(8,128)(2,1)} %get-tuple-element.74), channel_id=1, source_target_pairs={{0,8},{4,12},{9,1},{13,5},{18,26},{22,30},{27,19},{31,23},{8,24},{... | collective-permute-start | bytes 1572872 | tf_op jit(solution)/shard_map/ppermute | solution.py:438
  85.3 57.8 %collective-permute-start.12 = (bf16[1024,512]{1,0:T(8,128)(2,1)}, bf16[1024,512]{1,0:T(8,128)(2,1)}, u32[]{:S(2)}, u32[]{:S(2)}) collective-permute-start(bf16[1024,512]{1,0:T(8,128)(2,1)} %shard_map.82.own), channel_id=1, source_target_pairs={{0,4},{4,0},{8,12},{12,8},{16,20},{20,16},{24,28},{28,24},{1,5},{5... | collective-permute-start | bytes 3145736 | tf_op jit(solution)/shard_map/ppermute | solution.py:47
  86.1 38.9 %collective-permute-start.9 = (bf16[512,512]{1,0:T(8,128)(2,1)}, bf16[512,512]{1,0:T(8,128)(2,1)S(1)}, u32[]{:S(2)}, u32[]{:S(2)}) collective-permute-start(bf16[512,512]{1,0:T(8,128)(2,1)} %get-tuple-element.75), channel_id=1, source_target_pairs={{0,16},{4,20},{9,25},{13,29},{18,2},{22,6},{27,11},{31,15},{16,24}... | collective-permute-start | bytes 1572872 | tf_op jit(solution)/shard_map/ppermute | solution.py:438
  127.5 25.7 %collective-permute-start.17 = (bf16[1024,512]{1,0:T(8,128)(2,1)}, bf16[1024,512]{1,0:T(8,128)(2,1)}, u32[]{:S(2)}, u32[]{:S(2)}) collective-permute-start(bf16[1024,512]{1,0:T(8,128)(2,1)} %shard_map.84.own), channel_id=1, source_target_pairs={{0,4},{4,0},{8,12},{12,8},{16,20},{20,16},{24,28},{28,24},{1,5},{5... | collective-permute-start | bytes 3145736 | tf_op jit(solution)/shard_map/ppermute | solution.py:47
  129.7 108.4 %collective-permute-start.21 = (bf16[512,512]{1,0:T(8,128)(2,1)}, bf16[512,512]{1,0:T(8,128)(2,1)}, u32[]{:S(2)}, u32[]{:S(2)}) collective-permute-start(bf16[512,512]{1,0:T(8,128)(2,1)} %collective-permute-done.15.refs_1_.refs_2_), channel_id=1, source_target_pairs={{24,16},{28,20},{17,25},{21,29},{10,2},{14,6},{3,11},{7,15}} | collective-permute-start | bytes 1572872 | tf_op jit(solution)/shard_map/ppermute | solution.py:438
  131.3 108.2 %collective-permute-start.22 = (bf16[512,512]{1,0:T(8,128)(2,1)}, bf16[512,512]{1,0:T(8,128)(2,1)}, u32[]{:S(2)}, u32[]{:S(2)}) collective-permute-start(bf16[512,512]{1,0:T(8,128)(2,1)} %collective-permute-done.16.refs_4_.refs_5_), channel_id=1, source_target_pairs={{24,8},{28,12},{17,1},{21,5},{10,26},{14,30},{3,19},{7,23}} | collective-permute-start | bytes 1572872 | tf_op jit(solution)/shard_map/ppermute | solution.py:438
  142.5 169.8 %collective-permute-start.24 = (bf16[1024,512]{1,0:T(8,128)(2,1)}, bf16[1024,512]{1,0:T(8,128)(2,1)S(1)}, u32[]{:S(2)}, u32[]{:S(2)}) collective-permute-start(bf16[1024,512]{1,0:T(8,128)(2,1)} %shard_map.89.own), channel_id=1, source_target_pairs={{0,4},{4,0},{8,12},{12,8},{16,20},{20,16},{24,28},{28,24},{1,5},{5... | collective-permute-start | bytes 3145736 | tf_op jit(solution)/shard_map/ppermute | solution.py:47
  153.2 81.4 %collective-permute-start.14 = (bf16[512,512]{1,0:T(8,128)(2,1)S(1)}, bf16[512,512]{1,0:T(8,128)(2,1)S(1)}, u32[]{:S(2)}, u32[]{:S(2)}) collective-permute-start(bf16[512,512]{1,0:T(8,128)(2,1)S(1)} %copy-done.26), channel_id=1, source_target_pairs={{16,24},{20,28},{25,17},{29,21},{2,10},{6,14},{11,3},{15,7},{24,8}... | collective-permute-start | bytes 1572872 | tf_op jit(solution)/shard_map/ppermute | solution.py:438
  166.3 83.5 %collective-permute-start.38 = (s16[1040,128]{1,0:T(8,128)(2,1)}, s16[1040,128]{1,0:T(8,128)(2,1)S(1)}, u32[]{:S(2)}, u32[]{:S(2)}) collective-permute-start(s16[1040,128]{1,0:T(8,128)(2,1)} %get-tuple-element.101), channel_id=1, source_target_pairs={{0,1},{1,2},{2,3},{3,0},{4,5},{5,6},{6,7},{7,4},{8,9},{9,10},{10,1... | collective-permute-start | bytes 798728 | tf_op jit(solution)/shard_map/ppermute | solution.py:43
  238.1 99.4 %collective-permute-start.23 = (bf16[1024,512]{1,0:T(8,128)(2,1)}, bf16[1024,512]{1,0:T(8,128)(2,1)}, u32[]{:S(2)}, u32[]{:S(2)}) collective-permute-start(bf16[1024,512]{1,0:T(8,128)(2,1)} %shard_map.88.own), channel_id=1, source_target_pairs={{0,4},{4,0},{8,12},{12,8},{16,20},{20,16},{24,28},{28,24},{1,5},{5... | collective-permute-start | bytes 3145736 | tf_op jit(solution)/shard_map/ppermute | solution.py:47
  249.3 131.7 %collective-permute-start.29 = (bf16[1024,512]{1,0:T(8,128)(2,1)}, bf16[1024,512]{1,0:T(8,128)(2,1)}, u32[]{:S(2)}, u32[]{:S(2)}) collective-permute-start(bf16[1024,512]{1,0:T(8,128)(2,1)} %shard_map.87.own), channel_id=1, source_target_pairs={{0,4},{4,0},{8,12},{12,8},{16,20},{20,16},{24,28},{28,24},{1,5},{5... | collective-permute-start | bytes 3145736 | tf_op jit(solution)/shard_map/ppermute | solution.py:47
  254.0 159.9 %collective-permute-start.40 = (s16[2064,128]{1,0:T(8,128)(2,1)}, s16[2064,128]{1,0:T(8,128)(2,1)S(1)}, u32[]{:S(2)}, u32[]{:S(2)}) collective-permute-start(s16[2064,128]{1,0:T(8,128)(2,1)} %get-tuple-element.103), channel_id=1, source_target_pairs={{0,1},{1,2},{2,3},{3,0},{4,5},{5,6},{6,7},{7,4},{8,9},{9,10},{10,1... | collective-permute-start | bytes 1585160 | tf_op jit(solution)/shard_map/ppermute | solution.py:43
  312.4 23.4 %collective-permute-start.19 = (bf16[512,512]{1,0:T(8,128)(2,1)S(1)}, bf16[512,512]{1,0:T(8,128)(2,1)}, u32[]{:S(2)}, u32[]{:S(2)}) collective-permute-start(bf16[512,512]{1,0:T(8,128)(2,1)S(1)} %copy-done.40), channel_id=1, source_target_pairs={{24,8},{28,12},{17,1},{21,5},{10,26},{14,30},{3,19},{7,23}} | collective-permute-start | bytes 1572872 | tf_op jit(solution)/shard_map/ppermute | solution.py:438
  325.5 91.9 %collective-permute-start.41 = (s16[2064,128]{1,0:T(8,128)(2,1)}, s16[2064,128]{1,0:T(8,128)(2,1)}, u32[]{:S(2)}, u32[]{:S(2)}) collective-permute-start(s16[2064,128]{1,0:T(8,128)(2,1)} %get-tuple-element.104), channel_id=1, source_target_pairs={{0,3},{1,0},{2,1},{3,2},{4,7},{5,4},{6,5},{7,6},{8,11},{9,8},{10,9... | collective-permute-start | bytes 1585160 | tf_op jit(solution)/shard_map/ppermute | solution.py:43
  337.4 63.6 %collective-permute-start.20 = (bf16[1024,512]{1,0:T(8,128)(2,1)}, bf16[1024,512]{1,0:T(8,128)(2,1)S(1)}, u32[]{:S(2)}, u32[]{:S(2)}) collective-permute-start(bf16[1024,512]{1,0:T(8,128)(2,1)} %shard_map.86.own), channel_id=1, source_target_pairs={{0,4},{4,0},{8,12},{12,8},{16,20},{20,16},{24,28},{28,24},{1,5},{5... | collective-permute-start | bytes 3145736 | tf_op jit(solution)/shard_map/ppermute | solution.py:47
  352.0 41.6 %collective-permute-start.34 = (s16[1040,128]{1,0:T(8,128)(2,1)S(1)}, s16[1040,128]{1,0:T(8,128)(2,1)S(1)}, u32[]{:S(2)}, u32[]{:S(2)}) collective-permute-start(s16[1040,128]{1,0:T(8,128)(2,1)S(1)} %get-tuple-element.97), channel_id=1, source_target_pairs={{0,1},{1,2},{2,3},{3,0},{4,5},{5,6},{6,7},{7,4},{8,9},{9,10},{10,1... | collective-permute-start | bytes 798728 | tf_op jit(solution)/shard_map/ppermute | solution.py:43
  397.2 31.0 %collective-permute-start.36 = (s16[2064,128]{1,0:T(8,128)(2,1)}, s16[2064,128]{1,0:T(8,128)(2,1)S(1)}, u32[]{:S(2)}, u32[]{:S(2)}) collective-permute-start(s16[2064,128]{1,0:T(8,128)(2,1)} %get-tuple-element.99), channel_id=1, source_target_pairs={{0,1},{1,2},{2,3},{3,0},{4,5},{5,6},{6,7},{7,4},{8,9},{9,10},{10,1... | collective-permute-start | bytes 1585160 | tf_op jit(solution)/shard_map/ppermute | solution.py:43
  399.3 28.9 %collective-permute-start.37 = (s16[2064,128]{1,0:T(8,128)(2,1)}, s16[2064,128]{1,0:T(8,128)(2,1)S(1)}, u32[]{:S(2)}, u32[]{:S(2)}) collective-permute-start(s16[2064,128]{1,0:T(8,128)(2,1)} %get-tuple-element.100), channel_id=1, source_target_pairs={{0,3},{1,0},{2,1},{3,2},{4,7},{5,4},{6,5},{7,6},{8,11},{9,8},{10,9... | collective-permute-start | bytes 1585160 | tf_op jit(solution)/shard_map/ppermute | solution.py:43
  413.9 21.6 %collective-permute-start.31 = (s16[1040,128]{1,0:T(8,128)(2,1)}, s16[1040,128]{1,0:T(8,128)(2,1)}, u32[]{:S(2)}, u32[]{:S(2)}) collective-permute-start(s16[1040,128]{1,0:T(8,128)(2,1)} %get-tuple-element.94), channel_id=1, source_target_pairs={{0,3},{1,0},{2,1},{3,2},{4,7},{5,4},{6,5},{7,6},{8,11},{9,8},{10,9... | collective-permute-start | bytes 798728 | tf_op jit(solution)/shard_map/ppermute | solution.py:43
  436.7 24.2 %collective-permute-start.43 = (f32[64,1024]{1,0:T(8,128)S(1)}, f32[64,1024]{1,0:T(8,128)S(1)}, u32[]{:S(2)}, u32[]{:S(2)}) collective-permute-start(f32[64,1024]{1,0:T(8,128)S(1)} %dynamic-slice_add_fusion.1), channel_id=1, source_target_pairs={{0,8},{4,12},{8,0},{12,4},{16,24},{20,28},{24,16},{28,20},{1,9},{5... | collective-permute-start | bytes 786440 | tf_op jit(solution)/shard_map/ppermute | solution.py:47
  493.8 26.6 %collective-permute-start.33 = (s16[2064,128]{1,0:T(8,128)(2,1)S(1)}, s16[2064,128]{1,0:T(8,128)(2,1)S(1)}, u32[]{:S(2)}, u32[]{:S(2)}) collective-permute-start(s16[2064,128]{1,0:T(8,128)(2,1)S(1)} %get-tuple-element.96), channel_id=1, source_target_pairs={{0,3},{1,0},{2,1},{3,2},{4,7},{5,4},{6,5},{7,6},{8,11},{9,8},{10,9... | collective-permute-start | bytes 1585160 | tf_op jit(solution)/shard_map/ppermute | solution.py:43
  505.2 26.7 %collective-permute-start.52 = (f32[64,640]{1,0:T(8,128)S(1)}, f32[64,640]{1,0:T(8,128)S(1)}, u32[]{:S(2)}, u32[]{:S(2)}) collective-permute-start(f32[64,640]{1,0:T(8,128)S(1)} %get-tuple-element.116), channel_id=1, source_target_pairs={{0,3},{1,0},{2,1},{3,2},{4,7},{5,4},{6,5},{7,6},{8,11},{9,8},{10,9... | collective-permute-start | bytes 491528 | tf_op jit(solution)/shard_map/ppermute | solution.py:43
  (88 other events, 1260.1 us)

commit v4 on v3

--- a/solution.py
+++ b/solution.py
@@ -12,6 +12,7 @@
 LANES = 2
 STREAMS = 2
 FEED_COST = 10_000_000_000
+VMEM = 24 << 20
 HEAD = 4
 
 precise = lax.Precision.HIGHEST
@@ -145,7 +146,7 @@
             out_specs=pl.BlockSpec((TILE, width), lambda i, m: (i, 0)),
         ),
         out_shape=jax.ShapeDtypeStruct((rows, width), f32),
-        compiler_params=pltpu.CompilerParams(vmem_limit_bytes=24 << 20),
+        compiler_params=pltpu.CompilerParams(vmem_limit_bytes=VMEM),
         cost_estimate=pl.CostEstimate(
             flops=2 * rows * depth * width, bytes_accessed=2 * rows * depth, transcendentals=0
         ),
@@ -175,7 +176,7 @@
             scratch_shapes=[pltpu.VMEM((PAD, share), jnp.int32)],
         ),
         out_shape=[jax.ShapeDtypeStruct((cols, rows, share), f32), message, message],
-        compiler_params=pltpu.CompilerParams(vmem_limit_bytes=28 << 20),
+        compiler_params=pltpu.CompilerParams(vmem_limit_bytes=VMEM),
         cost_estimate=pl.CostEstimate(
             flops=2 * rows * depth * width, bytes_accessed=2 * rows * depth, transcendentals=0
         ),
@@ -218,7 +219,7 @@
             out_specs=[pl.BlockSpec((rows + PAD, share), everything)] * 2,
         ),
         out_shape=[message, message],
-        compiler_params=pltpu.CompilerParams(vmem_limit_bytes=20 << 20),
+        compiler_params=pltpu.CompilerParams(vmem_limit_bytes=VMEM),
     )(meta, part, part, got_right, got_left)
 
 
@@ -282,7 +283,7 @@
             jax.ShapeDtypeStruct((share, count * width), f32),
         ],
         input_output_aliases=aliases,
-        compiler_params=pltpu.CompilerParams(vmem_limit_bytes=20 << 20),
+        compiler_params=pltpu.CompilerParams(vmem_limit_bytes=VMEM),
     )(meta, *operands)
 
 
@@ -292,16 +293,19 @@
     return lax.dynamic_slice_in_dim(ring, size - 1 - col_number, size, 0)
 
 
-def row_sum_half(value, lane, row_size):
+def row_sum_half(value, lane, row_size, gates=()):
     half = value.shape[0] // 2
     keep = lax.dynamic_slice_in_dim(value, lane * half, half, 0)
     give = lax.dynamic_slice_in_dim(value, (1 - lane) * half, half, 0)
-    keep = keep + swap(give, 1, row_size)
+    stages = [keep + swap(give, 1, row_size)]
     bit = 2
     while bit < row_size:
-        keep = keep + swap(keep, bit, row_size)
+        value = stages[-1]
+        if len(stages) <= len(gates):
+            value = after(value, *gates[len(stages) - 1])
+        stages.append(value + swap(value, bit, row_size))
         bit *= 2
-    return keep
+    return stages
 
 
 def both_halves(half, lane, row_size, axis):
@@ -362,17 +366,16 @@
             out_specs=[block] * ways,
         ),
         out_shape=[jax.ShapeDtypeStruct((piece, width), bf16)] * ways,
+        compiler_params=pltpu.CompilerParams(vmem_limit_bytes=VMEM),
         cost_estimate=pl.CostEstimate(flops=FEED_COST, bytes_accessed=0, transcendentals=0),
     )(meta, *[panels] * ways, *arrived)
 
 
 def pick_kernel(k, spots, meta, panels, *refs):
     ways = len(spots)
-    zeros, sems = refs[-2:]
-    out = refs[-3]
-    turns = len(refs[:-3]) // ways
+    out, sems = refs[-2:]
+    turns = len(refs[:-2]) // ways
     piece = out.shape[0] // ways
-    zeros[...] = jnp.zeros_like(zeros)
 
     def each(act):
         for way, row in enumerate(spots):
@@ -393,11 +396,15 @@
                     source = panels.at[k, pl.ds(row + at, block)]
                     act(pltpu.make_async_copy(source, target, sems.at[way, n]))
 
-                @pl.when((turn == 0) & (flag == 0))
-                def _(way=way, n=n, target=target):
-                    act(pltpu.make_async_copy(zeros, target, sems.at[way, n]))
 
     each(lambda copy: copy.start())
+    for way, row in enumerate(spots):
+        for at, block, flag in own_blocks(meta, row, piece):
+
+            @pl.when((meta[2 + way] == 0) & (flag == 0))
+            def _(at=way * piece + at, block=block):
+                out[at : at + block, :] = jnp.zeros((block, out.shape[1]), out.dtype)
+
     each(lambda copy: copy.wait())
 
 
@@ -412,14 +419,12 @@
         grid_spec=pltpu.PrefetchScalarGridSpec(
             num_scalar_prefetch=1,
             grid=(1,),
-            in_specs=[pl.BlockSpec(memory_space=pl.ANY)] * len(operands),
-            out_specs=pl.BlockSpec(memory_space=pl.ANY),
-            scratch_shapes=[
-                pltpu.VMEM((block, width), bf16),
-                pltpu.SemaphoreType.DMA((ways, piece // block)),
-            ],
+            in_specs=[pl.BlockSpec(memory_space=pltpu.HBM)] * len(operands),
+            out_specs=pl.BlockSpec((ways * piece, width), lambda i, m: (0, 0)),
+            scratch_shapes=[pltpu.SemaphoreType.DMA((ways, piece // block))],
         ),
         out_shape=jax.ShapeDtypeStruct((ways * piece, width), bf16),
+        compiler_params=pltpu.CompilerParams(vmem_limit_bytes=VMEM),
     )(meta, *operands)
 
 
@@ -462,44 +467,79 @@
         ]
     )
 
-    flat = links.reshape(-1, width)
-    half = flat.shape[0] // 2
-    my_links = lax.dynamic_slice_in_dim(flat, lane * half, half, 0)
-    got = around([my_links] + [shift(my_links, s, col_size) for s in range(1, col_size)], col_number)
-    link_full = both_halves(got, lane, row_size, 1)
-    link_full = link_full.reshape(col_size, supernodes - 1, -1, width)
-    link_full = link_full.transpose(1, 0, 2, 3).reshape(supernodes - 1, width, width)
-
     cross_parts, diag_parts = [], []
     carried = cross = stacked = full_turned = None
+    link_full = None
     events = []
     steps = supernodes + col_size - 2
-    parts = []
-    befores = []
+    parts, products, hops, sums, summed = [], [], [], [], []
     done = 0
+
+    picked = []
+
+    def finish(k, ties=(), gates=()):
+        nonlocal carried
+        right, left = hops[k][-1]
+        if ties:
+            right = after(right, *ties)
+        carried, total = sum_parts(meta, parts[k], right, left, panels, k, carried)
+        sums.append(total)
+        summed.append(row_sum_half(total, lane, row_size, gates))
+
+    def scatter(k):
+        right, left = hops[k][-1]
+        for hop in range(col_size // 2 - 1, 0, -1):
+            right = after(right, products[-1])
+            right, left = pass_on(meta, parts[k], right, left, hop)
+            hops[k].append((right, left))
+            right, left = shift(right, 1, col_size), shift(left, -1, col_size)
+            hops[k].append((right, left))
+
+    def pick_now(q):
+        k, stream = q // 2, q % 2
+        flat = [
+            events[2 * (k + t - 1) + stream][way] for way in range(2) for t in range(1, col_size)
+        ]
+        gate = [products[max(q - 2, min(q - 1, 1))]] if q > 0 else []
+        flat = lax.optimization_barrier((*flat, *gate))
+        own = pick(
+            meta, panels, k, stream, [flat[: col_size - 1], flat[col_size - 1 : 2 * (col_size - 1)]]
+        )
+        picked.append((own, swap(own, 1, row_size)))
 
     def arrive(n):
         nonlocal done
-        while done < 2 * supernodes and 2 * (done // 2 + col_size - 2) + done % 2 <= n:
+        while done < 2 * supernodes:
+            need = min(done + 1, 2 * supernodes - 1) if done > 1 else done
+            if 2 * (need // 2 + col_size - 2) + need % 2 > n:
+                break
+            while len(picked) <= need:
+                pick_now(len(picked))
             k, stream = done // 2, done % 2
-            received = [
-                [events[2 * (k + t - 1) + stream][way] for t in range(1, col_size)]
-                for way in range(2)
-            ]
-            own = pick(meta, panels, k, stream, received)
-            oth = swap(own, 1, row_size)
+            own, oth = picked[done]
+            if need > done:
+                own = after(own, *[pair[0] for pair in picked[done + 1 : need + 1]])
             link = None if k == 0 else link_full[k - 1]
+            ties = products[-1:] or [link_full]
+            if k == supernodes - 1 and k > 1:
+                ties = ties + ([sums[0]] if stream == 0 else summed[0][:2])
+            if ties:
+                own = after(own, *ties)
             if stream == 0:
-                if k > 0:
-                    own = after(own, parts[-1][0])
-                befores.append(panel_first(meta, inverse_block, own, oth))
+                products.append(panel_first(meta, inverse_block, own, oth))
             else:
-                parts.append(
-                    panel_second(
-                        meta, inverse_block, own, oth, befores[-1], link,
-                        parts[-1][0] if k > 0 else None, col_size,
-                    )
+                part, right, left = panel_second(
+                    meta, inverse_block, own, oth, products[-1], link,
+                    parts[-1] if k > 0 else None, col_size,
                 )
+                parts.append(part)
+                products.append(part)
+                hops.append([(shift(right, 1, col_size), shift(left, -1, col_size))])
+            for k in range(supernodes):
+                if done == min(2 * k + 2, 2 * supernodes - 1):
+                    scatter(k)
+            if done == 3 and supernodes > 2:
+                finish(0, products[-1:])
             done += 1
 
     for step in range(steps):
@@ -510,35 +550,31 @@
             else:
                 values = arrived
             tie = events[-STREAMS - 1] if len(events) > STREAMS else []
-            if len(events) == 2 * col_size - 1 and befores:
-                tie = tie + befores[:1]
-            elif len(events) == 2 * col_size + 1 and parts:
-                tie = tie + [parts[0][0]]
+            if len(events) == 2 * col_size - 1:
+                tie = tie + products[:1]
+            elif len(events) == 2 * col_size + 1:
+                tie = tie + products[1:2]
             values = lax.optimization_barrier((*values, *tie))[: len(orders)]
             events.append(send_on(values, orders, step, supernodes))
+            if len(events) == 2:
+                flat = after(links, *events[0]).reshape(-1, width)
+                half = flat.shape[0] // 2
+                my_links = lax.dynamic_slice_in_dim(flat, lane * half, half, 0)
+                got = around([my_links] + [shift(my_links, s, col_size) for s in range(1, col_size)], col_number)
+                link_full = both_halves(got, lane, row_size, 1)
+                link_full = link_full.reshape(col_size, supernodes - 1, -1, width)
+                link_full = link_full.transpose(1, 0, 2, 3).reshape(supernodes - 1, width, width)
             arrive(len(events) - 1)
-    hops = []
-    for part, right, left in parts:
-        stages = []
-        for hop in range(col_size // 2 - 1, -1, -1):
-            right, left = shift(right, 1, col_size), shift(left, -1, col_size)
-            stages.append((right, left))
-            if hop > 0:
-                right, left = pass_on(meta, part, right, left, hop)
-                stages.append((right, left))
-        hops.append(stages)
-    gates = [[befores[-1]]] + [hops[-1][0]] * (supernodes - 2) + [()]
     for k in range(supernodes):
         last = k + 1 == supernodes
+        if last:
+            finish(k)
+        elif k > 0:
+            finish(k, hops[-1][min(1, len(hops[-1]) - 1)], ((), hops[-1][-1]))
         link = None if k == 0 else link_full[k - 1]
-        part = parts[k][0]
-        right, left = hops[k][-1]
-        carried, sums = sum_parts(meta, part, right, left, panels, k, carried)
-        sums = after(sums, *gates[k])
-
-        summed = row_sum_half(sums, lane, row_size)
+        total = summed[k][-1]
         mine = lax.dynamic_slice_in_dim(diag_inverse[k], lane * (share // 2), share // 2, 1).T
-        turned = mine - summed[:, :width]
+        turned = mine - total[:, :width]
         if k > 0:
             link_wide = link.astype(f32)
             link_share = lax.dynamic_slice_in_dim(link_wide, col_number * share, share, 1)
@@ -552,11 +588,13 @@
             arrived = []
             for s in range(col_size):
                 at = (col_number + s) % col_size * share
-                block = lax.dynamic_slice_in_dim(summed[:, width:], at, share, 1)
+                block = lax.dynamic_slice_in_dim(total[:, width:], at, share, 1)
                 message = jnp.concatenate([turned, block], axis=1)
-                message = after(message, *hops[-1][min(1, len(hops[-1]) - 1)])
                 arrived.append(shift(message, s, col_size) if s else message)
-            ordered = both_halves(around(arrived, col_number), lane, row_size, 1)
+            if k + 2 < supernodes:
+                arrived = after(tuple(arrived), *hops[-1][min(1, len(hops[-1]) - 1)])
+            ordered = around(list(arrived), col_number)
+            ordered = both_halves(ordered, lane, row_size, 1)
             full_turned = ordered[:, :, :width].reshape(width, width)
             stacked = ordered[:, :, width:].reshape(width, share)
             diag_parts.append(

time: 563 us -> 375 us (0.67)
  starting transfers between devices: 287 us -> 129 us
  Pallas kernels: 132 us -> 80.1 us
  waiting for transfers between devices: 73.3 us -> 113 us
  local copies, waits for them, and re-layouts: 47.2 us -> 36.5 us
    ppermute x21, starting transfers between devices: 194 us -> 73.9 us  [shift(): lax.ppermute(value, 'col', [(z, (z + by) % size) for z in range(size)])]
    ppermute x21, waiting for transfers between devices: 40 us -> 68 us  [shift(): lax.ppermute(value, 'col', [(z, (z + by) % size) for z in range(size)])]
    pallas_call x6, Pallas kernels: 34.4 us -> 6.51 us  [pick(): pl.pallas_call(functools.partial(pick_kernel, k, [(stream * ways + way) *...]
    ppermute x20, starting transfers between devices: 63.1 us -> 36.5 us  [send_on(): got.append(lax.ppermute(value, BOTH, pairs))]
    pallas_call x6, Pallas kernels: 18.8 us -> 7.49 us  [feed(): pl.pallas_call(functools.partial(feed_kernel, [(stream * ways + way) * pi...]
    ppermute x19, starting transfers between devices: 29.4 us -> 18.6 us  [swap(): return lax.ppermute(value, 'row', [(r, r ^ bit) for r in range(size)])]
    unnamed x124 -> x129, local copies, waits for them, and re-layouts: 37.3 us -> 26.6 us
    ppermute x20, waiting for transfers between devices: 18.8 us -> 28.7 us  [send_on(): got.append(lax.ppermute(value, BOTH, pairs))]
  transfers between devices with their start and end apart: 60 -> 60, of which waited for: 24 -> 26; matrix products, arithmetic and copies ran while one was open for 5% -> 4% of each run, Pallas kernels for 24% -> 20%
where the time goes in v4:
time: 375 us; the launch traced here: 372 us
  starting transfers between devices  129 us (34%)
  waiting for transfers between devices  113 us (30%)
  Pallas kernels  80.1 us (21%)
  local copies, waits for them, and re-layouts  36.5 us (10%)
  other arithmetic  10.1 us (3%)
    ppermute x21, starting transfers between devices, shift(): lax.ppermute(value, 'col', [(z, (z + by) % size) for z in range(size)])  73.9 us
    ppermute x21, waiting for transfers between devices, shift(): lax.ppermute(value, 'col', [(z, (z + by) % size) for z in range(size)])  68 us
    ppermute x20, starting transfers between devices, send_on(): got.append(lax.ppermute(value, BOTH, pairs))  36.5 us
    ppermute x20, waiting for transfers between devices, send_on(): got.append(lax.ppermute(value, BOTH, pairs))  28.7 us
    unnamed x129, local copies, waits for them, and re-layouts  26.6 us
    pallas_call x3, Pallas kernels, panel_first(): pl.pallas_call(first_kernel, grid_spec=pltpu.PrefetchScalarGridSpec(num_s...  25.4 us
    pallas_call x3, Pallas kernels, panel_second(): pl.pallas_call(functools.partial(second_kernel, cols, link is not None),...  24.7 us
    ppermute x19, starting transfers between devices, swap(): return lax.ppermute(value, 'row', [(r, r ^ bit) for r in range(size)])  18.6 us
  transfers between devices with their start and end apart: 60, of which 26 were waited for; matrix products, arithmetic and copies ran while one was open for 4% of the time, Pallas kernels for 20%

profile of v4, /device:TPU:0, one launch (start us, length us, event | category | flops | bytes accessed | tf_op | source)
XLA Modules:
  0.0 372.2 jit_solution(12882176966125654105)
XLA Ops:
  5.1 4.9 %collective-permute-start.2 = (bf16[512,512]{1,0:T(8,128)(2,1)S(1)}, bf16[512,512]{1,0:T(8,128)(2,1)S(1)}, u32[]{:S(2)}, u32[]{:S(2)}) collective-permute-start(bf16[512,512]{1,0:T(8,128)(2,1)S(1)} %get-tuple-element.109), channel_id=1, source_target_pairs={{0,8},{4,12},{9,1},{13,5},{18,26},{22,30},{27,19},{31,23}} | collective-permute-start | bytes 1572872 | tf_op jit(solution)/shard_map/ppermute | solution.py:443
  11.3 9.8 %collective-permute-done.2.refs_2_.refs_0_ = bf16[512,512]{1,0:T(8,128)(2,1)S(1)} collective-permute-done((bf16[512,512]{1,0:T(8,128)(2,1)S(1)}, bf16[512,512]{1,0:T(8,128)(2,1)S(1)}, u32[]{:S(2)}, u32[]{:S(2)}) %collective-permute-start.2) | collective-permute-done | bytes 524320 | tf_op jit(solution)/shard_map/ppermute | solution.py:443
  33.9 5.7 %collective-permute-done.6.refs_2_.refs_1_.refs_0_ = bf16[512,512]{1,0:T(8,128)(2,1)S(1)} collective-permute-done((bf16[512,512]{1,0:T(8,128)(2,1)}, bf16[512,512]{1,0:T(8,128)(2,1)S(1)}, u32[]{:S(2)}, u32[]{:S(2)}) %collective-permute-start.6) | collective-permute-done | bytes 524320 | tf_op jit(solution)/shard_map/ppermute | solution.py:443
  84.1 7.8 %shard_map.83.before = f32[2048,512]{1,0:T(8,128)S(1)} custom-call(s32[12]{0:T(128)S(1)} %concatenate.39.meta, f32[2048,4096]{1,0:T(8,128)} %s_oth.11, f32[2048,4096]{1,0:T(8,128)} %s_oth.11, bf16[1024,512]{1,0:T(8,128)(2,1)S(1)} %shard_map.82.own, bf16[1024,512]{1,0:T(8,128)(2,1)S(1)} %collective-permute-done.12.oth), custom_call_target="tpu_custom_call" | custom-call | flops 8589934592 | bytes 16777216 | tf_op jit(solution)/shard_map/pallas_call | solution.py:140
  97.6 8.2 %shard_map.85 = (f32[4,2048,128]{2,1,0:T(8,128)S(1)}, s16[1040,128]{1,0:T(8,128)(2,1)S(1)}, s16[1040,128]{1,0:T(8,128)(2,1)S(1)}) custom-call(s32[12]{0:T(128)S(1)} %concatenate.39.meta, f32[2048,4096]{1,0:T(8,128)} %s_oth.11, f32[2048,4096]{1,0:T(8,128)} %s_oth.11, bf16[1024,512]{1,0:T(8,128)(2,1)S(1)} %shard_map.84.own, ...), custom_call_target="tpu_custom_call" | custom-call | flops 8589934592 | bytes 16777216 | tf_op jit(solution)/shard_map/pallas_call | solution.py:169
  121.1 31.0 %collective-permute-start.28 = (s16[1040,128]{1,0:T(8,128)(2,1)S(1)}, s16[1040,128]{1,0:T(8,128)(2,1)S(1)}, u32[]{:S(2)}, u32[]{:S(2)}) collective-permute-start(s16[1040,128]{1,0:T(8,128)(2,1)S(1)} %copy-done.35), channel_id=1, source_target_pairs={{0,1},{1,2},{2,3},{3,0},{4,5},{5,6},{6,7},{7,4},{8,9},{9,10},{10,1... | collective-permute-start | bytes 798728 | tf_op jit(solution)/shard_map/ppermute | solution.py:44
  153.3 8.8 %shard_map.88.before = f32[2048,512]{1,0:T(8,128)S(1)} custom-call(s32[12]{0:T(128)S(1)} %concatenate.39.meta, f32[2048,4096]{1,0:T(8,128)} %s_oth.11, f32[2048,4096]{1,0:T(8,128)} %s_oth.11, bf16[1024,512]{1,0:T(8,128)(2,1)} %shard_map.87.own, bf16[1024,512]{1,0:T(8,128)(2,1)} %collective-permute-done.22.oth), custom_call_target="tpu_custom_call" | custom-call | flops 8589934592 | bytes 16777216 | tf_op jit(solution)/shard_map/pallas_call | solution.py:140
  171.2 5.6 %collective-permute-start.31 = (s16[2064,128]{1,0:T(8,128)(2,1)S(1)}, s16[2064,128]{1,0:T(8,128)(2,1)S(1)}, u32[]{:S(2)}, u32[]{:S(2)}) collective-permute-start(s16[2064,128]{1,0:T(8,128)(2,1)S(1)} %get-tuple-element.181), channel_id=1, source_target_pairs={{0,3},{1,0},{2,1},{3,2},{4,7},{5,4},{6,5},{7,6},{8,11},{9,8},{10,9... | collective-permute-start | bytes 1585160 | tf_op jit(solution)/shard_map/ppermute | solution.py:44
  176.8 8.2 %shard_map.90 = (f32[4,2048,128]{2,1,0:T(8,128)S(1)}, s16[1040,128]{1,0:T(8,128)(2,1)S(1)}, s16[1040,128]{1,0:T(8,128)(2,1)S(1)}) custom-call(s32[12]{0:T(128)S(1)} %concatenate.39.meta, f32[2048,4096]{1,0:T(8,128)} %s_oth.11, f32[2048,4096]{1,0:T(8,128)} %s_oth.11, bf16[1024,512]{1,0:T(8,128)(2,1)S(1)} %shard_map.86.own, ...), custom_call_target="tpu_custom_call" | custom-call | flops 8589934592 | bytes 16777216 | tf_op jit(solution)/shard_map/pallas_call | solution.py:169
  189.4 6.6 %collective-permute-done.31.got_left = s16[2064,128]{1,0:T(8,128)(2,1)S(1)} collective-permute-done((s16[2064,128]{1,0:T(8,128)(2,1)S(1)}, s16[2064,128]{1,0:T(8,128)(2,1)S(1)}, u32[]{:S(2)}, u32[]{:S(2)}) %collective-permute-start.31) | collective-permute-done | bytes 528416 | tf_op jit(solution)/shard_map/ppermute | solution.py:44
  196.0 4.4 %shard_map.93 = (f32[3,2048,128]{2,1,0:T(8,128)}, f32[128,1024]{1,0:T(8,128)S(1)}) custom-call(s32[12]{0:T(128)S(1)} %concatenate.39.meta, f32[4,2048,128]{2,1,0:T(8,128)S(1)} %copy-done.6, s16[2064,128]{1,0:T(8,128)(2,1)S(1)} %collective-permute-done.30.got_right, s16[2064,128]{1,0:T(8,128)(2,1)S(1)} %collective-permute-done.31.got_left, ...), custom_call_target="tpu_custom_call" | custom-call | tf_op jit(solution)/shard_map/pallas_call | solution.py:270
  202.5 4.4 %collective-permute-start.40 = (s16[1040,128]{1,0:T(8,128)(2,1)}, s16[1040,128]{1,0:T(8,128)(2,1)S(1)}, u32[]{:S(2)}, u32[]{:S(2)}) collective-permute-start(s16[1040,128]{1,0:T(8,128)(2,1)} %copy-done.36), channel_id=1, source_target_pairs={{0,1},{1,2},{2,3},{3,0},{4,5},{5,6},{6,7},{7,4},{8,9},{9,10},{10,1... | collective-permute-start | bytes 798728 | tf_op jit(solution)/shard_map/ppermute | solution.py:44
  210.6 8.8 %shard_map.94.before = f32[2048,512]{1,0:T(8,128)S(1)} custom-call(s32[12]{0:T(128)S(1)} %concatenate.39.meta, f32[2048,4096]{1,0:T(8,128)} %s_oth.11, f32[2048,4096]{1,0:T(8,128)} %s_oth.11, bf16[1024,512]{1,0:T(8,128)(2,1)} %shard_map.89.own, bf16[1024,512]{1,0:T(8,128)(2,1)} %collective-permute-done.32.oth), custom_call_target="tpu_custom_call" | custom-call | flops 8589934592 | bytes 16777216 | tf_op jit(solution)/shard_map/pallas_call | solution.py:140
  225.7 8.3 %shard_map.95 = (f32[4,2048,128]{2,1,0:T(8,128)S(1)}, s16[1040,128]{1,0:T(8,128)(2,1)S(1)}, s16[1040,128]{1,0:T(8,128)(2,1)S(1)}) custom-call(s32[12]{0:T(128)S(1)} %concatenate.39.meta, f32[2048,4096]{1,0:T(8,128)} %s_oth.11, f32[2048,4096]{1,0:T(8,128)} %s_oth.11, bf16[1024,512]{1,0:T(8,128)(2,1)S(1)} %shard_map.91.own, ...), custom_call_target="tpu_custom_call" | custom-call | flops 8589934592 | bytes 16777216 | tf_op jit(solution)/shard_map/pallas_call | solution.py:169
  237.9 17.7 %collective-permute-done.36.got_right = s16[1040,128]{1,0:T(8,128)(2,1)S(1)} collective-permute-done((s16[1040,128]{1,0:T(8,128)(2,1)S(1)}, s16[1040,128]{1,0:T(8,128)(2,1)S(1)}, u32[]{:S(2)}, u32[]{:S(2)}) %collective-permute-start.36) | collective-permute-done | bytes 266272 | tf_op jit(solution)/shard_map/ppermute | solution.py:44
  259.9 4.4 %shard_map.98 = (f32[3,2048,128]{2,1,0:T(8,128)}, f32[128,1024]{1,0:T(8,128)S(1)}) custom-call(s32[12]{0:T(128)S(1)} %concatenate.39.meta, f32[4,2048,128]{2,1,0:T(8,128)S(1)} %copy-done.8, s16[2064,128]{1,0:T(8,128)(2,1)S(1)} %collective-permute-done.42.got_right, ...), custom_call_target="tpu_custom_call", output_to_operand_aliasing={{0}: (6, {})} | custom-call | tf_op jit(solution)/shard_map/pallas_call | solution.py:270
  281.1 9.7 %collective-permute-done.39.got_left = s16[2064,128]{1,0:T(8,128)(2,1)S(1)} collective-permute-done((s16[2064,128]{1,0:T(8,128)(2,1)S(1)}, s16[2064,128]{1,0:T(8,128)(2,1)S(1)}, u32[]{:S(2)}, u32[]{:S(2)}) %collective-permute-start.39) | collective-permute-done | bytes 528416 | tf_op jit(solution)/shard_map/ppermute | solution.py:44
  290.9 5.9 %collective-permute-start.51 = (f32[64,1024]{1,0:T(8,128)S(1)}, f32[64,1024]{1,0:T(8,128)S(1)}, u32[]{:S(2)}, u32[]{:S(2)}) collective-permute-start(f32[64,1024]{1,0:T(8,128)S(1)} %add.160), channel_id=1, source_target_pairs={{0,16},{4,20},{8,24},{12,28},{16,0},{20,4},{24,8},{28,12},{1,17},{... | collective-permute-start | bytes 786440 | tf_op jit(solution)/shard_map/ppermute | solution.py:48
  298.2 4.8 %collective-permute-done.51 = f32[64,1024]{1,0:T(8,128)S(1)} collective-permute-done((f32[64,1024]{1,0:T(8,128)S(1)}, f32[64,1024]{1,0:T(8,128)S(1)}, u32[]{:S(2)}, u32[]{:S(2)}) %collective-permute-start.51) | collective-permute-done | bytes 262176 | tf_op jit(solution)/shard_map/ppermute | solution.py:48
  308.8 4.6 %collective-permute-done.45 = f32[64,640]{1,0:T(8,128)S(1)} collective-permute-done((f32[64,640]{1,0:T(8,128)S(1)}, f32[64,640]{1,0:T(8,128)S(1)}, u32[]{:S(2)}, u32[]{:S(2)}) %collective-permute-start.45) | collective-permute-done | bytes 163872 | tf_op jit(solution)/shard_map/ppermute | solution.py:44
  313.4 5.1 %collective-permute-done.46 = f32[64,640]{1,0:T(8,128)S(1)} collective-permute-done((f32[64,640]{1,0:T(8,128)S(1)}, f32[64,640]{1,0:T(8,128)S(1)}, u32[]{:S(2)}, u32[]{:S(2)}) %collective-permute-start.46) | collective-permute-done | bytes 163872 | tf_op jit(solution)/shard_map/ppermute | solution.py:44
  326.0 4.5 %collective-permute-start.52 = (f32[64,640]{1,0:T(8,128)S(1)}, f32[64,640]{1,0:T(8,128)S(1)}, u32[]{:S(2)}, u32[]{:S(2)}) collective-permute-start(f32[64,640]{1,0:T(8,128)S(1)} %get-tuple-element.237), channel_id=1, source_target_pairs={{0,3},{1,0},{2,1},{3,2},{4,7},{5,4},{6,5},{7,6},{8,11},{9,8},{10,9... | collective-permute-start | bytes 491528 | tf_op jit(solution)/shard_map/ppermute | solution.py:44
  340.4 12.1 %collective-permute-done.53 = f32[64,640]{1,0:T(8,128)S(1)} collective-permute-done((f32[64,640]{1,0:T(8,128)S(1)}, f32[64,640]{1,0:T(8,128)S(1)}, u32[]{:S(2)}, u32[]{:S(2)}) %collective-permute-start.53) | collective-permute-done | bytes 163872 | tf_op jit(solution)/shard_map/ppermute | solution.py:44
  356.3 5.4 %collective-permute-done.57 = f32[64,512]{1,0:T(8,128)} collective-permute-done((f32[64,512]{1,0:T(8,128)S(1)}, f32[64,512]{1,0:T(8,128)}, u32[]{:S(2)}, u32[]{:S(2)}) %collective-permute-start.57) | collective-permute-done | bytes 131104 | tf_op jit(solution)/shard_map/ppermute | solution.py:48
  (311 shorter events, 173.4 us)
Async XLA Ops:
  30.6 18.2 %collective-permute-start = (bf16[512,512]{1,0:T(8,128)(2,1)}, bf16[512,512]{1,0:T(8,128)(2,1)S(1)}, u32[]{:S(2)}, u32[]{:S(2)}) collective-permute-start(bf16[512,512]{1,0:T(8,128)(2,1)} %get-tuple-element.105), channel_id=1, source_target_pairs={{0,8},{4,12},{9,1},{13,5},{18,26},{22,30},{27,19},{31,23}} | collective-permute-start | bytes 1572872 | tf_op jit(solution)/shard_map/ppermute | solution.py:443
  31.9 18.7 %collective-permute-start.1 = (bf16[512,512]{1,0:T(8,128)(2,1)S(1)}, bf16[512,512]{1,0:T(8,128)(2,1)S(1)}, u32[]{:S(2)}, u32[]{:S(2)}) collective-permute-start(bf16[512,512]{1,0:T(8,128)(2,1)S(1)} %get-tuple-element.106), channel_id=1, source_target_pairs={{0,16},{4,20},{9,25},{13,29},{18,2},{22,6},{27,11},{31,15}} | collective-permute-start | bytes 1572872 | tf_op jit(solution)/shard_map/ppermute | solution.py:443
  33.9 29.3 %collective-permute-start.24 = (bf16[128,512]{1,0:T(8,128)(2,1)}, bf16[128,512]{1,0:T(8,128)(2,1)S(1)}, u32[]{:S(2)}, u32[]{:S(2)}) collective-permute-start(bf16[128,512]{1,0:T(8,128)(2,1)} %constant_dynamic-slice_fusion.17), channel_id=1, source_target_pairs={{0,3},{1,0},{2,1},{3,2},{4,7},{5,4},{6,5},{7,6},{8,11},{9,8},{10,9... | collective-permute-start | bytes 393224 | tf_op jit(solution)/shard_map/ppermute | solution.py:44
  58.0 16.8 %collective-permute-start.4 = (bf16[512,512]{1,0:T(8,128)(2,1)}, bf16[512,512]{1,0:T(8,128)(2,1)S(1)}, u32[]{:S(2)}, u32[]{:S(2)}) collective-permute-start(bf16[512,512]{1,0:T(8,128)(2,1)} %get-tuple-element.111), channel_id=1, source_target_pairs={{0,8},{4,12},{9,1},{13,5},{18,26},{22,30},{27,19},{31,23},{8,24},{... | collective-permute-start | bytes 1572872 | tf_op jit(solution)/shard_map/ppermute | solution.py:443
  59.3 18.0 %collective-permute-start.5 = (bf16[512,512]{1,0:T(8,128)(2,1)}, bf16[512,512]{1,0:T(8,128)(2,1)S(1)}, u32[]{:S(2)}, u32[]{:S(2)}) collective-permute-start(bf16[512,512]{1,0:T(8,128)(2,1)} %get-tuple-element.112), channel_id=1, source_target_pairs={{0,16},{4,20},{9,25},{13,29},{18,2},{22,6},{27,11},{31,15},{16,24}... | collective-permute-start | bytes 1572872 | tf_op jit(solution)/shard_map/ppermute | solution.py:443
  66.0 28.7 %collective-permute-start.26 = (bf16[128,512]{1,0:T(8,128)(2,1)}, bf16[128,512]{1,0:T(8,128)(2,1)S(1)}, u32[]{:S(2)}, u32[]{:S(2)}) collective-permute-start(bf16[128,512]{1,0:T(8,128)(2,1)} %constant_dynamic-slice_fusion.17), channel_id=1, source_target_pairs={{0,1},{1,2},{2,3},{3,0},{4,5},{5,6},{6,7},{7,4},{8,9},{9,10},{10,1... | collective-permute-start | bytes 393224 | tf_op jit(solution)/shard_map/ppermute | solution.py:44
  109.6 42.5 %collective-permute-start.22 = (bf16[1024,512]{1,0:T(8,128)(2,1)}, bf16[1024,512]{1,0:T(8,128)(2,1)}, u32[]{:S(2)}, u32[]{:S(2)}) collective-permute-start(bf16[1024,512]{1,0:T(8,128)(2,1)} %shard_map.87.own), channel_id=1, source_target_pairs={{0,4},{4,0},{8,12},{12,8},{16,20},{20,16},{24,28},{28,24},{1,5},{5... | collective-permute-start | bytes 3145736 | tf_op jit(solution)/shard_map/ppermute | solution.py:48
  118.7 52.5 %collective-permute-start.23 = (bf16[1024,512]{1,0:T(8,128)(2,1)S(1)}, bf16[1024,512]{1,0:T(8,128)(2,1)S(1)}, u32[]{:S(2)}, u32[]{:S(2)}) collective-permute-start(bf16[1024,512]{1,0:T(8,128)(2,1)S(1)} %shard_map.86.own), channel_id=1, source_target_pairs={{0,4},{4,0},{8,12},{12,8},{16,20},{20,16},{24,28},{28,24},{1,5},{5... | collective-permute-start | bytes 3145736 | tf_op jit(solution)/shard_map/ppermute | solution.py:48
  119.7 42.4 %collective-permute-start.20 = (bf16[512,512]{1,0:T(8,128)(2,1)S(1)}, bf16[512,512]{1,0:T(8,128)(2,1)S(1)}, u32[]{:S(2)}, u32[]{:S(2)}) collective-permute-start(bf16[512,512]{1,0:T(8,128)(2,1)S(1)} %copy-done.22), channel_id=1, source_target_pairs={{24,16},{28,20},{17,25},{21,29},{10,2},{14,6},{3,11},{7,15}} | collective-permute-start | bytes 1572872 | tf_op jit(solution)/shard_map/ppermute | solution.py:443
  120.4 42.5 %collective-permute-start.21 = (bf16[512,512]{1,0:T(8,128)(2,1)S(1)}, bf16[512,512]{1,0:T(8,128)(2,1)S(1)}, u32[]{:S(2)}, u32[]{:S(2)}) collective-permute-start(bf16[512,512]{1,0:T(8,128)(2,1)S(1)} %copy-done.24), channel_id=1, source_target_pairs={{24,8},{28,12},{17,1},{21,5},{10,26},{14,30},{3,19},{7,23}} | collective-permute-start | bytes 1572872 | tf_op jit(solution)/shard_map/ppermute | solution.py:443
  121.1 44.3 %collective-permute-start.28 = (s16[1040,128]{1,0:T(8,128)(2,1)S(1)}, s16[1040,128]{1,0:T(8,128)(2,1)S(1)}, u32[]{:S(2)}, u32[]{:S(2)}) collective-permute-start(s16[1040,128]{1,0:T(8,128)(2,1)S(1)} %copy-done.35), channel_id=1, source_target_pairs={{0,1},{1,2},{2,3},{3,0},{4,5},{5,6},{6,7},{7,4},{8,9},{9,10},{10,1... | collective-permute-start | bytes 798728 | tf_op jit(solution)/shard_map/ppermute | solution.py:44
  162.1 39.0 %collective-permute-start.18 = (bf16[512,512]{1,0:T(8,128)(2,1)S(1)}, bf16[512,512]{1,0:T(8,128)(2,1)S(1)}, u32[]{:S(2)}, u32[]{:S(2)}) collective-permute-start(bf16[512,512]{1,0:T(8,128)(2,1)S(1)} %copy-done.18), channel_id=1, source_target_pairs={{24,16},{28,20},{17,25},{21,29},{10,2},{14,6},{3,11},{7,15}} | collective-permute-start | bytes 1572872 | tf_op jit(solution)/shard_map/ppermute | solution.py:443
  162.9 38.4 %collective-permute-start.19 = (bf16[512,512]{1,0:T(8,128)(2,1)S(1)}, bf16[512,512]{1,0:T(8,128)(2,1)S(1)}, u32[]{:S(2)}, u32[]{:S(2)}) collective-permute-start(bf16[512,512]{1,0:T(8,128)(2,1)S(1)} %copy-done.20), channel_id=1, source_target_pairs={{24,8},{28,12},{17,1},{21,5},{10,26},{14,30},{3,19},{7,23}} | collective-permute-start | bytes 1572872 | tf_op jit(solution)/shard_map/ppermute | solution.py:443
  165.4 45.2 %collective-permute-start.32 = (bf16[1024,512]{1,0:T(8,128)(2,1)}, bf16[1024,512]{1,0:T(8,128)(2,1)}, u32[]{:S(2)}, u32[]{:S(2)}) collective-permute-start(bf16[1024,512]{1,0:T(8,128)(2,1)} %shard_map.89.own), channel_id=1, source_target_pairs={{0,4},{4,0},{8,12},{12,8},{16,20},{20,16},{24,28},{28,24},{1,5},{5... | collective-permute-start | bytes 3145736 | tf_op jit(solution)/shard_map/ppermute | solution.py:48
  167.3 22.1 %collective-permute-start.30 = (s16[2064,128]{1,0:T(8,128)(2,1)S(1)}, s16[2064,128]{1,0:T(8,128)(2,1)S(1)}, u32[]{:S(2)}, u32[]{:S(2)}) collective-permute-start(s16[2064,128]{1,0:T(8,128)(2,1)S(1)} %get-tuple-element.179), channel_id=1, source_target_pairs={{0,1},{1,2},{2,3},{3,0},{4,5},{5,6},{6,7},{7,4},{8,9},{9,10},{10,1... | collective-permute-start | bytes 1585160 | tf_op jit(solution)/shard_map/ppermute | solution.py:44
  171.2 24.8 %collective-permute-start.31 = (s16[2064,128]{1,0:T(8,128)(2,1)S(1)}, s16[2064,128]{1,0:T(8,128)(2,1)S(1)}, u32[]{:S(2)}, u32[]{:S(2)}) collective-permute-start(s16[2064,128]{1,0:T(8,128)(2,1)S(1)} %get-tuple-element.181), channel_id=1, source_target_pairs={{0,3},{1,0},{2,1},{3,2},{4,7},{5,4},{6,5},{7,6},{8,11},{9,8},{10,9... | collective-permute-start | bytes 1585160 | tf_op jit(solution)/shard_map/ppermute | solution.py:44
  202.0 23.7 %collective-permute-start.35 = (bf16[1024,512]{1,0:T(8,128)(2,1)S(1)}, bf16[1024,512]{1,0:T(8,128)(2,1)S(1)}, u32[]{:S(2)}, u32[]{:S(2)}) collective-permute-start(bf16[1024,512]{1,0:T(8,128)(2,1)S(1)} %shard_map.91.own), channel_id=1, source_target_pairs={{0,4},{4,0},{8,12},{12,8},{16,20},{20,16},{24,28},{28,24},{1,5},{5... | collective-permute-start | bytes 3145736 | tf_op jit(solution)/shard_map/ppermute | solution.py:48
  202.5 16.9 %collective-permute-start.40 = (s16[1040,128]{1,0:T(8,128)(2,1)}, s16[1040,128]{1,0:T(8,128)(2,1)S(1)}, u32[]{:S(2)}, u32[]{:S(2)}) collective-permute-start(s16[1040,128]{1,0:T(8,128)(2,1)} %copy-done.36), channel_id=1, source_target_pairs={{0,1},{1,2},{2,3},{3,0},{4,5},{5,6},{6,7},{7,4},{8,9},{9,10},{10,1... | collective-permute-start | bytes 798728 | tf_op jit(solution)/shard_map/ppermute | solution.py:44
  221.8 38.1 %collective-permute-start.42 = (s16[2064,128]{1,0:T(8,128)(2,1)S(1)}, s16[2064,128]{1,0:T(8,128)(2,1)S(1)}, u32[]{:S(2)}, u32[]{:S(2)}) collective-permute-start(s16[2064,128]{1,0:T(8,128)(2,1)S(1)} %get-tuple-element.194), channel_id=1, source_target_pairs={{0,1},{1,2},{2,3},{3,0},{4,5},{5,6},{6,7},{7,4},{8,9},{9,10},{10,1... | collective-permute-start | bytes 1585160 | tf_op jit(solution)/shard_map/ppermute | solution.py:44
  222.4 37.5 %collective-permute-start.43 = (s16[2064,128]{1,0:T(8,128)(2,1)S(1)}, s16[2064,128]{1,0:T(8,128)(2,1)S(1)}, u32[]{:S(2)}, u32[]{:S(2)}) collective-permute-start(s16[2064,128]{1,0:T(8,128)(2,1)S(1)} %get-tuple-element.196), channel_id=1, source_target_pairs={{0,3},{1,0},{2,1},{3,2},{4,7},{5,4},{6,5},{7,6},{8,11},{9,8},{10,9... | collective-permute-start | bytes 1585160 | tf_op jit(solution)/shard_map/ppermute | solution.py:44
  234.0 21.6 %collective-permute-start.36 = (s16[1040,128]{1,0:T(8,128)(2,1)S(1)}, s16[1040,128]{1,0:T(8,128)(2,1)S(1)}, u32[]{:S(2)}, u32[]{:S(2)}) collective-permute-start(s16[1040,128]{1,0:T(8,128)(2,1)S(1)} %get-tuple-element.186), channel_id=1, source_target_pairs={{0,1},{1,2},{2,3},{3,0},{4,5},{5,6},{6,7},{7,4},{8,9},{9,10},{10,1... | collective-permute-start | bytes 798728 | tf_op jit(solution)/shard_map/ppermute | solution.py:44
  234.1 24.7 %collective-permute-start.37 = (s16[1040,128]{1,0:T(8,128)(2,1)S(1)}, s16[1040,128]{1,0:T(8,128)(2,1)S(1)}, u32[]{:S(2)}, u32[]{:S(2)}) collective-permute-start(s16[1040,128]{1,0:T(8,128)(2,1)S(1)} %get-tuple-element.188), channel_id=1, source_target_pairs={{0,3},{1,0},{2,1},{3,2},{4,7},{5,4},{6,5},{7,6},{8,11},{9,8},{10,9... | collective-permute-start | bytes 798728 | tf_op jit(solution)/shard_map/ppermute | solution.py:44
  264.9 26.0 %collective-permute-start.39 = (s16[2064,128]{1,0:T(8,128)(2,1)S(1)}, s16[2064,128]{1,0:T(8,128)(2,1)S(1)}, u32[]{:S(2)}, u32[]{:S(2)}) collective-permute-start(s16[2064,128]{1,0:T(8,128)(2,1)S(1)} %get-tuple-element.190), channel_id=1, source_target_pairs={{0,3},{1,0},{2,1},{3,2},{4,7},{5,4},{6,5},{7,6},{8,11},{9,8},{10,9... | collective-permute-start | bytes 1585160 | tf_op jit(solution)/shard_map/ppermute | solution.py:44
  271.4 25.7 %collective-permute-start.44 = (f32[64,1024]{1,0:T(8,128)S(1)}, f32[64,1024]{1,0:T(8,128)}, u32[]{:S(2)}, u32[]{:S(2)}) collective-permute-start(f32[64,1024]{1,0:T(8,128)S(1)} %add.144), channel_id=1, source_target_pairs={{0,16},{4,20},{8,24},{12,28},{16,0},{20,4},{24,8},{28,12},{1,17},{... | collective-permute-start | bytes 786440 | tf_op jit(solution)/shard_map/ppermute | solution.py:48
  (91 other events, 757.2 us)

commit v5 on v4

--- a/solution.py
+++ b/solution.py
@@ -567,10 +567,13 @@
             arrive(len(events) - 1)
     for k in range(supernodes):
         last = k + 1 == supernodes
-        if last:
-            finish(k)
-        elif k > 0:
-            finish(k, hops[-1][min(1, len(hops[-1]) - 1)], ((), hops[-1][-1]))
+        if k == 0:
+            for later in range(1, supernodes):
+                if later + 1 < supernodes:
+                    stages = hops[-1]
+                    finish(later, stages[min(1, len(stages) - 1)], ((), stages[-1]))
+                else:
+                    finish(later)
         link = None if k == 0 else link_full[k - 1]
         total = summed[k][-1]
         mine = lax.dynamic_slice_in_dim(diag_inverse[k], lane * (share // 2), share // 2, 1).T
@@ -592,7 +595,7 @@
                 message = jnp.concatenate([turned, block], axis=1)
                 arrived.append(shift(message, s, col_size) if s else message)
             if k + 2 < supernodes:
-                arrived = after(tuple(arrived), *hops[-1][min(1, len(hops[-1]) - 1)])
+                arrived = after(tuple(arrived), sums[-1])
             ordered = around(list(arrived), col_number)
             ordered = both_halves(ordered, lane, row_size, 1)
             full_turned = ordered[:, :, :width].reshape(width, width)

time: 375 us -> 370 us (0.987)
  waiting for transfers between devices: 113 us -> 99.1 us
  Pallas kernels: 80.1 us -> 88.8 us
    ppermute x21, waiting for transfers between devices: 68 us -> 57.6 us  [shift(): lax.ppermute(value, 'col', [(z, (z + by) % size) for z in range(size)])]
    ppermute x19, starting transfers between devices: 18.6 us -> 26.3 us  [swap(): return lax.ppermute(value, 'row', [(r, r ^ bit) for r in range(size)])]
    ppermute x21, starting transfers between devices: 73.9 us -> 69.1 us  [shift(): lax.ppermute(value, 'col', [(z, (z + by) % size) for z in range(size)])]
    pallas_call x3, Pallas kernels: 24.7 us -> 29.1 us  [panel_second(): pl.pallas_call(functools.partial(second_kernel, cols, link is not None),...]
    pallas_call x3, Pallas kernels: 25.4 us -> 29.7 us  [panel_first(): pl.pallas_call(first_kernel, grid_spec=pltpu.PrefetchScalarGridSpec(num_s...]
  transfers between devices with their start and end apart: 60 -> 60, of which waited for: 26 -> 25; matrix products, arithmetic and copies ran while one was open for 4% -> 4% of each run, Pallas kernels for 20% -> 22%
where the time goes in v5:
time: 370 us; the launch traced here: 369 us
  starting transfers between devices  132 us (36%)
  waiting for transfers between devices  99.1 us (27%)
  Pallas kernels  88.8 us (24%)
  local copies, waits for them, and re-layouts  34.6 us (9%)
  other arithmetic  10.7 us (3%)
    ppermute x21, starting transfers between devices, shift(): lax.ppermute(value, 'col', [(z, (z + by) % size) for z in range(size)])  69.1 us
    ppermute x21, waiting for transfers between devices, shift(): lax.ppermute(value, 'col', [(z, (z + by) % size) for z in range(size)])  57.6 us
    ppermute x20, starting transfers between devices, send_on(): got.append(lax.ppermute(value, BOTH, pairs))  36.5 us
    pallas_call x3, Pallas kernels, panel_first(): pl.pallas_call(first_kernel, grid_spec=pltpu.PrefetchScalarGridSpec(num_s...  29.7 us
    pallas_call x3, Pallas kernels, panel_second(): pl.pallas_call(functools.partial(second_kernel, cols, link is not None),...  29.1 us
    ppermute x20, waiting for transfers between devices, send_on(): got.append(lax.ppermute(value, BOTH, pairs))  27.5 us
    ppermute x19, starting transfers between devices, swap(): return lax.ppermute(value, 'row', [(r, r ^ bit) for r in range(size)])  26.3 us
    unnamed x129, local copies, waits for them, and re-layouts  26.3 us
  transfers between devices with their start and end apart: 60, of which 25 were waited for; matrix products, arithmetic and copies ran while one was open for 4% of the time, Pallas kernels for 22%

profile of v5, /device:TPU:0, one launch (start us, length us, event | category | flops | bytes accessed | tf_op | source)
XLA Modules:
  0.0 369.0 jit_solution(2043583033422669011)
XLA Ops:
  5.1 4.9 %collective-permute-start.2 = (bf16[512,512]{1,0:T(8,128)(2,1)S(1)}, bf16[512,512]{1,0:T(8,128)(2,1)S(1)}, u32[]{:S(2)}, u32[]{:S(2)}) collective-permute-start(bf16[512,512]{1,0:T(8,128)(2,1)S(1)} %get-tuple-element.109), channel_id=1, source_target_pairs={{0,8},{4,12},{9,1},{13,5},{18,26},{22,30},{27,19},{31,23}} | collective-permute-start | bytes 1572872 | tf_op jit(solution)/shard_map/ppermute | solution.py:443
  11.3 9.8 %collective-permute-done.2.refs_2_.refs_0_ = bf16[512,512]{1,0:T(8,128)(2,1)S(1)} collective-permute-done((bf16[512,512]{1,0:T(8,128)(2,1)S(1)}, bf16[512,512]{1,0:T(8,128)(2,1)S(1)}, u32[]{:S(2)}, u32[]{:S(2)}) %collective-permute-start.2) | collective-permute-done | bytes 524320 | tf_op jit(solution)/shard_map/ppermute | solution.py:443
  33.9 5.7 %collective-permute-done.6.refs_2_.refs_1_.refs_0_ = bf16[512,512]{1,0:T(8,128)(2,1)S(1)} collective-permute-done((bf16[512,512]{1,0:T(8,128)(2,1)}, bf16[512,512]{1,0:T(8,128)(2,1)S(1)}, u32[]{:S(2)}, u32[]{:S(2)}) %collective-permute-start.6) | collective-permute-done | bytes 524320 | tf_op jit(solution)/shard_map/ppermute | solution.py:443
  59.3 3.9 %collective-permute-start.5 = (bf16[512,512]{1,0:T(8,128)(2,1)}, bf16[512,512]{1,0:T(8,128)(2,1)S(1)}, u32[]{:S(2)}, u32[]{:S(2)}) collective-permute-start(bf16[512,512]{1,0:T(8,128)(2,1)} %get-tuple-element.112), channel_id=1, source_target_pairs={{0,16},{4,20},{9,25},{13,29},{18,2},{22,6},{27,11},{31,15},{16,24}... | collective-permute-start | bytes 1572872 | tf_op jit(solution)/shard_map/ppermute | solution.py:443
  79.7 4.4 %collective-permute-start.9 = (bf16[512,512]{1,0:T(8,128)(2,1)S(1)}, bf16[512,512]{1,0:T(8,128)(2,1)S(1)}, u32[]{:S(2)}, u32[]{:S(2)}) collective-permute-start(bf16[512,512]{1,0:T(8,128)(2,1)S(1)} %get-tuple-element.118), channel_id=1, source_target_pairs={{0,16},{4,20},{9,25},{13,29},{18,2},{22,6},{27,11},{31,15},{16,24}... | collective-permute-start | bytes 1572872 | tf_op jit(solution)/shard_map/ppermute | solution.py:443
  84.1 9.0 %shard_map.83.before = f32[2048,512]{1,0:T(8,128)S(1)} custom-call(s32[12]{0:T(128)S(1)} %concatenate.39.meta, f32[2048,4096]{1,0:T(8,128)} %s_oth.11, f32[2048,4096]{1,0:T(8,128)} %s_oth.11, bf16[1024,512]{1,0:T(8,128)(2,1)S(1)} %shard_map.82.own, bf16[1024,512]{1,0:T(8,128)(2,1)S(1)} %collective-permute-done.12.oth), custom_call_target="tpu_custom_call" | custom-call | flops 8589934592 | bytes 16777216 | tf_op jit(solution)/shard_map/pallas_call | solution.py:140
  97.6 9.5 %shard_map.85 = (f32[4,2048,128]{2,1,0:T(8,128)S(1)}, s16[1040,128]{1,0:T(8,128)(2,1)S(1)}, s16[1040,128]{1,0:T(8,128)(2,1)S(1)}) custom-call(s32[12]{0:T(128)S(1)} %concatenate.39.meta, f32[2048,4096]{1,0:T(8,128)} %s_oth.11, f32[2048,4096]{1,0:T(8,128)} %s_oth.11, bf16[1024,512]{1,0:T(8,128)(2,1)S(1)} %shard_map.84.own, ...), custom_call_target="tpu_custom_call" | custom-call | flops 8589934592 | bytes 16777216 | tf_op jit(solution)/shard_map/pallas_call | solution.py:169
  121.1 32.7 %collective-permute-start.28 = (s16[1040,128]{1,0:T(8,128)(2,1)S(1)}, s16[1040,128]{1,0:T(8,128)(2,1)S(1)}, u32[]{:S(2)}, u32[]{:S(2)}) collective-permute-start(s16[1040,128]{1,0:T(8,128)(2,1)S(1)} %copy-done.35), channel_id=1, source_target_pairs={{0,1},{1,2},{2,3},{3,0},{4,5},{5,6},{6,7},{7,4},{8,9},{9,10},{10,1... | collective-permute-start | bytes 798728 | tf_op jit(solution)/shard_map/ppermute | solution.py:44
  153.9 10.8 %shard_map.88.before = f32[2048,512]{1,0:T(8,128)S(1)} custom-call(s32[12]{0:T(128)S(1)} %concatenate.39.meta, f32[2048,4096]{1,0:T(8,128)} %s_oth.11, f32[2048,4096]{1,0:T(8,128)} %s_oth.11, bf16[1024,512]{1,0:T(8,128)(2,1)} %shard_map.87.own, bf16[1024,512]{1,0:T(8,128)(2,1)} %collective-permute-done.22.oth), custom_call_target="tpu_custom_call" | custom-call | flops 8589934592 | bytes 16777216 | tf_op jit(solution)/shard_map/pallas_call | solution.py:140
  175.8 9.8 %shard_map.90 = (f32[4,2048,128]{2,1,0:T(8,128)S(1)}, s16[1040,128]{1,0:T(8,128)(2,1)S(1)}, s16[1040,128]{1,0:T(8,128)(2,1)S(1)}) custom-call(s32[12]{0:T(128)S(1)} %concatenate.39.meta, f32[2048,4096]{1,0:T(8,128)} %s_oth.11, f32[2048,4096]{1,0:T(8,128)} %s_oth.11, bf16[1024,512]{1,0:T(8,128)(2,1)S(1)} %shard_map.86.own, ...), custom_call_target="tpu_custom_call" | custom-call | flops 8589934592 | bytes 16777216 | tf_op jit(solution)/shard_map/pallas_call | solution.py:169
  188.4 9.2 %collective-permute-done.31.got_left = s16[2064,128]{1,0:T(8,128)(2,1)S(1)} collective-permute-done((s16[2064,128]{1,0:T(8,128)(2,1)S(1)}, s16[2064,128]{1,0:T(8,128)(2,1)S(1)}, u32[]{:S(2)}, u32[]{:S(2)}) %collective-permute-start.31) | collective-permute-done | bytes 528416 | tf_op jit(solution)/shard_map/ppermute | solution.py:44
  197.6 4.4 %shard_map.93 = (f32[3,2048,128]{2,1,0:T(8,128)}, f32[128,1024]{1,0:T(8,128)S(1)}) custom-call(s32[12]{0:T(128)S(1)} %concatenate.39.meta, f32[4,2048,128]{2,1,0:T(8,128)S(1)} %copy-done.6, s16[2064,128]{1,0:T(8,128)(2,1)S(1)} %collective-permute-done.30.got_right, s16[2064,128]{1,0:T(8,128)(2,1)S(1)} %collective-permute-done.31.got_left, ...), custom_call_target="tpu_custom_call" | custom-call | tf_op jit(solution)/shard_map/pallas_call | solution.py:270
  209.3 9.9 %shard_map.94.before = f32[2048,512]{1,0:T(8,128)S(1)} custom-call(s32[12]{0:T(128)S(1)} %concatenate.39.meta, f32[2048,4096]{1,0:T(8,128)} %s_oth.11, f32[2048,4096]{1,0:T(8,128)} %s_oth.11, bf16[1024,512]{1,0:T(8,128)(2,1)} %shard_map.89.own, bf16[1024,512]{1,0:T(8,128)(2,1)} %collective-permute-done.32.oth), custom_call_target="tpu_custom_call" | custom-call | flops 8589934592 | bytes 16777216 | tf_op jit(solution)/shard_map/pallas_call | solution.py:140
  224.8 9.8 %shard_map.95 = (f32[4,2048,128]{2,1,0:T(8,128)S(1)}, s16[1040,128]{1,0:T(8,128)(2,1)S(1)}, s16[1040,128]{1,0:T(8,128)(2,1)S(1)}) custom-call(s32[12]{0:T(128)S(1)} %concatenate.39.meta, f32[2048,4096]{1,0:T(8,128)} %s_oth.11, f32[2048,4096]{1,0:T(8,128)} %s_oth.11, bf16[1024,512]{1,0:T(8,128)(2,1)S(1)} %shard_map.91.own, ...), custom_call_target="tpu_custom_call" | custom-call | flops 8589934592 | bytes 16777216 | tf_op jit(solution)/shard_map/pallas_call | solution.py:169
  238.5 16.2 %collective-permute-done.36.got_right = s16[1040,128]{1,0:T(8,128)(2,1)S(1)} collective-permute-done((s16[1040,128]{1,0:T(8,128)(2,1)S(1)}, s16[1040,128]{1,0:T(8,128)(2,1)S(1)}, u32[]{:S(2)}, u32[]{:S(2)}) %collective-permute-start.36) | collective-permute-done | bytes 266272 | tf_op jit(solution)/shard_map/ppermute | solution.py:44
  258.5 4.4 %shard_map.98 = (f32[3,2048,128]{2,1,0:T(8,128)}, f32[128,1024]{1,0:T(8,128)S(1)}) custom-call(s32[12]{0:T(128)S(1)} %concatenate.39.meta, f32[4,2048,128]{2,1,0:T(8,128)S(1)} %copy-done.8, s16[2064,128]{1,0:T(8,128)(2,1)S(1)} %collective-permute-done.42.got_right, ...), custom_call_target="tpu_custom_call", output_to_operand_aliasing={{0}: (6, {})} | custom-call | tf_op jit(solution)/shard_map/pallas_call | solution.py:270
  267.8 10.1 %collective-permute-start.44 = (f32[64,1024]{1,0:T(8,128)S(1)}, f32[64,1024]{1,0:T(8,128)}, u32[]{:S(2)}, u32[]{:S(2)}) collective-permute-start(f32[64,1024]{1,0:T(8,128)S(1)} %add.144), channel_id=1, source_target_pairs={{0,16},{4,20},{8,24},{12,28},{16,0},{20,4},{24,8},{28,12},{1,17},{... | collective-permute-start | bytes 786440 | tf_op jit(solution)/shard_map/ppermute | solution.py:48
  279.8 9.6 %collective-permute-done.39.got_left = s16[2064,128]{1,0:T(8,128)(2,1)S(1)} collective-permute-done((s16[2064,128]{1,0:T(8,128)(2,1)S(1)}, s16[2064,128]{1,0:T(8,128)(2,1)S(1)}, u32[]{:S(2)}, u32[]{:S(2)}) %collective-permute-start.39) | collective-permute-done | bytes 528416 | tf_op jit(solution)/shard_map/ppermute | solution.py:44
  289.4 10.8 %collective-permute-start.51 = (f32[64,1024]{1,0:T(8,128)S(1)}, f32[64,1024]{1,0:T(8,128)S(1)}, u32[]{:S(2)}, u32[]{:S(2)}) collective-permute-start(f32[64,1024]{1,0:T(8,128)S(1)} %add.160), channel_id=1, source_target_pairs={{0,16},{4,20},{8,24},{12,28},{16,0},{20,4},{24,8},{28,12},{1,17},{... | collective-permute-start | bytes 786440 | tf_op jit(solution)/shard_map/ppermute | solution.py:48
  301.6 4.8 %collective-permute-done.51 = f32[64,1024]{1,0:T(8,128)S(1)} collective-permute-done((f32[64,1024]{1,0:T(8,128)S(1)}, f32[64,1024]{1,0:T(8,128)S(1)}, u32[]{:S(2)}, u32[]{:S(2)}) %collective-permute-start.51) | collective-permute-done | bytes 262176 | tf_op jit(solution)/shard_map/ppermute | solution.py:48
  317.2 3.9 %shard_map.99 = (f32[3,2048,128]{2,1,0:T(8,128)}, f32[128,512]{1,0:T(8,128)S(1)}) custom-call(s32[12]{0:T(128)S(1)} %concatenate.39.meta, f32[4,2048,128]{2,1,0:T(8,128)S(1)} %copy-done.10, s16[2064,128]{1,0:T(8,128)(2,1)S(1)} %collective-permute-done.38.got_right, ...), custom_call_target="tpu_custom_call", output_to_operand_aliasing={{0}: (5, {})} | custom-call | tf_op jit(solution)/shard_map/pallas_call | solution.py:270
  328.4 4.5 %collective-permute-start.52 = (f32[64,640]{1,0:T(8,128)S(1)}, f32[64,640]{1,0:T(8,128)S(1)}, u32[]{:S(2)}, u32[]{:S(2)}) collective-permute-start(f32[64,640]{1,0:T(8,128)S(1)} %get-tuple-element.237), channel_id=1, source_target_pairs={{0,3},{1,0},{2,1},{3,2},{4,7},{5,4},{6,5},{7,6},{8,11},{9,8},{10,9... | collective-permute-start | bytes 491528 | tf_op jit(solution)/shard_map/ppermute | solution.py:44
  337.6 11.1 %collective-permute-done.53 = f32[64,640]{1,0:T(8,128)S(1)} collective-permute-done((f32[64,640]{1,0:T(8,128)S(1)}, f32[64,640]{1,0:T(8,128)S(1)}, u32[]{:S(2)}, u32[]{:S(2)}) %collective-permute-start.53) | collective-permute-done | bytes 163872 | tf_op jit(solution)/shard_map/ppermute | solution.py:44
  353.3 5.1 %collective-permute-done.57 = f32[64,512]{1,0:T(8,128)S(1)} collective-permute-done((f32[64,512]{1,0:T(8,128)}, f32[64,512]{1,0:T(8,128)S(1)}, u32[]{:S(2)}, u32[]{:S(2)}) %collective-permute-start.57) | collective-permute-done | bytes 131104 | tf_op jit(solution)/shard_map/ppermute | solution.py:48
  (311 shorter events, 152.6 us)
Async XLA Ops:
  30.6 18.2 %collective-permute-start = (bf16[512,512]{1,0:T(8,128)(2,1)}, bf16[512,512]{1,0:T(8,128)(2,1)S(1)}, u32[]{:S(2)}, u32[]{:S(2)}) collective-permute-start(bf16[512,512]{1,0:T(8,128)(2,1)} %get-tuple-element.105), channel_id=1, source_target_pairs={{0,8},{4,12},{9,1},{13,5},{18,26},{22,30},{27,19},{31,23}} | collective-permute-start | bytes 1572872 | tf_op jit(solution)/shard_map/ppermute | solution.py:443
  31.9 18.7 %collective-permute-start.1 = (bf16[512,512]{1,0:T(8,128)(2,1)S(1)}, bf16[512,512]{1,0:T(8,128)(2,1)S(1)}, u32[]{:S(2)}, u32[]{:S(2)}) collective-permute-start(bf16[512,512]{1,0:T(8,128)(2,1)S(1)} %get-tuple-element.106), channel_id=1, source_target_pairs={{0,16},{4,20},{9,25},{13,29},{18,2},{22,6},{27,11},{31,15}} | collective-permute-start | bytes 1572872 | tf_op jit(solution)/shard_map/ppermute | solution.py:443
  33.9 29.3 %collective-permute-start.24 = (bf16[128,512]{1,0:T(8,128)(2,1)}, bf16[128,512]{1,0:T(8,128)(2,1)S(1)}, u32[]{:S(2)}, u32[]{:S(2)}) collective-permute-start(bf16[128,512]{1,0:T(8,128)(2,1)} %constant_dynamic-slice_fusion.17), channel_id=1, source_target_pairs={{0,3},{1,0},{2,1},{3,2},{4,7},{5,4},{6,5},{7,6},{8,11},{9,8},{10,9... | collective-permute-start | bytes 393224 | tf_op jit(solution)/shard_map/ppermute | solution.py:44
  58.0 16.8 %collective-permute-start.4 = (bf16[512,512]{1,0:T(8,128)(2,1)}, bf16[512,512]{1,0:T(8,128)(2,1)S(1)}, u32[]{:S(2)}, u32[]{:S(2)}) collective-permute-start(bf16[512,512]{1,0:T(8,128)(2,1)} %get-tuple-element.111), channel_id=1, source_target_pairs={{0,8},{4,12},{9,1},{13,5},{18,26},{22,30},{27,19},{31,23},{8,24},{... | collective-permute-start | bytes 1572872 | tf_op jit(solution)/shard_map/ppermute | solution.py:443
  59.3 18.0 %collective-permute-start.5 = (bf16[512,512]{1,0:T(8,128)(2,1)}, bf16[512,512]{1,0:T(8,128)(2,1)S(1)}, u32[]{:S(2)}, u32[]{:S(2)}) collective-permute-start(bf16[512,512]{1,0:T(8,128)(2,1)} %get-tuple-element.112), channel_id=1, source_target_pairs={{0,16},{4,20},{9,25},{13,29},{18,2},{22,6},{27,11},{31,15},{16,24}... | collective-permute-start | bytes 1572872 | tf_op jit(solution)/shard_map/ppermute | solution.py:443
  66.0 28.7 %collective-permute-start.26 = (bf16[128,512]{1,0:T(8,128)(2,1)}, bf16[128,512]{1,0:T(8,128)(2,1)S(1)}, u32[]{:S(2)}, u32[]{:S(2)}) collective-permute-start(bf16[128,512]{1,0:T(8,128)(2,1)} %constant_dynamic-slice_fusion.17), channel_id=1, source_target_pairs={{0,1},{1,2},{2,3},{3,0},{4,5},{5,6},{6,7},{7,4},{8,9},{9,10},{10,1... | collective-permute-start | bytes 393224 | tf_op jit(solution)/shard_map/ppermute | solution.py:44
  110.9 42.9 %collective-permute-start.22 = (bf16[1024,512]{1,0:T(8,128)(2,1)}, bf16[1024,512]{1,0:T(8,128)(2,1)}, u32[]{:S(2)}, u32[]{:S(2)}) collective-permute-start(bf16[1024,512]{1,0:T(8,128)(2,1)} %shard_map.87.own), channel_id=1, source_target_pairs={{0,4},{4,0},{8,12},{12,8},{16,20},{20,16},{24,28},{28,24},{1,5},{5... | collective-permute-start | bytes 3145736 | tf_op jit(solution)/shard_map/ppermute | solution.py:48
  118.7 54.2 %collective-permute-start.23 = (bf16[1024,512]{1,0:T(8,128)(2,1)S(1)}, bf16[1024,512]{1,0:T(8,128)(2,1)S(1)}, u32[]{:S(2)}, u32[]{:S(2)}) collective-permute-start(bf16[1024,512]{1,0:T(8,128)(2,1)S(1)} %shard_map.86.own), channel_id=1, source_target_pairs={{0,4},{4,0},{8,12},{12,8},{16,20},{20,16},{24,28},{28,24},{1,5},{5... | collective-permute-start | bytes 3145736 | tf_op jit(solution)/shard_map/ppermute | solution.py:48
  119.7 45.0 %collective-permute-start.20 = (bf16[512,512]{1,0:T(8,128)(2,1)S(1)}, bf16[512,512]{1,0:T(8,128)(2,1)S(1)}, u32[]{:S(2)}, u32[]{:S(2)}) collective-permute-start(bf16[512,512]{1,0:T(8,128)(2,1)S(1)} %copy-done.22), channel_id=1, source_target_pairs={{24,16},{28,20},{17,25},{21,29},{10,2},{14,6},{3,11},{7,15}} | collective-permute-start | bytes 1572872 | tf_op jit(solution)/shard_map/ppermute | solution.py:443
  120.4 45.0 %collective-permute-start.21 = (bf16[512,512]{1,0:T(8,128)(2,1)S(1)}, bf16[512,512]{1,0:T(8,128)(2,1)S(1)}, u32[]{:S(2)}, u32[]{:S(2)}) collective-permute-start(bf16[512,512]{1,0:T(8,128)(2,1)S(1)} %copy-done.24), channel_id=1, source_target_pairs={{24,8},{28,12},{17,1},{21,5},{10,26},{14,30},{3,19},{7,23}} | collective-permute-start | bytes 1572872 | tf_op jit(solution)/shard_map/ppermute | solution.py:443
  121.1 46.8 %collective-permute-start.28 = (s16[1040,128]{1,0:T(8,128)(2,1)S(1)}, s16[1040,128]{1,0:T(8,128)(2,1)S(1)}, u32[]{:S(2)}, u32[]{:S(2)}) collective-permute-start(s16[1040,128]{1,0:T(8,128)(2,1)S(1)} %copy-done.35), channel_id=1, source_target_pairs={{0,1},{1,2},{2,3},{3,0},{4,5},{5,6},{6,7},{7,4},{8,9},{9,10},{10,1... | collective-permute-start | bytes 798728 | tf_op jit(solution)/shard_map/ppermute | solution.py:44
  164.7 38.1 %collective-permute-start.18 = (bf16[512,512]{1,0:T(8,128)(2,1)S(1)}, bf16[512,512]{1,0:T(8,128)(2,1)S(1)}, u32[]{:S(2)}, u32[]{:S(2)}) collective-permute-start(bf16[512,512]{1,0:T(8,128)(2,1)S(1)} %copy-done.18), channel_id=1, source_target_pairs={{24,16},{28,20},{17,25},{21,29},{10,2},{14,6},{3,11},{7,15}} | collective-permute-start | bytes 1572872 | tf_op jit(solution)/shard_map/ppermute | solution.py:443
  165.4 37.5 %collective-permute-start.19 = (bf16[512,512]{1,0:T(8,128)(2,1)S(1)}, bf16[512,512]{1,0:T(8,128)(2,1)S(1)}, u32[]{:S(2)}, u32[]{:S(2)}) collective-permute-start(bf16[512,512]{1,0:T(8,128)(2,1)S(1)} %copy-done.20), channel_id=1, source_target_pairs={{24,8},{28,12},{17,1},{21,5},{10,26},{14,30},{3,19},{7,23}} | collective-permute-start | bytes 1572872 | tf_op jit(solution)/shard_map/ppermute | solution.py:443
  167.9 41.3 %collective-permute-start.32 = (bf16[1024,512]{1,0:T(8,128)(2,1)}, bf16[1024,512]{1,0:T(8,128)(2,1)}, u32[]{:S(2)}, u32[]{:S(2)}) collective-permute-start(bf16[1024,512]{1,0:T(8,128)(2,1)} %shard_map.89.own), channel_id=1, source_target_pairs={{0,4},{4,0},{8,12},{12,8},{16,20},{20,16},{24,28},{28,24},{1,5},{5... | collective-permute-start | bytes 3145736 | tf_op jit(solution)/shard_map/ppermute | solution.py:48
  169.8 18.6 %collective-permute-start.30 = (s16[2064,128]{1,0:T(8,128)(2,1)S(1)}, s16[2064,128]{1,0:T(8,128)(2,1)S(1)}, u32[]{:S(2)}, u32[]{:S(2)}) collective-permute-start(s16[2064,128]{1,0:T(8,128)(2,1)S(1)} %get-tuple-element.179), channel_id=1, source_target_pairs={{0,1},{1,2},{2,3},{3,0},{4,5},{5,6},{6,7},{7,4},{8,9},{9,10},{10,1... | collective-permute-start | bytes 1585160 | tf_op jit(solution)/shard_map/ppermute | solution.py:44
  172.9 24.8 %collective-permute-start.31 = (s16[2064,128]{1,0:T(8,128)(2,1)S(1)}, s16[2064,128]{1,0:T(8,128)(2,1)S(1)}, u32[]{:S(2)}, u32[]{:S(2)}) collective-permute-start(s16[2064,128]{1,0:T(8,128)(2,1)S(1)} %get-tuple-element.181), channel_id=1, source_target_pairs={{0,3},{1,0},{2,1},{3,2},{4,7},{5,4},{6,5},{7,6},{8,11},{9,8},{10,9... | collective-permute-start | bytes 1585160 | tf_op jit(solution)/shard_map/ppermute | solution.py:44
  203.7 21.1 %collective-permute-start.35 = (bf16[1024,512]{1,0:T(8,128)(2,1)S(1)}, bf16[1024,512]{1,0:T(8,128)(2,1)S(1)}, u32[]{:S(2)}, u32[]{:S(2)}) collective-permute-start(bf16[1024,512]{1,0:T(8,128)(2,1)S(1)} %shard_map.91.own), channel_id=1, source_target_pairs={{0,4},{4,0},{8,12},{12,8},{16,20},{20,16},{24,28},{28,24},{1,5},{5... | collective-permute-start | bytes 3145736 | tf_op jit(solution)/shard_map/ppermute | solution.py:48
  220.8 37.6 %collective-permute-start.42 = (s16[2064,128]{1,0:T(8,128)(2,1)S(1)}, s16[2064,128]{1,0:T(8,128)(2,1)S(1)}, u32[]{:S(2)}, u32[]{:S(2)}) collective-permute-start(s16[2064,128]{1,0:T(8,128)(2,1)S(1)} %get-tuple-element.194), channel_id=1, source_target_pairs={{0,1},{1,2},{2,3},{3,0},{4,5},{5,6},{6,7},{7,4},{8,9},{9,10},{10,1... | collective-permute-start | bytes 1585160 | tf_op jit(solution)/shard_map/ppermute | solution.py:44
  221.5 37.0 %collective-permute-start.43 = (s16[2064,128]{1,0:T(8,128)(2,1)S(1)}, s16[2064,128]{1,0:T(8,128)(2,1)S(1)}, u32[]{:S(2)}, u32[]{:S(2)}) collective-permute-start(s16[2064,128]{1,0:T(8,128)(2,1)S(1)} %get-tuple-element.196), channel_id=1, source_target_pairs={{0,3},{1,0},{2,1},{3,2},{4,7},{5,4},{6,5},{7,6},{8,11},{9,8},{10,9... | collective-permute-start | bytes 1585160 | tf_op jit(solution)/shard_map/ppermute | solution.py:44
  234.6 20.1 %collective-permute-start.36 = (s16[1040,128]{1,0:T(8,128)(2,1)S(1)}, s16[1040,128]{1,0:T(8,128)(2,1)S(1)}, u32[]{:S(2)}, u32[]{:S(2)}) collective-permute-start(s16[1040,128]{1,0:T(8,128)(2,1)S(1)} %get-tuple-element.186), channel_id=1, source_target_pairs={{0,1},{1,2},{2,3},{3,0},{4,5},{5,6},{6,7},{7,4},{8,9},{9,10},{10,1... | collective-permute-start | bytes 798728 | tf_op jit(solution)/shard_map/ppermute | solution.py:44
  234.7 22.7 %collective-permute-start.37 = (s16[1040,128]{1,0:T(8,128)(2,1)S(1)}, s16[1040,128]{1,0:T(8,128)(2,1)S(1)}, u32[]{:S(2)}, u32[]{:S(2)}) collective-permute-start(s16[1040,128]{1,0:T(8,128)(2,1)S(1)} %get-tuple-element.188), channel_id=1, source_target_pairs={{0,3},{1,0},{2,1},{3,2},{4,7},{5,4},{6,5},{7,6},{8,11},{9,8},{10,9... | collective-permute-start | bytes 798728 | tf_op jit(solution)/shard_map/ppermute | solution.py:44
  263.9 25.4 %collective-permute-start.39 = (s16[2064,128]{1,0:T(8,128)(2,1)S(1)}, s16[2064,128]{1,0:T(8,128)(2,1)S(1)}, u32[]{:S(2)}, u32[]{:S(2)}) collective-permute-start(s16[2064,128]{1,0:T(8,128)(2,1)S(1)} %get-tuple-element.190), channel_id=1, source_target_pairs={{0,3},{1,0},{2,1},{3,2},{4,7},{5,4},{6,5},{7,6},{8,11},{9,8},{10,9... | collective-permute-start | bytes 1585160 | tf_op jit(solution)/shard_map/ppermute | solution.py:44
  267.8 32.7 %collective-permute-start.44 = (f32[64,1024]{1,0:T(8,128)S(1)}, f32[64,1024]{1,0:T(8,128)}, u32[]{:S(2)}, u32[]{:S(2)}) collective-permute-start(f32[64,1024]{1,0:T(8,128)S(1)} %add.144), channel_id=1, source_target_pairs={{0,16},{4,20},{8,24},{12,28},{16,0},{20,4},{24,8},{28,12},{1,17},{... | collective-permute-start | bytes 786440 | tf_op jit(solution)/shard_map/ppermute | solution.py:48
  289.4 17.0 %collective-permute-start.51 = (f32[64,1024]{1,0:T(8,128)S(1)}, f32[64,1024]{1,0:T(8,128)S(1)}, u32[]{:S(2)}, u32[]{:S(2)}) collective-permute-start(f32[64,1024]{1,0:T(8,128)S(1)} %add.160), channel_id=1, source_target_pairs={{0,16},{4,20},{8,24},{12,28},{16,0},{20,4},{24,8},{28,12},{1,17},{... | collective-permute-start | bytes 786440 | tf_op jit(solution)/shard_map/ppermute | solution.py:48
  (91 other events, 778.3 us)

commit v6 on v5

--- a/solution.py
+++ b/solution.py
@@ -284,6 +284,7 @@
         ],
         input_output_aliases=aliases,
         compiler_params=pltpu.CompilerParams(vmem_limit_bytes=VMEM),
+        cost_estimate=pl.CostEstimate(flops=FEED_COST, bytes_accessed=0, transcendentals=0),
     )(meta, *operands)
 
 
@@ -482,14 +483,17 @@
         right, left = hops[k][-1]
         if ties:
             right = after(right, *ties)
-        carried, total = sum_parts(meta, parts[k], right, left, panels, k, carried)
-        sums.append(total)
-        summed.append(row_sum_half(total, lane, row_size, gates))
+        if len(sums) <= k:
+            carried, total = sum_parts(meta, parts[k], right, left, panels, k, carried)
+            sums.append(total)
+        total = sums[k]
+        if gates is not None:
+            summed.append(row_sum_half(total, lane, row_size, gates))
 
     def scatter(k):
         right, left = hops[k][-1]
         for hop in range(col_size // 2 - 1, 0, -1):
-            right = after(right, products[-1])
+            right = after(right, products[-1], *(sums[-1:] if k == supernodes - 1 else []))
             right, left = pass_on(meta, parts[k], right, left, hop)
             hops[k].append((right, left))
             right, left = shift(right, 1, col_size), shift(left, -1, col_size)
@@ -537,6 +541,9 @@
                 hops.append([(shift(right, 1, col_size), shift(left, -1, col_size))])
             for k in range(supernodes):
                 if done == min(2 * k + 2, 2 * supernodes - 1):
+                    if k == supernodes - 1 > 1:
+                        for earlier in range(1, k):
+                            finish(earlier, products[-1:], None)
                     scatter(k)
             if done == 3 and supernodes > 2:
                 finish(0, products[-1:])
@@ -571,7 +578,7 @@
             for later in range(1, supernodes):
                 if later + 1 < supernodes:
                     stages = hops[-1]
-                    finish(later, stages[min(1, len(stages) - 1)], ((), stages[-1]))
+                    finish(later, (), ((), stages[-1]))
                 else:
                     finish(later)
         link = None if k == 0 else link_full[k - 1]

time: 370 us -> 366 us (0.989)
  Pallas kernels: 88.8 us -> 113 us
  starting transfers between devices: 132 us -> 112 us
  waiting for transfers between devices: 99.1 us -> 88.6 us
    ppermute x19, starting transfers between devices: 26.3 us -> 9.5 us  [swap(): return lax.ppermute(value, 'row', [(r, r ^ bit) for r in range(size)])]
    ppermute x21, waiting for transfers between devices: 57.6 us -> 42.8 us  [shift(): lax.ppermute(value, 'col', [(z, (z + by) % size) for z in range(size)])]
    pallas_call x3, Pallas kernels: 29.1 us -> 43.4 us  [panel_second(): pl.pallas_call(functools.partial(second_kernel, cols, link is not None),...]
    pallas_call x3, Pallas kernels: 29.7 us -> 39.2 us  [panel_first(): pl.pallas_call(first_kernel, grid_spec=pltpu.PrefetchScalarGridSpec(num_s...]
    ppermute x19, waiting for transfers between devices: 13.9 us -> 19.1 us  [swap(): return lax.ppermute(value, 'row', [(r, r ^ bit) for r in range(size)])]
  transfers between devices with their start and end apart: 60 -> 60, of which waited for: 25 -> 24; matrix products, arithmetic and copies ran while one was open for 4% -> 4% of each run, Pallas kernels for 22% -> 30%
where the time goes in v6:
time: 366 us; the launch traced here: 363 us
  Pallas kernels  113 us (31%)
  starting transfers between devices  112 us (31%)
  waiting for transfers between devices  88.6 us (24%)
  local copies, waits for them, and re-layouts  34.6 us (9%)
  other arithmetic  11.7 us (3%)
    ppermute x21, starting transfers between devices, shift(): lax.ppermute(value, 'col', [(z, (z + by) % size) for z in range(size)])  66 us
    pallas_call x3, Pallas kernels, panel_second(): pl.pallas_call(functools.partial(second_kernel, cols, link is not None),...  43.4 us
    ppermute x21, waiting for transfers between devices, shift(): lax.ppermute(value, 'col', [(z, (z + by) % size) for z in range(size)])  42.8 us
    pallas_call x3, Pallas kernels, panel_first(): pl.pallas_call(first_kernel, grid_spec=pltpu.PrefetchScalarGridSpec(num_s...  39.2 us
    ppermute x20, starting transfers between devices, send_on(): got.append(lax.ppermute(value, BOTH, pairs))  36.5 us
    ppermute x20, waiting for transfers between devices, send_on(): got.append(lax.ppermute(value, BOTH, pairs))  26.7 us
    unnamed x129, local copies, waits for them, and re-layouts  26.3 us
    ppermute x19, waiting for transfers between devices, swap(): return lax.ppermute(value, 'row', [(r, r ^ bit) for r in range(size)])  19.1 us
  transfers between devices with their start and end apart: 60, of which 24 were waited for; matrix products, arithmetic and copies ran while one was open for 4% of the time, Pallas kernels for 30%

profile of v6, /device:TPU:0, one launch (start us, length us, event | category | flops | bytes accessed | tf_op | source)
XLA Modules:
  0.0 363.4 jit_solution(16602209489778207979)
XLA Ops:
  5.1 4.9 %collective-permute-start.2 = (bf16[512,512]{1,0:T(8,128)(2,1)S(1)}, bf16[512,512]{1,0:T(8,128)(2,1)S(1)}, u32[]{:S(2)}, u32[]{:S(2)}) collective-permute-start(bf16[512,512]{1,0:T(8,128)(2,1)S(1)} %get-tuple-element.109), channel_id=1, source_target_pairs={{0,8},{4,12},{9,1},{13,5},{18,26},{22,30},{27,19},{31,23}} | collective-permute-start | bytes 1572872 | tf_op jit(solution)/shard_map/ppermute | solution.py:444
  11.3 9.8 %collective-permute-done.2.refs_2_.refs_0_ = bf16[512,512]{1,0:T(8,128)(2,1)S(1)} collective-permute-done((bf16[512,512]{1,0:T(8,128)(2,1)S(1)}, bf16[512,512]{1,0:T(8,128)(2,1)S(1)}, u32[]{:S(2)}, u32[]{:S(2)}) %collective-permute-start.2) | collective-permute-done | bytes 524320 | tf_op jit(solution)/shard_map/ppermute | solution.py:444
  33.9 5.7 %collective-permute-done.6.refs_2_.refs_1_.refs_0_ = bf16[512,512]{1,0:T(8,128)(2,1)S(1)} collective-permute-done((bf16[512,512]{1,0:T(8,128)(2,1)}, bf16[512,512]{1,0:T(8,128)(2,1)S(1)}, u32[]{:S(2)}, u32[]{:S(2)}) %collective-permute-start.6) | collective-permute-done | bytes 524320 | tf_op jit(solution)/shard_map/ppermute | solution.py:444
  59.3 3.9 %collective-permute-start.5 = (bf16[512,512]{1,0:T(8,128)(2,1)}, bf16[512,512]{1,0:T(8,128)(2,1)S(1)}, u32[]{:S(2)}, u32[]{:S(2)}) collective-permute-start(bf16[512,512]{1,0:T(8,128)(2,1)} %get-tuple-element.112), channel_id=1, source_target_pairs={{0,16},{4,20},{9,25},{13,29},{18,2},{22,6},{27,11},{31,15},{16,24}... | collective-permute-start | bytes 1572872 | tf_op jit(solution)/shard_map/ppermute | solution.py:444
  79.7 4.4 %collective-permute-start.9 = (bf16[512,512]{1,0:T(8,128)(2,1)S(1)}, bf16[512,512]{1,0:T(8,128)(2,1)S(1)}, u32[]{:S(2)}, u32[]{:S(2)}) collective-permute-start(bf16[512,512]{1,0:T(8,128)(2,1)S(1)} %get-tuple-element.118), channel_id=1, source_target_pairs={{0,16},{4,20},{9,25},{13,29},{18,2},{22,6},{27,11},{31,15},{16,24}... | collective-permute-start | bytes 1572872 | tf_op jit(solution)/shard_map/ppermute | solution.py:444
  84.1 12.7 %shard_map.83.before = f32[2048,512]{1,0:T(8,128)S(1)} custom-call(s32[12]{0:T(128)S(1)} %concatenate.39.meta, f32[2048,4096]{1,0:T(8,128)} %s_oth.11, f32[2048,4096]{1,0:T(8,128)} %s_oth.11, bf16[1024,512]{1,0:T(8,128)(2,1)S(1)} %shard_map.82.own, bf16[1024,512]{1,0:T(8,128)(2,1)S(1)} %collective-permute-done.12.oth), custom_call_target="tpu_custom_call" | custom-call | flops 8589934592 | bytes 16777216 | tf_op jit(solution)/shard_map/pallas_call | solution.py:140
  100.7 13.2 %shard_map.85 = (f32[4,2048,128]{2,1,0:T(8,128)S(1)}, s16[1040,128]{1,0:T(8,128)(2,1)S(1)}, s16[1040,128]{1,0:T(8,128)(2,1)S(1)}) custom-call(s32[12]{0:T(128)S(1)} %concatenate.39.meta, f32[2048,4096]{1,0:T(8,128)} %s_oth.11, f32[2048,4096]{1,0:T(8,128)} %s_oth.11, bf16[1024,512]{1,0:T(8,128)(2,1)S(1)} %shard_map.84.own, ...), custom_call_target="tpu_custom_call" | custom-call | flops 8589934592 | bytes 16777216 | tf_op jit(solution)/shard_map/pallas_call | solution.py:169
  127.9 19.3 %collective-permute-start.28 = (s16[1040,128]{1,0:T(8,128)(2,1)S(1)}, s16[1040,128]{1,0:T(8,128)(2,1)S(1)}, u32[]{:S(2)}, u32[]{:S(2)}) collective-permute-start(s16[1040,128]{1,0:T(8,128)(2,1)S(1)} %copy-done.35), channel_id=1, source_target_pairs={{0,1},{1,2},{2,3},{3,0},{4,5},{5,6},{6,7},{7,4},{8,9},{9,10},{10,1... | collective-permute-start | bytes 798728 | tf_op jit(solution)/shard_map/ppermute | solution.py:44
  147.2 8.9 %collective-permute-start.29 = (s16[1040,128]{1,0:T(8,128)(2,1)S(1)}, s16[1040,128]{1,0:T(8,128)(2,1)S(1)}, u32[]{:S(2)}, u32[]{:S(2)}) collective-permute-start(s16[1040,128]{1,0:T(8,128)(2,1)S(1)} %get-tuple-element.178), channel_id=1, source_target_pairs={{0,3},{1,0},{2,1},{3,2},{4,7},{5,4},{6,5},{7,6},{8,11},{9,8},{10,9... | collective-permute-start | bytes 798728 | tf_op jit(solution)/shard_map/ppermute | solution.py:44
  156.1 13.1 %shard_map.88.before = f32[2048,512]{1,0:T(8,128)S(1)} custom-call(s32[12]{0:T(128)S(1)} %concatenate.39.meta, f32[2048,4096]{1,0:T(8,128)} %s_oth.11, f32[2048,4096]{1,0:T(8,128)} %s_oth.11, bf16[1024,512]{1,0:T(8,128)(2,1)} %shard_map.87.own, bf16[1024,512]{1,0:T(8,128)(2,1)} %collective-permute-done.22.oth), custom_call_target="tpu_custom_call" | custom-call | flops 8589934592 | bytes 16777216 | tf_op jit(solution)/shard_map/pallas_call | solution.py:140
  174.4 6.5 %collective-permute-start.31 = (s16[2064,128]{1,0:T(8,128)(2,1)S(1)}, s16[2064,128]{1,0:T(8,128)(2,1)S(1)}, u32[]{:S(2)}, u32[]{:S(2)}) collective-permute-start(s16[2064,128]{1,0:T(8,128)(2,1)S(1)} %get-tuple-element.181), channel_id=1, source_target_pairs={{0,3},{1,0},{2,1},{3,2},{4,7},{5,4},{6,5},{7,6},{8,11},{9,8},{10,9... | collective-permute-start | bytes 1585160 | tf_op jit(solution)/shard_map/ppermute | solution.py:44
  180.9 15.1 %shard_map.90 = (f32[4,2048,128]{2,1,0:T(8,128)S(1)}, s16[1040,128]{1,0:T(8,128)(2,1)S(1)}, s16[1040,128]{1,0:T(8,128)(2,1)S(1)}) custom-call(s32[12]{0:T(128)S(1)} %concatenate.39.meta, f32[2048,4096]{1,0:T(8,128)} %s_oth.11, f32[2048,4096]{1,0:T(8,128)} %s_oth.11, bf16[1024,512]{1,0:T(8,128)(2,1)S(1)} %shard_map.86.own, ...), custom_call_target="tpu_custom_call" | custom-call | flops 8589934592 | bytes 16777216 | tf_op jit(solution)/shard_map/pallas_call | solution.py:169
  196.0 3.9 %collective-permute-done.31.got_left = s16[2064,128]{1,0:T(8,128)(2,1)S(1)} collective-permute-done((s16[2064,128]{1,0:T(8,128)(2,1)S(1)}, s16[2064,128]{1,0:T(8,128)(2,1)S(1)}, u32[]{:S(2)}, u32[]{:S(2)}) %collective-permute-start.31) | collective-permute-done | bytes 528416 | tf_op jit(solution)/shard_map/ppermute | solution.py:44
  199.9 4.4 %shard_map.93 = (f32[3,2048,128]{2,1,0:T(8,128)}, f32[128,1024]{1,0:T(8,128)S(1)}) custom-call(s32[12]{0:T(128)S(1)} %concatenate.39.meta, f32[4,2048,128]{2,1,0:T(8,128)S(1)} %copy-done.6, s16[2064,128]{1,0:T(8,128)(2,1)S(1)} %collective-permute-done.30.got_right, s16[2064,128]{1,0:T(8,128)(2,1)S(1)} %collective-permute-done.31.got_left, ...), custom_call_target="tpu_custom_call" | custom-call | flops 10000000000 | tf_op jit(solution)/shard_map/pallas_call | solution.py:270
  206.4 4.7 %collective-permute-start.37 = (s16[1040,128]{1,0:T(8,128)(2,1)}, s16[1040,128]{1,0:T(8,128)(2,1)S(1)}, u32[]{:S(2)}, u32[]{:S(2)}) collective-permute-start(s16[1040,128]{1,0:T(8,128)(2,1)} %copy-done.36), channel_id=1, source_target_pairs={{0,1},{1,2},{2,3},{3,0},{4,5},{5,6},{6,7},{7,4},{8,9},{9,10},{10,1... | collective-permute-start | bytes 798728 | tf_op jit(solution)/shard_map/ppermute | solution.py:44
  214.2 13.4 %shard_map.94.before = f32[2048,512]{1,0:T(8,128)S(1)} custom-call(s32[12]{0:T(128)S(1)} %concatenate.39.meta, f32[2048,4096]{1,0:T(8,128)} %s_oth.11, f32[2048,4096]{1,0:T(8,128)} %s_oth.11, bf16[1024,512]{1,0:T(8,128)(2,1)} %shard_map.89.own, bf16[1024,512]{1,0:T(8,128)(2,1)} %collective-permute-done.32.oth), custom_call_target="tpu_custom_call" | custom-call | flops 8589934592 | bytes 16777216 | tf_op jit(solution)/shard_map/pallas_call | solution.py:140
  232.6 15.1 %shard_map.95 = (f32[4,2048,128]{2,1,0:T(8,128)S(1)}, s16[1040,128]{1,0:T(8,128)(2,1)S(1)}, s16[1040,128]{1,0:T(8,128)(2,1)S(1)}) custom-call(s32[12]{0:T(128)S(1)} %concatenate.39.meta, f32[2048,4096]{1,0:T(8,128)} %s_oth.11, f32[2048,4096]{1,0:T(8,128)} %s_oth.11, bf16[1024,512]{1,0:T(8,128)(2,1)S(1)} %shard_map.91.own, ...), custom_call_target="tpu_custom_call" | custom-call | flops 8589934592 | bytes 16777216 | tf_op jit(solution)/shard_map/pallas_call | solution.py:169
  251.6 5.4 %collective-permute-done.40.got_left = s16[2064,128]{1,0:T(8,128)(2,1)S(1)} collective-permute-done((s16[2064,128]{1,0:T(8,128)(2,1)S(1)}, s16[2064,128]{1,0:T(8,128)(2,1)S(1)}, u32[]{:S(2)}, u32[]{:S(2)}) %collective-permute-start.40) | collective-permute-done | bytes 528416 | tf_op jit(solution)/shard_map/ppermute | solution.py:44
  257.1 4.4 %shard_map.97 = (f32[3,2048,128]{2,1,0:T(8,128)}, f32[128,1024]{1,0:T(8,128)S(1)}) custom-call(s32[12]{0:T(128)S(1)} %concatenate.39.meta, f32[4,2048,128]{2,1,0:T(8,128)S(1)} %copy-done.8, s16[2064,128]{1,0:T(8,128)(2,1)S(1)} %collective-permute-done.39.got_right, ...), custom_call_target="tpu_custom_call", output_to_operand_aliasing={{0}: (6, {})} | custom-call | flops 10000000000 | tf_op jit(solution)/shard_map/pallas_call | solution.py:270
  276.7 5.8 %collective-permute-done.42.got_right = s16[2064,128]{1,0:T(8,128)(2,1)S(1)} collective-permute-done((s16[2064,128]{1,0:T(8,128)(2,1)S(1)}, s16[2064,128]{1,0:T(8,128)(2,1)S(1)}, u32[]{:S(2)}, u32[]{:S(2)}) %collective-permute-start.42) | collective-permute-done | bytes 528416 | tf_op jit(solution)/shard_map/ppermute | solution.py:44
  282.4 8.5 %collective-permute-done.43.got_left = s16[2064,128]{1,0:T(8,128)(2,1)S(1)} collective-permute-done((s16[2064,128]{1,0:T(8,128)(2,1)S(1)}, s16[2064,128]{1,0:T(8,128)(2,1)S(1)}, u32[]{:S(2)}, u32[]{:S(2)}) %collective-permute-start.43) | collective-permute-done | bytes 528416 | tf_op jit(solution)/shard_map/ppermute | solution.py:44
  292.3 6.9 %collective-permute-done.51 = f32[64,1024]{1,0:T(8,128)} collective-permute-done((f32[64,1024]{1,0:T(8,128)S(1)}, f32[64,1024]{1,0:T(8,128)}, u32[]{:S(2)}, u32[]{:S(2)}) %collective-permute-start.51) | collective-permute-done | bytes 262176 | tf_op jit(solution)/shard_map/ppermute | solution.py:48
  310.5 3.9 %shard_map.99 = (f32[3,2048,128]{2,1,0:T(8,128)}, f32[128,512]{1,0:T(8,128)S(1)}) custom-call(s32[12]{0:T(128)S(1)} %concatenate.39.meta, f32[4,2048,128]{2,1,0:T(8,128)S(1)} %copy-done.10, s16[2064,128]{1,0:T(8,128)(2,1)S(1)} %collective-permute-done.42.got_right, ...), custom_call_target="tpu_custom_call", output_to_operand_aliasing={{0}: (5, {})} | custom-call | flops 10000000000 | tf_op jit(solution)/shard_map/pallas_call | solution.py:270
  330.3 11.7 %collective-permute-done.53 = f32[64,640]{1,0:T(8,128)S(1)} collective-permute-done((f32[64,640]{1,0:T(8,128)S(1)}, f32[64,640]{1,0:T(8,128)S(1)}, u32[]{:S(2)}, u32[]{:S(2)}) %collective-permute-start.53) | collective-permute-done | bytes 163872 | tf_op jit(solution)/shard_map/ppermute | solution.py:44
  (311 shorter events, 155.8 us)
Async XLA Ops:
  30.6 18.2 %collective-permute-start = (bf16[512,512]{1,0:T(8,128)(2,1)}, bf16[512,512]{1,0:T(8,128)(2,1)S(1)}, u32[]{:S(2)}, u32[]{:S(2)}) collective-permute-start(bf16[512,512]{1,0:T(8,128)(2,1)} %get-tuple-element.105), channel_id=1, source_target_pairs={{0,8},{4,12},{9,1},{13,5},{18,26},{22,30},{27,19},{31,23}} | collective-permute-start | bytes 1572872 | tf_op jit(solution)/shard_map/ppermute | solution.py:444
  31.9 18.7 %collective-permute-start.1 = (bf16[512,512]{1,0:T(8,128)(2,1)S(1)}, bf16[512,512]{1,0:T(8,128)(2,1)S(1)}, u32[]{:S(2)}, u32[]{:S(2)}) collective-permute-start(bf16[512,512]{1,0:T(8,128)(2,1)S(1)} %get-tuple-element.106), channel_id=1, source_target_pairs={{0,16},{4,20},{9,25},{13,29},{18,2},{22,6},{27,11},{31,15}} | collective-permute-start | bytes 1572872 | tf_op jit(solution)/shard_map/ppermute | solution.py:444
  33.9 29.3 %collective-permute-start.24 = (bf16[128,512]{1,0:T(8,128)(2,1)}, bf16[128,512]{1,0:T(8,128)(2,1)S(1)}, u32[]{:S(2)}, u32[]{:S(2)}) collective-permute-start(bf16[128,512]{1,0:T(8,128)(2,1)} %constant_dynamic-slice_fusion.17), channel_id=1, source_target_pairs={{0,3},{1,0},{2,1},{3,2},{4,7},{5,4},{6,5},{7,6},{8,11},{9,8},{10,9... | collective-permute-start | bytes 393224 | tf_op jit(solution)/shard_map/ppermute | solution.py:44
  66.0 31.8 %collective-permute-start.26 = (bf16[128,512]{1,0:T(8,128)(2,1)}, bf16[128,512]{1,0:T(8,128)(2,1)S(1)}, u32[]{:S(2)}, u32[]{:S(2)}) collective-permute-start(bf16[128,512]{1,0:T(8,128)(2,1)} %constant_dynamic-slice_fusion.17), channel_id=1, source_target_pairs={{0,1},{1,2},{2,3},{3,0},{4,5},{5,6},{6,7},{7,4},{8,9},{9,10},{10,1... | collective-permute-start | bytes 393224 | tf_op jit(solution)/shard_map/ppermute | solution.py:44
  78.1 18.7 %collective-permute-start.8 = (bf16[512,512]{1,0:T(8,128)(2,1)S(1)}, bf16[512,512]{1,0:T(8,128)(2,1)S(1)}, u32[]{:S(2)}, u32[]{:S(2)}) collective-permute-start(bf16[512,512]{1,0:T(8,128)(2,1)S(1)} %get-tuple-element.117), channel_id=1, source_target_pairs={{0,8},{4,12},{9,1},{13,5},{18,26},{22,30},{27,19},{31,23},{8,24},{... | collective-permute-start | bytes 1572872 | tf_op jit(solution)/shard_map/ppermute | solution.py:444
  98.8 20.4 %collective-permute-start.27 = (bf16[4,128,512]{2,1,0:T(8,128)(2,1)}, bf16[4,128,512]{2,1,0:T(8,128)(2,1)}, u32[]{:S(2)}, u32[]{:S(2)}) collective-permute-start(bf16[4,128,512]{2,1,0:T(8,128)(2,1)} %constant_dynamic-slice_fusion.16), channel_id=1, source_target_pairs={{0,4},{4,0},{8,12},{12,8},{16,20},{20,16},{24,28},{28,24},{1,5},{5... | collective-permute-start | bytes 1572872 | tf_op jit(solution)/shard_map/ppermute | solution.py:48
  117.7 29.5 %collective-permute-start.22 = (bf16[1024,512]{1,0:T(8,128)(2,1)}, bf16[1024,512]{1,0:T(8,128)(2,1)}, u32[]{:S(2)}, u32[]{:S(2)}) collective-permute-start(bf16[1024,512]{1,0:T(8,128)(2,1)} %shard_map.87.own), channel_id=1, source_target_pairs={{0,4},{4,0},{8,12},{12,8},{16,20},{20,16},{24,28},{28,24},{1,5},{5... | collective-permute-start | bytes 3145736 | tf_op jit(solution)/shard_map/ppermute | solution.py:48
  125.5 48.9 %collective-permute-start.23 = (bf16[1024,512]{1,0:T(8,128)(2,1)S(1)}, bf16[1024,512]{1,0:T(8,128)(2,1)S(1)}, u32[]{:S(2)}, u32[]{:S(2)}) collective-permute-start(bf16[1024,512]{1,0:T(8,128)(2,1)S(1)} %shard_map.86.own), channel_id=1, source_target_pairs={{0,4},{4,0},{8,12},{12,8},{16,20},{20,16},{24,28},{28,24},{1,5},{5... | collective-permute-start | bytes 3145736 | tf_op jit(solution)/shard_map/ppermute | solution.py:48
  126.5 42.7 %collective-permute-start.20 = (bf16[512,512]{1,0:T(8,128)(2,1)S(1)}, bf16[512,512]{1,0:T(8,128)(2,1)S(1)}, u32[]{:S(2)}, u32[]{:S(2)}) collective-permute-start(bf16[512,512]{1,0:T(8,128)(2,1)S(1)} %copy-done.22), channel_id=1, source_target_pairs={{24,16},{28,20},{17,25},{21,29},{10,2},{14,6},{3,11},{7,15}} | collective-permute-start | bytes 1572872 | tf_op jit(solution)/shard_map/ppermute | solution.py:444
  127.2 42.8 %collective-permute-start.21 = (bf16[512,512]{1,0:T(8,128)(2,1)S(1)}, bf16[512,512]{1,0:T(8,128)(2,1)S(1)}, u32[]{:S(2)}, u32[]{:S(2)}) collective-permute-start(bf16[512,512]{1,0:T(8,128)(2,1)S(1)} %copy-done.24), channel_id=1, source_target_pairs={{24,8},{28,12},{17,1},{21,5},{10,26},{14,30},{3,19},{7,23}} | collective-permute-start | bytes 1572872 | tf_op jit(solution)/shard_map/ppermute | solution.py:444
  127.9 44.6 %collective-permute-start.28 = (s16[1040,128]{1,0:T(8,128)(2,1)S(1)}, s16[1040,128]{1,0:T(8,128)(2,1)S(1)}, u32[]{:S(2)}, u32[]{:S(2)}) collective-permute-start(s16[1040,128]{1,0:T(8,128)(2,1)S(1)} %copy-done.35), channel_id=1, source_target_pairs={{0,1},{1,2},{2,3},{3,0},{4,5},{5,6},{6,7},{7,4},{8,9},{9,10},{10,1... | collective-permute-start | bytes 798728 | tf_op jit(solution)/shard_map/ppermute | solution.py:44
  147.2 25.4 %collective-permute-start.29 = (s16[1040,128]{1,0:T(8,128)(2,1)S(1)}, s16[1040,128]{1,0:T(8,128)(2,1)S(1)}, u32[]{:S(2)}, u32[]{:S(2)}) collective-permute-start(s16[1040,128]{1,0:T(8,128)(2,1)S(1)} %get-tuple-element.178), channel_id=1, source_target_pairs={{0,3},{1,0},{2,1},{3,2},{4,7},{5,4},{6,5},{7,6},{8,11},{9,8},{10,9... | collective-permute-start | bytes 798728 | tf_op jit(solution)/shard_map/ppermute | solution.py:44
  169.2 35.8 %collective-permute-start.18 = (bf16[512,512]{1,0:T(8,128)(2,1)S(1)}, bf16[512,512]{1,0:T(8,128)(2,1)S(1)}, u32[]{:S(2)}, u32[]{:S(2)}) collective-permute-start(bf16[512,512]{1,0:T(8,128)(2,1)S(1)} %copy-done.18), channel_id=1, source_target_pairs={{24,16},{28,20},{17,25},{21,29},{10,2},{14,6},{3,11},{7,15}} | collective-permute-start | bytes 1572872 | tf_op jit(solution)/shard_map/ppermute | solution.py:444
  170.0 35.2 %collective-permute-start.19 = (bf16[512,512]{1,0:T(8,128)(2,1)S(1)}, bf16[512,512]{1,0:T(8,128)(2,1)S(1)}, u32[]{:S(2)}, u32[]{:S(2)}) collective-permute-start(bf16[512,512]{1,0:T(8,128)(2,1)S(1)} %copy-done.20), channel_id=1, source_target_pairs={{24,8},{28,12},{17,1},{21,5},{10,26},{14,30},{3,19},{7,23}} | collective-permute-start | bytes 1572872 | tf_op jit(solution)/shard_map/ppermute | solution.py:444
  172.5 41.7 %collective-permute-start.32 = (bf16[1024,512]{1,0:T(8,128)(2,1)}, bf16[1024,512]{1,0:T(8,128)(2,1)}, u32[]{:S(2)}, u32[]{:S(2)}) collective-permute-start(bf16[1024,512]{1,0:T(8,128)(2,1)} %shard_map.89.own), channel_id=1, source_target_pairs={{0,4},{4,0},{8,12},{12,8},{16,20},{20,16},{24,28},{28,24},{1,5},{5... | collective-permute-start | bytes 3145736 | tf_op jit(solution)/shard_map/ppermute | solution.py:48
  174.3 21.6 %collective-permute-start.30 = (s16[2064,128]{1,0:T(8,128)(2,1)S(1)}, s16[2064,128]{1,0:T(8,128)(2,1)S(1)}, u32[]{:S(2)}, u32[]{:S(2)}) collective-permute-start(s16[2064,128]{1,0:T(8,128)(2,1)S(1)} %get-tuple-element.179), channel_id=1, source_target_pairs={{0,1},{1,2},{2,3},{3,0},{4,5},{5,6},{6,7},{7,4},{8,9},{9,10},{10,1... | collective-permute-start | bytes 1585160 | tf_op jit(solution)/shard_map/ppermute | solution.py:44
  174.4 25.4 %collective-permute-start.31 = (s16[2064,128]{1,0:T(8,128)(2,1)S(1)}, s16[2064,128]{1,0:T(8,128)(2,1)S(1)}, u32[]{:S(2)}, u32[]{:S(2)}) collective-permute-start(s16[2064,128]{1,0:T(8,128)(2,1)S(1)} %get-tuple-element.181), channel_id=1, source_target_pairs={{0,3},{1,0},{2,1},{3,2},{4,7},{5,4},{6,5},{7,6},{8,11},{9,8},{10,9... | collective-permute-start | bytes 1585160 | tf_op jit(solution)/shard_map/ppermute | solution.py:44
  205.9 26.7 %collective-permute-start.35 = (bf16[1024,512]{1,0:T(8,128)(2,1)S(1)}, bf16[1024,512]{1,0:T(8,128)(2,1)S(1)}, u32[]{:S(2)}, u32[]{:S(2)}) collective-permute-start(bf16[1024,512]{1,0:T(8,128)(2,1)S(1)} %shard_map.91.own), channel_id=1, source_target_pairs={{0,4},{4,0},{8,12},{12,8},{16,20},{20,16},{24,28},{28,24},{1,5},{5... | collective-permute-start | bytes 3145736 | tf_op jit(solution)/shard_map/ppermute | solution.py:48
  206.4 21.2 %collective-permute-start.37 = (s16[1040,128]{1,0:T(8,128)(2,1)}, s16[1040,128]{1,0:T(8,128)(2,1)S(1)}, u32[]{:S(2)}, u32[]{:S(2)}) collective-permute-start(s16[1040,128]{1,0:T(8,128)(2,1)} %copy-done.36), channel_id=1, source_target_pairs={{0,1},{1,2},{2,3},{3,0},{4,5},{5,6},{6,7},{7,4},{8,9},{9,10},{10,1... | collective-permute-start | bytes 798728 | tf_op jit(solution)/shard_map/ppermute | solution.py:44
  213.3 19.2 %collective-permute-start.34 = (f32[64,1024]{1,0:T(8,128)S(1)}, f32[64,1024]{1,0:T(8,128)S(1)}, u32[]{:S(2)}, u32[]{:S(2)}) collective-permute-start(f32[64,1024]{1,0:T(8,128)S(1)} %dynamic-slice_add_fusion.1), channel_id=1, source_target_pairs={{0,8},{4,12},{8,0},{12,4},{16,24},{20,28},{24,16},{28,20},{1,9},{5... | collective-permute-start | bytes 786440 | tf_op jit(solution)/shard_map/ppermute | solution.py:48
  228.7 23.0 %collective-permute-start.39 = (s16[2064,128]{1,0:T(8,128)(2,1)S(1)}, s16[2064,128]{1,0:T(8,128)(2,1)S(1)}, u32[]{:S(2)}, u32[]{:S(2)}) collective-permute-start(s16[2064,128]{1,0:T(8,128)(2,1)S(1)} %get-tuple-element.190), channel_id=1, source_target_pairs={{0,1},{1,2},{2,3},{3,0},{4,5},{5,6},{6,7},{7,4},{8,9},{9,10},{10,1... | collective-permute-start | bytes 1585160 | tf_op jit(solution)/shard_map/ppermute | solution.py:44
  228.8 28.3 %collective-permute-start.40 = (s16[2064,128]{1,0:T(8,128)(2,1)S(1)}, s16[2064,128]{1,0:T(8,128)(2,1)S(1)}, u32[]{:S(2)}, u32[]{:S(2)}) collective-permute-start(s16[2064,128]{1,0:T(8,128)(2,1)S(1)} %get-tuple-element.192), channel_id=1, source_target_pairs={{0,3},{1,0},{2,1},{3,2},{4,7},{5,4},{6,5},{7,6},{8,11},{9,8},{10,9... | collective-permute-start | bytes 1585160 | tf_op jit(solution)/shard_map/ppermute | solution.py:44
  267.0 23.9 %collective-permute-start.43 = (s16[2064,128]{1,0:T(8,128)(2,1)S(1)}, s16[2064,128]{1,0:T(8,128)(2,1)S(1)}, u32[]{:S(2)}, u32[]{:S(2)}) collective-permute-start(s16[2064,128]{1,0:T(8,128)(2,1)S(1)} %get-tuple-element.198), channel_id=1, source_target_pairs={{0,3},{1,0},{2,1},{3,2},{4,7},{5,4},{6,5},{7,6},{8,11},{9,8},{10,9... | collective-permute-start | bytes 1585160 | tf_op jit(solution)/shard_map/ppermute | solution.py:44
  272.3 19.0 %collective-permute-start.44 = (f32[64,1024]{1,0:T(8,128)S(1)}, f32[64,1024]{1,0:T(8,128)}, u32[]{:S(2)}, u32[]{:S(2)}) collective-permute-start(f32[64,1024]{1,0:T(8,128)S(1)} %add.144), channel_id=1, source_target_pairs={{0,16},{4,20},{8,24},{12,28},{16,0},{20,4},{24,8},{28,12},{1,17},{... | collective-permute-start | bytes 786440 | tf_op jit(solution)/shard_map/ppermute | solution.py:48
  (91 other events, 811.8 us)
